TPU v7x, 32 devices: a whole 2x2x4 slice. The times are simulated.
32 devices in a mesh: band: 16 (over z, y, core), grp: 2 (over x).
Axes of the slice: x: 2, y: 2, z: 4, core: 2. Of those that a mesh axis runs over, the one named last changes fastest.
Arguments:
- tokens: bfloat16 [2, 16, 1536, 512], P('grp', 'band'), may hold values from -6 to 6
- row_place: int32 [2, 16], P('grp', 'band'), may hold values from 0 to 7, as said below
- row_width: int32 [2, 16], P('grp', 'band'), may hold values from 96 to 192, as said below
- cotangent: bfloat16 [2, 16, 1536, 512], P('grp', 'band'), may hold values from -6 to 6
- chan_embed: bfloat16 [3, 512], replicated, may hold values from -3 to 3
- w_query: bfloat16 [512, 512], replicated, may hold values from -0.25 to 0.25
- w_key: bfloat16 [512, 512], replicated, may hold values from -0.25 to 0.25
- w_value: bfloat16 [512, 512], replicated, may hold values from -0.25 to 0.25
- w_out: bfloat16 [512, 512], replicated, may hold values from -4 to 4
- w_in: bfloat16 [512, 2048], replicated, may hold values from -0.25 to 0.25
- bias_in: bfloat16 [2048], replicated, may hold values from -3 to 3
- w_back: bfloat16 [2048, 512], replicated, may hold values from -0.125 to 0.125
- bias_back: bfloat16 [512], replicated, may hold values from -3 to 3
- gain_first: bfloat16 [512], replicated, may hold values from 0.099609375 to 1.8984375
- shift_first: bfloat16 [512], replicated, may hold values from -2 to 2
- gain_second: bfloat16 [512], replicated, may hold values from 0.099609375 to 1.8984375
- shift_second: bfloat16 [512], replicated, may hold values from -2 to 2
Outputs:
- layer_out: bfloat16 [2, 16, 1536, 512], P('grp', 'band')
- grad_tokens: bfloat16 [2, 16, 1536, 512], P('grp', 'band')
- grad_query: float32 [512, 512], P('band')
- grad_key: float32 [512, 512], P('band')
- grad_value: float32 [512, 512], P('band')
- grad_out: float32 [512, 512], P('band')
- grad_in: float32 [512, 2048], P('band')
- grad_bias_in: float32 [2048], P('band')
- grad_back: float32 [2048, 512], P('band')
- grad_bias_back: float32 [512], P('band')
- grad_gain_first: float32 [512], P('band')
- grad_shift_first: float32 [512], P('band')
- grad_gain_second: float32 [512], P('band')
- grad_shift_second: float32 [512], P('band')
- grad_embed: float32 [3, 512], P(None, 'band')
Inputs may be any that keep to these rules, and one draw needn't show every extreme that they name: The block rows of each group hold images one after another; the first one has begun 2 or 3 block rows above the first block row and the last one may be cut short. A tall image has 8 block rows and a short one 8 / 2, and row_place numbers an image's block rows from 0. In every group the first image is tall and the second is short. No image begins at the first, the middle or the last block row of a group. `row_width`: 192 on the block rows of tall images and 96 on those of short ones; the other channel positions of a row are padding.
All inputs are finite; a program needn't handle non-finite values.
Results may differ from a plain program's by a relative error of at most 0.012.
The roundings to bfloat16 on the way count: a program that leaves them out, or rounds other values in their place, can miss the bound.
Values may be sent and summed in bfloat16 or wider, within the bound.
A program may use at most 256 MiB of HBM per device.

v0:
```python
import jax
import jax.numpy as jnp
from jax import lax
from jax.sharding import PartitionSpec as P

HEAD_DIM = 64
ROW_POS = 192
BLOCK_ROWS = 8
BLOCK_COLS = 32
FLANK_COLS = 16


norm_eps = 1e-06
big_negative = -1e30


def passed_along(value, axis, steps):
    count = lax.axis_size(axis)
    leading, last = (max(0, -steps), min(count, count - steps))
    return lax.ppermute(value, axis, [(source, source + steps) for source in range(leading, last)])


def layer_norm(values, gain_vec, shift_vec):
    center = values - jnp.mean(values, axis=-1, keepdims=True)
    spread = jnp.mean(center * center, axis=-1, keepdims=True)
    return center * lax.rsqrt(spread + norm_eps) * gain_vec + shift_vec


def window_mask(row_place, row_width):
    windows = ROW_POS // BLOCK_COLS
    span_cols = BLOCK_COLS + 2 * FLANK_COLS
    queries = jnp.arange(BLOCK_ROWS * BLOCK_COLS, dtype=jnp.int32)
    memory = jnp.arange(2 * BLOCK_ROWS * span_cols, dtype=jnp.int32)
    starts = jnp.arange(windows, dtype=jnp.int32) * BLOCK_COLS
    query_row = (queries // BLOCK_COLS)[None, :, None]
    query_col = starts[:, None, None] + (queries % BLOCK_COLS)[None, :, None]
    memory_row = (memory // span_cols)[None, None, :] - BLOCK_ROWS
    memory_col = starts[:, None, None] - FLANK_COLS + (memory % span_cols)[None, None, :]
    col_limit = row_width[:, None, None, None]
    inside = (memory_col >= 0)[None] & (memory_col[None] < col_limit)
    upper_ok = (memory_row < 0)[None] & (row_place[:, None, None, None] > 0)
    earlier = (memory_row >= 0) & (
        (memory_row < query_row) | (memory_row == query_row) & (memory_col <= query_col)
    )
    itself = (memory_row == query_row) & (memory_col == query_col)
    return inside & (upper_ok | earlier[None]) | itself[None]


def gather_windows(upper_rows, lower_rows):
    count = upper_rows.shape[0]
    chans = upper_rows.shape[-1]
    windows = ROW_POS // BLOCK_COLS
    span_cols = BLOCK_COLS + 2 * FLANK_COLS
    stacked = jnp.concatenate(
        [
            upper_rows.reshape(count, BLOCK_ROWS, ROW_POS, chans),
            lower_rows.reshape(count, BLOCK_ROWS, ROW_POS, chans),
        ],
        axis=1,
    )
    padded = jnp.pad(stacked, ((0, 0), (0, 0), (FLANK_COLS, FLANK_COLS), (0, 0)))
    pieces = [
        padded[:, :, window * BLOCK_COLS : window * BLOCK_COLS + span_cols]
        for window in range(windows)
    ]
    return jnp.stack(pieces, axis=1).reshape(count, windows, 2 * BLOCK_ROWS * span_cols, chans)


def scatter_windows(grads):
    count = grads.shape[0]
    windows = grads.shape[1]
    chans = grads.shape[-1]
    span_cols = BLOCK_COLS + 2 * FLANK_COLS
    pieces = grads.reshape(count, windows, 2 * BLOCK_ROWS, span_cols, chans)
    padded = jnp.zeros((count, 2 * BLOCK_ROWS, ROW_POS + 2 * FLANK_COLS, chans), jnp.float32)
    for window in range(windows):
        padded = padded.at[:, :, window * BLOCK_COLS : window * BLOCK_COLS + span_cols].add(
            pieces[:, window]
        )
    inner = padded[:, :, FLANK_COLS : FLANK_COLS + ROW_POS]
    return (
        inner[:, :BLOCK_ROWS].reshape(count, -1, chans),
        inner[:, BLOCK_ROWS:].reshape(count, -1, chans),
    )


def to_blocks(flat_rows):
    count = flat_rows.shape[0]
    chans = flat_rows.shape[-1]
    windows = ROW_POS // BLOCK_COLS
    parted = flat_rows.reshape(count, BLOCK_ROWS, windows, BLOCK_COLS, chans)
    return parted.transpose(0, 2, 1, 3, 4).reshape(count, windows, BLOCK_ROWS * BLOCK_COLS, chans)


def from_blocks(blocks):
    count = blocks.shape[0]
    chans = blocks.shape[-1]
    windows = ROW_POS // BLOCK_COLS
    parted = blocks.reshape(count, windows, BLOCK_ROWS, BLOCK_COLS, chans)
    return parted.transpose(0, 2, 1, 3, 4).reshape(count, BLOCK_ROWS * ROW_POS, chans)


def to_pairs(blocks):
    leading = blocks.shape[:3]
    parted = blocks.reshape(leading + (-1, 2 * HEAD_DIM))
    return jnp.moveaxis(parted, 3, 0)


def from_pairs(pairs):
    merged = jnp.moveaxis(pairs, 0, 3)
    return merged.reshape(merged.shape[:3] + (-1,))


def split_heads(packed):
    return packed.reshape(packed.shape[:-1] + (2, HEAD_DIM))


def merge_heads(packed):
    return packed.reshape(packed.shape[:-2] + (-1,))


def project(left, right):
    return jnp.dot(left, right, preferred_element_type=jnp.float32).astype(jnp.bfloat16)


def shards(
    tokens,
    row_place,
    row_width,
    cotangent,
    chan_embed,
    w_query,
    w_key,
    w_value,
    w_out,
    w_in,
    bias_in,
    w_back,
    bias_back,
    gain_first,
    shift_first,
    gain_second,
    shift_second,
):
    block_count = tokens.shape[1]
    block_len = tokens.shape[2]
    model_width = tokens.shape[3]
    flat_len = block_count * block_len
    last_row = block_count - 1
    score_scale = HEAD_DIM ** (-0.5)
    allowed = window_mask(row_place[0], row_width[0])
    embed = chan_embed.astype(jnp.float32)
    start = (
        tokens[0].astype(jnp.float32).reshape(block_count, block_len // 3, 3, model_width) + embed
    )
    start = start.reshape(flat_len, model_width)
    start_low = start.astype(jnp.bfloat16)
    query_low = project(start_low, w_query)
    key_low = project(start_low, w_key)
    value_low = project(start_low, w_value)
    key_rows = key_low.reshape(block_count, block_len, model_width)
    value_rows = value_low.reshape(block_count, block_len, model_width)
    halo_key, halo_value = passed_along((key_rows[last_row], value_rows[last_row]), "band", 1)
    upper_key = jnp.concatenate([halo_key[None], key_rows[:last_row]], axis=0)
    upper_value = jnp.concatenate([halo_value[None], value_rows[:last_row]], axis=0)
    query_pairs = to_pairs(to_blocks(query_low.reshape(block_count, block_len, model_width)))
    key_pairs = to_pairs(gather_windows(upper_key, key_rows))
    value_pairs = to_pairs(gather_windows(upper_value, value_rows))

    def scores_of(query_pair, key_pair):
        raw_scores = (
            jnp.einsum(
                "rwqhe,rwkhe->rwhqk",
                split_heads(query_pair),
                split_heads(key_pair),
                preferred_element_type=jnp.float32,
            )
            * score_scale
        )
        return jnp.where(allowed[:, :, None], raw_scores, big_negative)

    def attend(pieces):
        query_pair, key_pair, value_pair = pieces
        scores = scores_of(query_pair, key_pair)
        peak = jnp.max(scores, axis=-1, keepdims=True)
        raised = jnp.exp(scores - peak)
        totals = jnp.sum(raised, axis=-1, keepdims=True)
        probs_low = (raised / totals).astype(jnp.bfloat16)
        mixed = jnp.einsum(
            "rwhqk,rwkhe->rwqhe",
            probs_low,
            split_heads(value_pair),
            preferred_element_type=jnp.float32,
        )
        return (merge_heads(mixed), (peak + jnp.log(totals))[..., 0])

    attended, log_totals = lax.map(attend, (query_pairs, key_pairs, value_pairs))
    attn_low = from_blocks(from_pairs(attended)).reshape(flat_len, model_width).astype(jnp.bfloat16)
    branch = jnp.dot(attn_low, w_out, preferred_element_type=jnp.float32)
    normed, first_norm_back = jax.vjp(
        layer_norm, start + branch, gain_first.astype(jnp.float32), shift_first.astype(jnp.float32)
    )
    normed_low = normed.astype(jnp.bfloat16)
    hidden_pre = jnp.dot(normed_low, w_in, preferred_element_type=jnp.float32) + bias_in.astype(
        jnp.float32
    )
    activated, gelu_back = jax.vjp(jax.nn.gelu, hidden_pre)
    act_low = activated.astype(jnp.bfloat16)
    ffn_out = jnp.dot(act_low, w_back, preferred_element_type=jnp.float32) + bias_back.astype(
        jnp.float32
    )
    result, second_norm_back = jax.vjp(
        layer_norm,
        normed + ffn_out,
        gain_second.astype(jnp.float32),
        shift_second.astype(jnp.float32),
    )
    layer_out = result.astype(jnp.bfloat16).reshape(1, block_count, block_len, model_width)
    cot_flat = cotangent[0].astype(jnp.float32).reshape(flat_len, model_width)
    d_second, g_gain_second, g_shift_second = second_norm_back(cot_flat)
    d_ffn = d_second.astype(jnp.bfloat16)
    g_bias_back = jnp.sum(d_ffn, axis=0, dtype=jnp.float32)
    g_back = jnp.einsum("tf,td->fd", act_low, d_ffn, preferred_element_type=jnp.float32)
    d_act = jnp.einsum("td,fd->tf", d_ffn, w_back, preferred_element_type=jnp.float32)
    d_pre_low = gelu_back(d_act)[0].astype(jnp.bfloat16)
    g_bias_in = jnp.sum(d_pre_low, axis=0, dtype=jnp.float32)
    g_in = jnp.einsum("td,tf->df", normed_low, d_pre_low, preferred_element_type=jnp.float32)
    d_normed = d_second + jnp.einsum(
        "tf,df->td", d_pre_low, w_in, preferred_element_type=jnp.float32
    )
    d_first, g_gain_first, g_shift_first = first_norm_back(d_normed)
    d_branch = d_first.astype(jnp.bfloat16)
    g_out = jnp.einsum("td,te->de", attn_low, d_branch, preferred_element_type=jnp.float32)
    d_attn_low = jnp.einsum(
        "te,de->td", d_branch, w_out, preferred_element_type=jnp.float32
    ).astype(jnp.bfloat16)
    d_out_pairs = to_pairs(to_blocks(d_attn_low.reshape(block_count, block_len, model_width)))

    def attend_back(pieces):
        query_pair, key_pair, value_pair, d_out_pair, log_total = pieces
        scores = scores_of(query_pair, key_pair)
        probs = jnp.exp(scores - log_total[..., None])
        d_out_heads = split_heads(d_out_pair)
        d_probs = jnp.einsum(
            "rwqhe,rwkhe->rwhqk",
            d_out_heads,
            split_heads(value_pair),
            preferred_element_type=jnp.float32,
        )
        inner = jnp.sum(probs * d_probs, axis=-1, keepdims=True)
        d_scores = (probs * (d_probs - inner)).astype(jnp.bfloat16)
        d_query = (
            jnp.einsum(
                "rwhqk,rwkhe->rwqhe",
                d_scores,
                split_heads(key_pair),
                preferred_element_type=jnp.float32,
            )
            * score_scale
        )
        d_key = (
            jnp.einsum(
                "rwhqk,rwqhe->rwkhe",
                d_scores,
                split_heads(query_pair),
                preferred_element_type=jnp.float32,
            )
            * score_scale
        )
        d_value = jnp.einsum(
            "rwhqk,rwqhe->rwkhe",
            probs.astype(jnp.bfloat16),
            d_out_heads,
            preferred_element_type=jnp.float32,
        )
        return (merge_heads(d_query), merge_heads(d_key), merge_heads(d_value))

    d_query_pairs, d_key_pairs, d_value_pairs = lax.map(
        attend_back, (query_pairs, key_pairs, value_pairs, d_out_pairs, log_totals)
    )
    d_query_low = (
        from_blocks(from_pairs(d_query_pairs)).reshape(flat_len, model_width).astype(jnp.bfloat16)
    )
    d_key_upper, d_key_lower = scatter_windows(from_pairs(d_key_pairs))
    d_value_upper, d_value_lower = scatter_windows(from_pairs(d_value_pairs))
    key_upper_low = d_key_upper.astype(jnp.bfloat16)
    value_upper_low = d_value_upper.astype(jnp.bfloat16)
    d_key_low = d_key_lower.reshape(flat_len, model_width).astype(jnp.bfloat16)
    d_value_low = d_value_lower.reshape(flat_len, model_width).astype(jnp.bfloat16)
    below_key, below_value = passed_along((key_upper_low[0], value_upper_low[0]), "band", -1)
    next_key = jnp.concatenate([key_upper_low[1:], below_key[None]], axis=0).reshape(
        flat_len, model_width
    )
    next_value = jnp.concatenate([value_upper_low[1:], below_value[None]], axis=0).reshape(
        flat_len, model_width
    )
    above_grad = jnp.zeros((block_len, model_width), jnp.float32)
    g_query = jnp.einsum("td,te->de", start_low, d_query_low, preferred_element_type=jnp.float32)
    g_key = jnp.einsum("td,te->de", start_low, d_key_low, preferred_element_type=jnp.float32)
    g_key = g_key + jnp.einsum("td,te->de", start_low, next_key, preferred_element_type=jnp.float32)
    g_value = jnp.einsum("td,te->de", start_low, d_value_low, preferred_element_type=jnp.float32)
    g_value = g_value + jnp.einsum(
        "td,te->de", start_low, next_value, preferred_element_type=jnp.float32
    )
    d_start = d_first + jnp.einsum(
        "te,de->td", d_query_low, w_query, preferred_element_type=jnp.float32
    )
    d_start = d_start + jnp.einsum(
        "te,de->td", d_key_low, w_key, preferred_element_type=jnp.float32
    )
    d_start = d_start + jnp.einsum(
        "te,de->td", d_value_low, w_value, preferred_element_type=jnp.float32
    )
    d_start = d_start + jnp.einsum("te,de->td", next_key, w_key, preferred_element_type=jnp.float32)
    d_start = d_start + jnp.einsum(
        "te,de->td", next_value, w_value, preferred_element_type=jnp.float32
    )
    d_start = d_start + jnp.concatenate(
        [jnp.zeros((flat_len - block_len, model_width), jnp.float32), above_grad], axis=0
    )
    grad_tokens = d_start.astype(jnp.bfloat16).reshape(1, block_count, block_len, model_width)
    g_embed = d_start.reshape(flat_len // 3, 3, model_width).sum(axis=0)
    summed = lax.psum(
        (
            g_query,
            g_key,
            g_value,
            g_out,
            g_in,
            g_bias_in,
            g_back,
            g_bias_back,
            g_gain_first,
            g_shift_first,
            g_gain_second,
            g_shift_second,
            g_embed,
        ),
        ("band", "grp"),
    )
    band_index = lax.axis_index("band")
    band_size = lax.axis_size("band")
    shard_dims = (0, 0, 0, 0, 0, 0, 0, 0, 0, 0, 0, 0, 1)
    shares = tuple(
        (
            lax.dynamic_slice_in_dim(
                full_sum,
                band_index * (full_sum.shape[axis_dim] // band_size),
                full_sum.shape[axis_dim] // band_size,
                axis_dim,
            )
            for full_sum, axis_dim in zip(summed, shard_dims)
        )
    )
    return (
        layer_out,
        grad_tokens,
        shares[0],
        shares[1],
        shares[2],
        shares[3],
        shares[4],
        shares[5],
        shares[6],
        shares[7],
        shares[8],
        shares[9],
        shares[10],
        shares[11],
        shares[12],
    )


def solution(mesh):
    return jax.shard_map(
        shards,
        mesh=mesh,
        in_specs=(
            P("grp", "band", None, None),
            P("grp", "band"),
            P("grp", "band"),
            P("grp", "band", None, None),
            P(),
            P(),
            P(),
            P(),
            P(),
            P(),
            P(),
            P(),
            P(),
            P(),
            P(),
            P(),
            P(),
        ),
        out_specs=(
            P("grp", "band", None, None),
            P("grp", "band", None, None),
            P("band", None),
            P("band", None),
            P("band", None),
            P("band", None),
            P("band", None),
            P("band"),
            P("band", None),
            P("band"),
            P("band"),
            P("band"),
            P("band"),
            P("band"),
            P(None, "band"),
        ),
        check_vma=False,
    )
```

profile of v0, /device:TPU:0, one launch (start us, length us, event | category | flops | bytes accessed | tf_op | source)
XLA Modules:
  0.0 827.1 jit_solution(4406957547811383419)
XLA Ops:
  10.6 5.9 add.412
  32.4 5.5 reshape.1078
  117.7 10.6 %copy.45 = bf16[4,1,6,1024,128]{3,4,2,1,0:T(8,128)(2,1)} copy(bf16[4,1,6,1024,128]{4,0,3,2,1:T(4,128)(2,1)} %bitcast.3) | data formatting | bytes 12582912
  139.2 10.7 %copy.47 = bf16[4,1,6,1024,128]{3,4,2,1,0:T(8,128)(2,1)} copy(bf16[4,1,6,1024,128]{4,0,3,2,1:T(4,128)(2,1)} %bitcast.9) | data formatting | bytes 12582912
  151.2 75.2 %while.40 = (s32[]{:T(128)}, bf16[4,1,6,256,128]{3,4,2,1,0:T(8,128)(2,1)}, f32[4,1,6,2,256]{4,3,2,1,0:T(2,128)}, bf16[4,1,6,1024,128]{3,4,2,1,0:T(8,128)(2,1)}, ...) while((s32[]{:T(128)}, ...), condition=%wide.region_3.4_spmd.clone, body=%wide.region_0.3_spmd.clone.sunk | while | flops 857207808 | bytes 56498332 | solution.py:197
  240.1 9.2 %multiply_convert_fusion.1 = (bf16[1536,2048]{1,0:T(8,128)(2,1)S(1)}, f32[1536,2048]{1,0:T(8,128)}) fusion(f32[2048]{0:T(1024)S(1)} %copy-done.56, bf16[512,2048]{1,0:T(8,128)(2,1)S(1)} %copy-done, f32[1536,512]{1,0:T(8,128)S(1)} %get-tuple-element.471, f32[512]{0:T(512)S(1)} %copy-done.61, f32[512]{0:T(512)S(1)} %copy-done.58, f32[1536]{0:T(1024)S(1)} %fusion.61, ...), kind=kOutput, calls=%fused_computation.45 | convolution fusion | flops 3256614912 | bytes 24141824 | tf_op jit(solution)/shard_map/dot_general | solution.py:204
  265.6 14.4 %convert_reduce_fusion = (f32[2048]{0:T(1024)}, bf16[1536,2048]{1,0:T(8,128)(2,1)S(1)}) fusion(f32[1536,2048]{1,0:T(8,128)} %get-tuple-element.473, f32[2048]{0:T(1024)S(1)} %copy-done.56, bf16[1536,512]{1,0:T(8,128)(2,1)S(1)} %get-tuple-element.438, bf16[2048,512]{1,0:T(8,128)(2,1)S(1)} %copy-done.71), kind=kOutput, calls=%fused_computation.44 | convolution fusion | flops 3293575168 | bytes 22560768 | tf_op jit(solution)/shard_map/td,fd->tf/dot_general | solution.py:224
  296.2 151.1 %while.41 = (s32[]{:T(128)}, bf16[4,1,6,256,128]{3,4,2,1,0:T(8,128)(2,1)}, f32[4,1,6,1024,128]{3,4,2,1,0:T(8,128)}, f32[4,1,6,1024,128]{3,4,2,1,0:T(8,128)}, bf1...) while((s32[]{:T(128)}, ...), condition=%wide.region_14.15_spmd.clone, body=%wide.region_12.14_spmd.clone.sunk | while | flops 2075784192 | bytes 164882832 | solution.py:278
  312.3 7.6 multiply_reduce_fusion.6
  319.9 6.9 multiply_convert_fusion.3
  349.9 7.6 multiply_reduce_fusion.6
  357.5 6.9 multiply_convert_fusion.3
  387.6 7.6 multiply_reduce_fusion.6
  395.2 6.9 multiply_convert_fusion.3
  425.5 7.6 multiply_reduce_fusion.6
  433.0 6.9 multiply_convert_fusion.3
  447.3 14.8 %copy.58 = f32[1,6,1024,4,128]{4,3,0,2,1:T(4,128)} copy(f32[1,6,1024,4,128]{2,4,1,0,3:T(8,128)} %bitcast.330) | data formatting | bytes 25165824 | tf_op jit(solution)/shard_map/transpose | solution.py:110
  471.6 8.4 %scatter-add.50 = f32[1,16,224,512]{3,0,2,1:T(1,128)S(1)} pad(f32[1,16,64,512]{3,0,2,1:T(1,128)S(1)} %slice_bitcast_fusion.5, f32[]{:T(128)} %constant.419.clone.1), padding=0_0x0_0x0_160x0_0 | pad | bytes 9437188 | tf_op jit(solution)/shard_map/scatter-add | solution.py:77
  502.4 14.7 %copy.57 = f32[1,6,1024,4,128]{4,3,0,2,1:T(4,128)} copy(f32[1,6,1024,4,128]{2,4,1,0,3:T(8,128)} %bitcast.331) | data formatting | bytes 25165824 | tf_op jit(solution)/shard_map/transpose | solution.py:110
  520.6 8.0 scatter-add.40
  554.4 5.4 fusion.72
  579.4 6.0 reshape.1076
  588.4 48.2 %all-reduce.4 = (f32[2048]{0:T(1024)S(1)}, f32[512]{0:T(512)S(1)}, f32[512]{0:T(512)S(1)}, f32[512]{0:T(512)S(1)}, f32[512]{0:T(512)S(1)}, /*index=5*/f32[512]{0:T(512)S(1)}, f32[3,512]{1,0:T(4,128)S(1)}) all-reduce(f32[2048]{0:T(1024)S(1)} %copy-done.57, f32[512]{0:T(512)S(1)} %copy-done.55, ...), channel_id=1, replica_groups=mesh['band'=16,'grp'=2] {'band','grp'}, use_global_device_ids=true, to_apply=%region_21.22 | all-reduce | flops 6144 | bytes 49152 | tf_op jit(solution)/shard_map/psum | solution.py:323
  644.1 166.7 %all-reduce.8.cloned.1.call-done = (f32[512,512]{1,0:T(8,128)}, f32[512,512]{1,0:T(8,128)}, f32[512,512]{1,0:T(8,128)}, f32[512,512]{1,0:T(8,128)}, f32[512,2048]{1,0:T(8,128)}, /*index=5*/f32[2048,512]{1,0:T(8,128)}) async-done(((f32[512,512]{1,0:T(8,128)}, f32[512,512]{1,0:T(8,128)}, f32[512,512]{1,0:T(8,128)}, f32[512,512]{1,0:T(8,128)}, f32[512,2048]{1,0:T(8,128)}, /*index=5*/f32[2048,512]{1,0:T(8,128)}), ...) | async-done | bytes 12582928 | tf_op jit(solution)/shard_map/psum | solution.py:323
  (416 shorter events, 423.3 us)
Async XLA Ops:
  7.2 232.8 %copy-start = (bf16[512,2048]{1,0:T(8,128)(2,1)S(1)}, bf16[512,2048]{1,0:T(8,128)(2,1)}, u32[]{:S(2)}) copy-start(bf16[512,2048]{1,0:T(8,128)(2,1)} %param.54) | copy-start | bytes 6291460
  7.2 803.6 %all-reduce.8.cloned.1.call-start = ((), (), s32[]{:S(2)}) async-start(), calls=%async_computation | async-start | bytes 25165824 | tf_op jit(solution)/shard_map/psum | solution.py:323
  21.6 10.7 %copy-start.52 = (bf16[3,512]{1,0:T(4,128)(2,1)S(1)}, bf16[3,512]{1,0:T(4,128)(2,1)}, u32[]{:S(2)}) copy-start(bf16[3,512]{1,0:T(4,128)(2,1)} %param.49) | copy-start | bytes 9220
  21.6 47.7 %collective-permute-start = (bf16[1536,512]{1,0:T(8,128)(2,1)}, bf16[1536,512]{1,0:T(8,128)(2,1)}, u32[]{:S(2)}, u32[]{:S(2)}) collective-permute-start(bf16[1536,512]{1,0:T(8,128)(2,1)} %convolution_convert_fusion.3), channel_id=1, source_target_pairs={{0,2},{2,4},{4,6},{6,8},{8,10},{10,12},{12,14},{14,16},{16,18},{18... | collective-permute-start | bytes 4718600 | tf_op jit(solution)/shard_map/ppermute | solution.py:20
  27.4 11.7 %copy-start.66 = (bf16[512]{0:T(512)(128)(2,1)S(1)}, bf16[512]{0:T(512)(128)(2,1)}, u32[]{:S(2)}) copy-start(bf16[512]{0:T(512)(128)(2,1)} %param.58) | copy-start | bytes 3076
  27.5 12.3 %copy-start.67 = (bf16[512]{0:T(512)(128)(2,1)S(1)}, bf16[512]{0:T(512)(128)(2,1)}, u32[]{:S(2)}) copy-start(bf16[512]{0:T(512)(128)(2,1)} %param.59) | copy-start | bytes 3076
  27.5 12.9 %copy-start.68 = (bf16[512]{0:T(512)(128)(2,1)S(1)}, bf16[512]{0:T(512)(128)(2,1)}, u32[]{:S(2)}) copy-start(bf16[512]{0:T(512)(128)(2,1)} %param.60) | copy-start | bytes 3076
  27.5 13.5 %copy-start.69 = (bf16[512]{0:T(512)(128)(2,1)S(1)}, bf16[512]{0:T(512)(128)(2,1)}, u32[]{:S(2)}) copy-start(bf16[512]{0:T(512)(128)(2,1)} %param.57) | copy-start | bytes 3076
  27.5 14.1 %copy-start.70 = (bf16[512]{0:T(512)(128)(2,1)S(1)}, bf16[512]{0:T(512)(128)(2,1)}, u32[]{:S(2)}) copy-start(bf16[512]{0:T(512)(128)(2,1)} %param.61) | copy-start | bytes 3076
  27.5 14.6 %copy-start.60 = (bf16[2048]{0:T(1024)(128)(2,1)S(1)}, bf16[2048]{0:T(1024)(128)(2,1)}, u32[]{:S(2)}) copy-start(bf16[2048]{0:T(1024)(128)(2,1)} %param.55) | copy-start | bytes 12292
  27.5 15.2 %copy-start.41 = (bf16[512,512]{1,0:T(8,128)(2,1)S(1)}, bf16[512,512]{1,0:T(8,128)(2,1)}, u32[]{:S(2)}) copy-start(bf16[512,512]{1,0:T(8,128)(2,1)} %param.50) | copy-start | bytes 1572868
  27.5 36.0 %collective-permute-start.1 = (bf16[1536,512]{1,0:T(8,128)(2,1)}, bf16[1536,512]{1,0:T(8,128)(2,1)}, u32[]{:S(2)}, u32[]{:S(2)}) collective-permute-start(bf16[1536,512]{1,0:T(8,128)(2,1)} %convolution_convert_fusion.1), channel_id=1, source_target_pairs={{0,2},{2,4},{4,6},{6,8},{8,10},{10,12},{12,14},{14,16},{16,18},{18... | collective-permute-start | bytes 4718600 | tf_op jit(solution)/shard_map/ppermute | solution.py:20
  239.3 46.0 %copy-start.10 = (f32[1536,512]{1,0:T(8,128)}, f32[1536,512]{1,0:T(8,128)S(1)}, u32[]{:S(2)}) copy-start(f32[1536,512]{1,0:T(8,128)S(1)} %get-tuple-element.471) | copy-start | bytes 9437188
  239.4 46.0 %copy-start.45 = (f32[1536]{0:T(1024)}, f32[1536]{0:T(1024)S(1)}, u32[]{:S(2)}) copy-start(f32[1536]{0:T(1024)S(1)} %broadcast_multiply_fusion.1) | copy-start | bytes 18436
  240.0 45.3 %copy-start.49 = (f32[1536]{0:T(1024)}, f32[1536]{0:T(1024)S(1)}, u32[]{:S(2)}) copy-start(f32[1536]{0:T(1024)S(1)} %fusion.61) | copy-start | bytes 18436
  240.0 9.3 %copy-start.71 = (bf16[2048,512]{1,0:T(8,128)(2,1)S(1)}, bf16[2048,512]{1,0:T(8,128)(2,1)}, u32[]{:S(2)}) copy-start(bf16[2048,512]{1,0:T(8,128)(2,1)} %param.56) | copy-start | bytes 6291460
  447.3 14.8 %copy-start.25 = (bf16[4,1,6,256,128]{3,4,2,1,0:T(8,128)(2,1)S(1)}, bf16[4,1,6,256,128]{3,4,2,1,0:T(8,128)(2,1)}, u32[]{:S(2)}) copy-start(bf16[4,1,6,256,128]{3,4,2,1,0:T(8,128)(2,1)} %get-tuple-element.253) | copy-start | bytes 4718596
  468.1 12.0 %copy-start.3 = (f32[1,6,1024,4,128]{4,3,0,2,1:T(4,128)S(1)}, f32[1,6,1024,4,128]{4,3,0,2,1:T(4,128)}, u32[]{:S(2)}) copy-start(f32[1,6,1024,4,128]{4,3,0,2,1:T(4,128)} %copy.58) | copy-start | bytes 37748740
  501.1 58.6 %collective-permute-start.3 = (bf16[1536,512]{1,0:T(8,128)(2,1)}, bf16[1536,512]{1,0:T(8,128)(2,1)}, u32[]{:S(2)}, u32[]{:S(2)}) collective-permute-start(bf16[1536,512]{1,0:T(8,128)(2,1)} %bitcast.74), channel_id=1, source_target_pairs={{2,0},{4,2},{6,4},{8,6},{10,8},{12,10},{14,12},{16,14},{18,16},{20... | collective-permute-start | bytes 4718600 | tf_op jit(solution)/shard_map/ppermute | solution.py:20
  517.1 11.5 %copy-start.4 = (f32[1,6,1024,4,128]{4,3,0,2,1:T(4,128)S(1)}, f32[1,6,1024,4,128]{4,3,0,2,1:T(4,128)}, u32[]{:S(2)}) copy-start(f32[1,6,1024,4,128]{4,3,0,2,1:T(4,128)} %copy.57) | copy-start | bytes 37748740
  536.6 17.0 %slice-start = ((s8[6291456]{0:T(1024)(128)(4,1)}), s8[2097152]{0:T(1024)(128)(4,1)S(1)}, s32[]{:S(2)}) async-start(s8[6291456]{0:T(1024)(128)(4,1)} %bitcast.346), calls=%async_computation.1 | async-start | bytes 4194304
  542.1 11.5 %slice-start.1 = ((s8[6291456]{0:T(1024)(128)(4,1)}), s8[4194304]{0:T(1024)(128)(4,1)S(1)}, s32[]{:S(2)}) async-start(s8[6291456]{0:T(1024)(128)(4,1)} %bitcast.346), calls=%async_computation.2 | async-start | bytes 8388608
  547.5 15.6 %collective-permute-start.2 = (bf16[1536,512]{1,0:T(8,128)(2,1)S(1)}, bf16[1536,512]{1,0:T(8,128)(2,1)S(1)}, u32[]{:S(2)}, u32[]{:S(2)}) collective-permute-start(bf16[1536,512]{1,0:T(8,128)(2,1)S(1)} %bitcast.345), channel_id=1, source_target_pairs={{2,0},{4,2},{6,4},{8,6},{10,8},{12,10},{14,12},{16,14},{18,16},{20... | collective-permute-start | bytes 4718600 | tf_op jit(solution)/shard_map/ppermute | solution.py:20
  640.1 179.9 %copy-start.1 = (bf16[512,2048]{1,0:T(8,128)(2,1)S(1)}, bf16[512,2048]{1,0:T(8,128)(2,1)}, u32[]{:S(2)}) copy-start(bf16[512,2048]{1,0:T(8,128)(2,1)} %param.54) | copy-start | bytes 6291460
  (77 other events, 250.3 us)
Sparse Core Ops, SparseCore 0:
  566.5 244.2 all-reduce.7
where the time goes:
time: 834 us; the launch traced here: 827 us
  local copies, waits for them, and re-layouts  266 us (32%)
  matrix products  176 us (21%)
  waiting for transfers between devices  167 us (20%)
  other arithmetic  141 us (17%)
  blocking collectives  48.2 us (6%)
  between operations  16.5 us (2%)
  starting transfers between devices  11.3 us (1%)
    psum x1, waiting for transfers between devices, shards(): lax.psum((g_query, g_key, g_value, g_out, g_in, g_bias_in, g_back, g_bias...  167 us
    unnamed x154, local copies, waits for them, and re-layouts  55.9 us
    psum x1, blocking collectives, shards(): lax.psum((g_query, g_key, g_value, g_out, g_in, g_bias_in, g_back, g_bias...  48.2 us
    dot_general x4, matrix products, attend_back(): jnp.einsum('rwqhe,rwkhe->rwhqk', d_out_heads, split_heads(value_pair), pr...  30.3 us
    dynamic_slice x24, local copies, waits for them, and re-layouts, shards(): lax.map(attend, (query_pairs, key_pairs, value_pairs))  30 us
    transpose x2, local copies, waits for them, and re-layouts, from_pairs(): merged = jnp.moveaxis(pairs, 0, 3)  29.4 us
    broadcast_in_dim x8, other arithmetic, scores_of(): return jnp.where(allowed[:, :, None], raw_scores, big_negative)  28.8 us
    another operation x14, local copies, waits for them, and re-layouts, gather_windows(): jnp.stack(pieces, axis=1)  28.4 us
  transfers between devices with their start and end apart: 5, of which 1 were waited for; matrix products, arithmetic and copies ran while one was open for 15% of the time, Pallas kernels for 0%

commit v1 on v0

v1 whole, which is shorter than its diff:
```python
import functools

import jax
import jax.numpy as jnp
from jax import lax
from jax.experimental import pallas as pl
from jax.experimental.pallas import tpu as pltpu
from jax.sharding import PartitionSpec as P

HEAD_DIM = 64
ROW_POS = 192
BLOCK_ROWS = 8
BLOCK_COLS = 32
FLANK_COLS = 16
WINDOWS = ROW_POS // BLOCK_COLS
BLOCKS = ROW_POS // FLANK_COLS
TILE = BLOCK_ROWS * FLANK_COLS
QUERIES = 2 * TILE
SPAN = 4 * TILE
LEN = BLOCK_ROWS * ROW_POS
PADDED = LEN + 2 * TILE

norm_eps = 1e-06
big_negative = -1e30
F32 = jnp.float32
BF16 = jnp.bfloat16
GELU_SCALE = 0.7978845608028654
GELU_CUBE = 0.044715


def dot(left, right):
    return jnp.dot(left, right, preferred_element_type=F32)


def dot_nt(left, right):
    return lax.dot_general(left, right, (((1,), (1,)), ((), ())), preferred_element_type=F32)


def iota(shape, dim):
    return lax.broadcasted_iota(jnp.int32, shape, dim)


def identity(size):
    return jnp.where(iota((size, size), 0) == iota((size, size), 1), 1.0, 0.0).astype(BF16)


def lanes(start, size):
    return pl.ds(pl.multiple_of(start, 128), size)


def transposed(eye, value):
    step = eye.shape[0]
    parts = [
        dot_nt(eye, value[:, at : at + step]).astype(BF16) for at in range(0, value.shape[1], step)
    ]
    return jnp.concatenate(parts, axis=0)


def column(eye, row):
    step = eye.shape[0]
    ones = jnp.ones((128, step), BF16)
    parts = [
        dot_nt(jnp.where(eye > 0, row[:, at : at + step], 0).astype(BF16), ones)
        for at in range(0, row.shape[1], step)
    ]
    return jnp.concatenate(parts, axis=0)


def wide(value):
    return jnp.concatenate([value, value], axis=1)


def halves(value):
    return value[:, :128] + value[:, 128:]


def lane_sums(value):
    ones = jnp.ones((8, 128), BF16)
    high = value.astype(BF16)
    rest = value - high.astype(F32)
    middle = rest.astype(BF16)
    low = (rest - middle.astype(F32)).astype(BF16)
    return dot_nt(ones, high) + dot_nt(ones, middle) + dot_nt(ones, low)


def fill_embed(embed_ref, rows_ref):
    embed = embed_ref[...].astype(F32)
    channel = lax.rem(iota(rows_ref.shape, 0), 3)
    rows_ref[...] = jnp.where(
        channel == 0, embed[0:1], jnp.where(channel == 1, embed[1:2], embed[2:3])
    )


def block_rows(rows_ref, block):
    return rows_ref[:, pl.ds(pl.multiple_of(block * FLANK_COLS, FLANK_COLS), FLANK_COLS), :]


def raw_window(rows_ref, window):
    parts = [block_rows(rows_ref, 2 * window + half).reshape(TILE, -1) for half in range(2)]
    return jnp.concatenate(parts, axis=0)


def embed_window(embed_rows, window):
    parts = []
    for half in range(2):
        at = pl.multiple_of((2 * window + half) * FLANK_COLS, FLANK_COLS)
        part = embed_rows[pl.ds(at, FLANK_COLS), :][None]
        parts.append(jnp.broadcast_to(part, (BLOCK_ROWS,) + part.shape[1:]).reshape(TILE, -1))
    return jnp.concatenate(parts, axis=0)


def start_window(rows_ref, embed_rows, window):
    return raw_window(rows_ref, window).astype(F32) + embed_window(embed_rows, window)


def norm_stats(value):
    center = value - jnp.mean(value, axis=0, keepdims=True)
    spread = jnp.mean(center * center, axis=0, keepdims=True)
    inverse = lax.rsqrt(spread + norm_eps)
    return center * inverse, inverse


def norm_back(normed, inverse, grad, gain):
    scaled = grad * gain
    first = jnp.mean(scaled, axis=0, keepdims=True)
    second = jnp.mean(scaled * normed, axis=0, keepdims=True)
    return (scaled - first - normed * second) * inverse


def vmem():
    return pl.BlockSpec(memory_space=pltpu.VMEM)


def smem():
    return pl.BlockSpec(memory_space=pltpu.SMEM)


def hbm():
    return pl.BlockSpec(memory_space=pl.ANY)


LIMIT = 60 * 1024 * 1024


def head_of_pair(value, half):
    keep = (iota(value.shape, 0) // HEAD_DIM) == half
    return jnp.where(keep, value, jnp.zeros_like(value))


def store_pairs(ref, at, value):
    for pair in range(value.shape[1] // 128):
        ref[pair, pl.ds(at, value.shape[0]), :] = value[:, pair * 128 : (pair + 1) * 128]


def clear_pads_rows(ref):
    pad = jnp.zeros((ref.shape[0], TILE, ref.shape[2]), ref.dtype)
    ref[:, 0:TILE, :] = pad
    ref[:, PADDED - TILE : PADDED, :] = pad


def clear_pads_lanes(ref):
    pad = jnp.zeros((ref.shape[0], TILE), ref.dtype)
    ref[:, 0:TILE] = pad
    ref[:, PADDED - TILE : PADDED] = pad


def attend_kernel(
    place_ref, width_ref, has_ref, tok_ref, up_ref, embed_ref, wq_ref, wk_ref, wv_ref,
    xt_ref, xut_ref, qt_ref, ot_ref, inv_ref, e_ref,
    embed_rows, wqt, wvt, keys, keys_up, vt, vt_up, bias_low, bias_up, e_buf, e_sem,
):
    eye = identity(256)
    fill_embed(embed_ref, embed_rows)
    wqt[...] = transposed(eye, wq_ref[...])
    wvt[...] = transposed(eye, wv_ref[...])
    clear_pads_rows(keys)
    clear_pads_rows(keys_up)
    clear_pads_lanes(vt)
    clear_pads_lanes(vt_up)
    has_up = has_ref[0, 0].astype(F32)
    place = place_ref[0, 0]
    width = width_ref[0, 0]

    @pl.loop(0, WINDOWS)
    def _(window):
        at = pl.multiple_of(window * QUERIES, QUERIES)
        padded_at = pl.multiple_of(window * QUERIES + TILE, TILE)
        low = start_window(tok_ref, embed_rows, window).astype(BF16)
        low_t = transposed(eye, low)
        xt_ref[:, pl.ds(at, QUERIES)] = low_t
        qt_ref[:, pl.ds(at, QUERIES)] = dot(wqt[...], low_t).astype(BF16) * BF16(0.125)
        store_pairs(keys, padded_at, dot(low, wk_ref[...]).astype(BF16))
        vt[:, pl.ds(padded_at, QUERIES)] = dot(wvt[...], low_t).astype(BF16)
        upper = (start_window(up_ref, embed_rows, window) * has_up).astype(BF16)
        upper_t = transposed(eye, upper)
        xut_ref[:, pl.ds(at, QUERIES)] = upper_t
        store_pairs(keys_up, padded_at, dot(upper, wk_ref[...]).astype(BF16))
        vt_up[:, pl.ds(padded_at, QUERIES)] = dot(wvt[...], upper_t).astype(BF16)

    def e_copy(window, slot):
        return pltpu.make_async_copy(e_buf.at[slot], e_ref.at[window], e_sem.at[slot])

    @pl.loop(0, WINDOWS)
    def _(window):
        at = pl.multiple_of(window * QUERIES, QUERIES)
        slot = lax.rem(window, 2)

        @pl.when(window >= 2)
        def _():
            e_copy(window - 2, slot).wait()

        shape = (SPAN, QUERIES)
        memory, query = iota(shape, 0), iota(shape, 1)
        memory_col = (memory // TILE) * FLANK_COLS + memory % FLANK_COLS - FLANK_COLS
        query_col = (query // TILE) * FLANK_COLS + query % FLANK_COLS
        memory_row = (memory % TILE) // FLANK_COLS
        query_row = (query % TILE) // FLANK_COLS
        column_at = memory_col + window * BLOCK_COLS
        inside = (column_at >= 0) & (column_at < width)
        earlier = (memory_row < query_row) | ((memory_row == query_row) & (memory_col <= query_col))
        itself = (memory_row == query_row) & (memory_col == query_col)
        bias_low[...] = jnp.where((inside & earlier) | itself, 0.0, big_negative)
        bias_up[...] = jnp.where(inside & (place > 0), 0.0, big_negative)

        @pl.loop(0, 4)
        def _(pair):
            feats = pl.ds(pl.multiple_of(pair * 128, 128), 128)
            q_pair = qt_ref[feats, pl.ds(at, QUERIES)]
            span = pl.ds(at, SPAN)
            k_low = keys[pair, span, :]
            k_up = keys_up[pair, span, :]
            for half in range(2):
                q_head = head_of_pair(q_pair, half)
                s_up = dot(k_up, q_head) + bias_up[...]
                s_low = dot(k_low, q_head) + bias_low[...]
                peak = jnp.maximum(
                    jnp.max(s_up, axis=0, keepdims=True), jnp.max(s_low, axis=0, keepdims=True)
                )
                r_up = jnp.exp(s_up - peak)
                r_low = jnp.exp(s_low - peak)
                total = jnp.sum(r_up, axis=0, keepdims=True) + jnp.sum(r_low, axis=0, keepdims=True)
                e_up = r_up.astype(BF16)
                e_low = r_low.astype(BF16)
                head = 2 * pair + half
                e_buf[slot, head, 0:SPAN, :] = e_up
                e_buf[slot, head, SPAN : 2 * SPAN, :] = e_low
                mine = pl.ds(pl.multiple_of(pair * 128 + half * HEAD_DIM, HEAD_DIM), HEAD_DIM)
                mixed = dot(vt_up[mine, span], e_up) + dot(vt[mine, span], e_low)
                inverse = 1.0 / total
                ot_ref[mine, pl.ds(at, QUERIES)] = (mixed * inverse).astype(BF16)
                inv_ref[pl.ds(head, 1), pl.ds(at, QUERIES)] = inverse

        e_copy(window, slot).start()

    for last in range(2):
        e_copy(WINDOWS - 2 + last, last).wait()


def feed_kernel(
    tok_ref, cot_ref, embed_ref, ot_ref, inv_ref, wo_ref, wi_ref, bi_ref, wb_ref, bb_ref,
    g1_ref, s1_ref, g2_ref, s2_ref,
    out_ref, dr1_ref, dot_ref, dd_ref, gout_ref, gin_ref, gback_ref, small_ref, gbi_ref,
    embed_rows, wot, wit, wbt, cols, bi_col, acc, acc_bi, n1_buf, y1_buf, slope, yl, df, da, hl, dh,
):
    eye = identity(256)
    fill_embed(embed_ref, embed_rows)
    wot[...] = transposed(eye, wo_ref[...])
    wit[...] = transposed(eye, wi_ref[...])
    wbt[...] = transposed(eye, wb_ref[...])
    for index, ref in enumerate((bb_ref, g1_ref, s1_ref, g2_ref, s2_ref)):
        cols[index] = column(eye, ref[...])
    bi_col[...] = column(eye, bi_ref[...])
    acc[...] = jnp.zeros_like(acc)
    acc_bi[...] = jnp.zeros_like(acc_bi)
    ff = wi_ref.shape[1]
    part = 512

    @pl.loop(0, WINDOWS)
    def _(window):
        here = pl.ds(pl.multiple_of(window * QUERIES, QUERIES), QUERIES)
        raw = raw_window(tok_ref, window)
        embed = embed_window(embed_rows, window).astype(BF16)
        start = jnp.concatenate(
            [
                dot_nt(eye, raw[:, half * 256 : half * 256 + 256])
                + dot_nt(eye, embed[:, half * 256 : half * 256 + 256])
                for half in range(2)
            ],
            axis=0,
        )
        n1, inv1 = norm_stats(start + dot(wot[...], ot_ref[:, here]))
        y1 = n1 * wide(cols[1]) + wide(cols[2])
        low = y1.astype(BF16)
        n1_buf[...] = n1
        y1_buf[...] = y1
        yl[:, here] = low

        @pl.loop(0, ff // part)
        def _(index):
            rows = pl.ds(pl.multiple_of(index * part, part), part)
            u = dot(wit[rows, :], low) + wide(bi_col[rows, :])
            square = u * u
            t = jnp.tanh(GELU_SCALE * u * (1.0 + GELU_CUBE * square))
            half_up = 0.5 * (1.0 + t)
            hl[rows, here] = (u * half_up).astype(BF16)
            slope[rows, :] = half_up + (0.5 * GELU_SCALE) * u * (1.0 - t * t) * (
                1.0 + 3.0 * GELU_CUBE * square
            )

        f = dot(wbt[...], hl[:, here]) + wide(cols[0])
        n2, inv2 = norm_stats(y1_buf[...] + f)
        g2 = wide(cols[3])
        result = (n2 * g2 + wide(cols[4])).astype(BF16)
        result = dot_nt(eye, result).astype(BF16)
        for half in range(2):
            at = pl.multiple_of((2 * window + half) * FLANK_COLS, FLANK_COLS)
            out_ref[:, pl.ds(at, FLANK_COLS), :] = result[half * TILE : half * TILE + TILE].reshape(
                BLOCK_ROWS, FLANK_COLS, -1
            )
        raw_cot = raw_window(cot_ref, window)
        cot = jnp.concatenate(
            [dot_nt(eye, raw_cot[:, half * 256 : half * 256 + 256]) for half in range(2)], axis=0
        )
        acc[0] += halves(cot * n2)
        acc[1] += halves(cot)
        dr2 = norm_back(n2, inv2, cot, g2)
        df_low = dr2.astype(BF16)
        acc[2] += halves(df_low.astype(F32))
        df[:, here] = df_low

        @pl.loop(0, ff // part)
        def _(index):
            rows = pl.ds(pl.multiple_of(index * part, part), part)
            dh_low = (dot(wb_ref[rows, :], df_low) * slope[rows, :]).astype(BF16)
            dh[rows, here] = dh_low
            acc_bi[rows, :] += halves(dh_low.astype(F32))

        dy1 = dr2 + dot(wi_ref[...], dh[:, here])
        n1 = n1_buf[...]
        acc[3] += halves(dy1 * n1)
        acc[4] += halves(dy1)
        dr1 = norm_back(n1, inv1, dy1, wide(cols[1]))
        dr1_ref[:, here] = dr1
        da_low = dr1.astype(BF16)
        da[:, here] = da_low
        d_o = dot(wo_ref[...], da_low)
        product = d_o * ot_ref[:, here].astype(F32)
        for head in range(8):
            rows = slice(head * HEAD_DIM, head * HEAD_DIM + HEAD_DIM)
            inverse = inv_ref[head : head + 1, here]
            dot_ref[rows, here] = (d_o[rows] * inverse).astype(BF16)
            dd_ref[head : head + 1, here] = (
                jnp.sum(product[rows], axis=0, keepdims=True) * inverse
            )

    @pl.loop(0, ff // 256)
    def _(index):
        rows = pl.ds(pl.multiple_of(index * 256, 256), 256)
        gback_ref[rows, :] = dot_nt(hl[rows, :], df[...])
        gin_ref[:, rows] = dot_nt(yl[...], dh[rows, :])

    gout_ref[...] = dot_nt(ot_ref[...], da[...])
    for index in range(5):
        small_ref[index : index + 1, :] = lane_sums(acc[index])[0:1]
    gbi_ref[...] = lane_sums(acc_bi[...])[0:1]


def back_kernel(
    has_ref, tok_ref, up_ref, embed_ref, wq_ref, wk_ref, wv_ref, xt_ref, xut_ref, qt_ref,
    e_ref, dot_ref, dd_ref, dr1_ref,
    dx_ref, dxu_ref, gq_ref, gk_ref, gv_ref,
    embed_rows, wkt, vals, vals_up, kt, kt_up, dqt, dkt, dvt, dkt_up, dvt_up, e_buf, e_sem,
):
    eye = identity(256)
    fill_embed(embed_ref, embed_rows)
    wkt[...] = transposed(eye, wk_ref[...])
    clear_pads_rows(vals)
    clear_pads_rows(vals_up)
    clear_pads_lanes(kt)
    clear_pads_lanes(kt_up)
    for ref in (dkt, dvt, dkt_up, dvt_up):
        ref[...] = jnp.zeros_like(ref)
    has_up = has_ref[0, 0].astype(F32)

    def e_copy(window, slot):
        return pltpu.make_async_copy(e_ref.at[window], e_buf.at[slot], e_sem.at[slot])

    e_copy(0, 0).start()

    @pl.loop(0, WINDOWS)
    def _(window):
        here = pl.ds(pl.multiple_of(window * QUERIES, QUERIES), QUERIES)
        padded_at = pl.multiple_of(window * QUERIES + TILE, TILE)
        low = start_window(tok_ref, embed_rows, window).astype(BF16)
        store_pairs(vals, padded_at, dot(low, wv_ref[...]).astype(BF16))
        kt[:, pl.ds(padded_at, QUERIES)] = dot(wkt[...], xt_ref[:, here]).astype(BF16)
        upper = (start_window(up_ref, embed_rows, window) * has_up).astype(BF16)
        store_pairs(vals_up, padded_at, dot(upper, wv_ref[...]).astype(BF16))
        kt_up[:, pl.ds(padded_at, QUERIES)] = dot(wkt[...], xut_ref[:, here]).astype(BF16)

    @pl.loop(0, WINDOWS)
    def _(window):
        at = pl.multiple_of(window * QUERIES, QUERIES)
        here = pl.ds(at, QUERIES)
        span = pl.ds(at, SPAN)
        slot = lax.rem(window, 2)

        @pl.when(window + 1 < WINDOWS)
        def _():
            e_copy(window + 1, 1 - slot).start()

        e_copy(window, slot).wait()

        @pl.loop(0, 4)
        def _(pair):
            feats = pl.ds(pl.multiple_of(pair * 128, 128), 128)
            do_pair = dot_ref[feats, here]
            v_low = vals[pair, span, :]
            v_up = vals_up[pair, span, :]
            for half in range(2):
                head = 2 * pair + half
                mine = pl.ds(pl.multiple_of(pair * 128 + half * HEAD_DIM, HEAD_DIM), HEAD_DIM)
                do_head = head_of_pair(do_pair, half)
                inner = dd_ref[pl.ds(head, 1), here]
                e_up = e_buf[slot, head, 0:SPAN, :]
                e_low = e_buf[slot, head, SPAN : 2 * SPAN, :]
                ds_up = (e_up.astype(F32) * (dot(v_up, do_head) - inner)).astype(BF16)
                ds_low = (e_low.astype(F32) * (dot(v_low, do_head) - inner)).astype(BF16)
                dq = dot(kt_up[mine, span], ds_up) + dot(kt[mine, span], ds_low)
                dqt[mine, here] = (dq * 0.125).astype(BF16)
                q_head = qt_ref[mine, here]
                do_mine = dot_ref[mine, here]
                dkt[mine, span] += dot_nt(q_head, ds_low)
                dkt_up[mine, span] += dot_nt(q_head, ds_up)
                dvt[mine, span] += dot_nt(do_mine, e_low)
                dvt_up[mine, span] += dot_nt(do_mine, e_up)

    inner = slice(TILE, PADDED - TILE)
    xt, xut = xt_ref[...], xut_ref[...]
    gq_ref[...] = dot_nt(xt, dqt[...])
    dk_low, dv_low = dkt[:, inner].astype(BF16), dvt[:, inner].astype(BF16)
    dk_up, dv_up = dkt_up[:, inner].astype(BF16), dvt_up[:, inner].astype(BF16)
    gk_ref[...] = dot_nt(xt, dk_low) + dot_nt(xut, dk_up)
    gv_ref[...] = dot_nt(xt, dv_low) + dot_nt(xut, dv_up)
    dxu_ref[...] = (dot(wk_ref[...], dk_up) + dot(wv_ref[...], dv_up)).astype(BF16)
    dx_ref[...] = (
        dr1_ref[...] + dot(wq_ref[...], dqt[...]) + dot(wk_ref[...], dk_low) + dot(wv_ref[...], dv_low)
    )


def finish_kernel(dx_ref, below_ref, gt_ref, ge_ref):
    eye = identity(256)
    sums = [0.0, 0.0, 0.0]
    for window in range(WINDOWS):
        here = slice(window * QUERIES, window * QUERIES + QUERIES)
        dx = dx_ref[:, here] + below_ref[:, here].astype(F32)
        for half in range(2):
            kind = (2 * window + half) % 3
            sums[kind] = sums[kind] + dx[:, half * TILE : half * TILE + TILE]
        rows = dot_nt(eye, dx.astype(BF16)).astype(BF16)
        for half in range(2):
            at = (2 * window + half) * FLANK_COLS
            gt_ref[:, at : at + FLANK_COLS, :] = rows[half * TILE : half * TILE + TILE].reshape(
                BLOCK_ROWS, FLANK_COLS, -1
            )
    lane = iota(sums[0].shape, 1) % FLANK_COLS
    for channel in range(3):
        total = 0.0
        for kind in range(3):
            total = total + jnp.where((lane + kind) % 3 == channel, sums[kind], 0.0)
        ge_ref[channel : channel + 1, :] = lane_sums(total)[0:1]


def passed_along(value, axis, steps):
    count = lax.axis_size(axis)
    leading, last = (max(0, -steps), min(count, count - steps))
    return lax.ppermute(value, axis, [(source, source + steps) for source in range(leading, last)])


def shards(
    tokens, row_place, row_width, cotangent, chan_embed, w_query, w_key, w_value, w_out, w_in,
    bias_in, w_back, bias_back, gain_first, shift_first, gain_second, shift_second,
):
    width = tokens.shape[3]
    ff = w_in.shape[1]
    tok = tokens.reshape(BLOCK_ROWS, ROW_POS, width)
    cot = cotangent.reshape(BLOCK_ROWS, ROW_POS, width)
    up = passed_along(tok, "band", 1)
    has_up = (lax.axis_index("band") > 0).astype(jnp.int32).reshape(1, 1)
    shape = jax.ShapeDtypeStruct
    params = pltpu.CompilerParams(vmem_limit_bytes=LIMIT)
    xt, xut, qt, ot, inv, e_all = pl.pallas_call(
        attend_kernel,
        name="attend_forward",
        out_shape=(
            shape((width, LEN), BF16),
            shape((width, LEN), BF16),
            shape((width, LEN), BF16),
            shape((width, LEN), BF16),
            shape((8, LEN), F32),
            shape((WINDOWS, 8, 2 * SPAN, QUERIES), BF16),
        ),
        in_specs=[smem()] * 3 + [vmem()] * 6,
        out_specs=(vmem(), vmem(), vmem(), vmem(), vmem(), hbm()),
        scratch_shapes=[
            pltpu.VMEM((ROW_POS, width), F32),
            pltpu.VMEM((width, width), BF16),
            pltpu.VMEM((width, width), BF16),
            pltpu.VMEM((4, PADDED, 128), BF16),
            pltpu.VMEM((4, PADDED, 128), BF16),
            pltpu.VMEM((width, PADDED), BF16),
            pltpu.VMEM((width, PADDED), BF16),
            pltpu.VMEM((SPAN, QUERIES), F32),
            pltpu.VMEM((SPAN, QUERIES), F32),
            pltpu.VMEM((2, 8, 2 * SPAN, QUERIES), BF16),
            pltpu.SemaphoreType.DMA((2,)),
        ],
        compiler_params=params,
    )(row_place, row_width, has_up, tok, up, chan_embed, w_query, w_key, w_value)
    row = lambda value: value.reshape(1, -1)
    layer_out, dr1, do_t, dd, g_out, g_in, g_back, small, g_bias_in = pl.pallas_call(
        feed_kernel,
        name="feed_forward_and_back",
        out_shape=(
            shape((BLOCK_ROWS, ROW_POS, width), BF16),
            shape((width, LEN), F32),
            shape((width, LEN), BF16),
            shape((8, LEN), F32),
            shape((width, width), F32),
            shape((width, ff), F32),
            shape((ff, width), F32),
            shape((5, width), F32),
            shape((1, ff), F32),
        ),
        in_specs=[vmem()] * 14,
        out_specs=(vmem(),) * 9,
        scratch_shapes=[
            pltpu.VMEM((ROW_POS, width), F32),
            pltpu.VMEM((width, width), BF16),
            pltpu.VMEM((ff, width), BF16),
            pltpu.VMEM((width, ff), BF16),
            pltpu.VMEM((5, width, 128), F32),
            pltpu.VMEM((ff, 128), F32),
            pltpu.VMEM((5, width, 128), F32),
            pltpu.VMEM((ff, 128), F32),
            pltpu.VMEM((width, QUERIES), F32),
            pltpu.VMEM((width, QUERIES), F32),
            pltpu.VMEM((ff, QUERIES), F32),
            pltpu.VMEM((width, LEN), BF16),
            pltpu.VMEM((width, LEN), BF16),
            pltpu.VMEM((width, LEN), BF16),
            pltpu.VMEM((ff, LEN), BF16),
            pltpu.VMEM((ff, LEN), BF16),
        ],
        compiler_params=params,
    )(
        tok, cot, chan_embed, ot, inv, w_out, w_in, row(bias_in), w_back, row(bias_back),
        row(gain_first), row(shift_first), row(gain_second), row(shift_second),
    )
    dx, dxu, g_query, g_key, g_value = pl.pallas_call(
        back_kernel,
        name="attend_backward",
        out_shape=(
            shape((width, LEN), F32),
            shape((width, LEN), BF16),
            shape((width, width), F32),
            shape((width, width), F32),
            shape((width, width), F32),
        ),
        in_specs=[smem()] + [vmem()] * 9 + [hbm()] + [vmem()] * 3,
        out_specs=(vmem(),) * 5,
        scratch_shapes=[
            pltpu.VMEM((ROW_POS, width), F32),
            pltpu.VMEM((width, width), BF16),
            pltpu.VMEM((4, PADDED, 128), BF16),
            pltpu.VMEM((4, PADDED, 128), BF16),
            pltpu.VMEM((width, PADDED), BF16),
            pltpu.VMEM((width, PADDED), BF16),
            pltpu.VMEM((width, LEN), BF16),
            pltpu.VMEM((width, PADDED), F32),
            pltpu.VMEM((width, PADDED), F32),
            pltpu.VMEM((width, PADDED), F32),
            pltpu.VMEM((width, PADDED), F32),
            pltpu.VMEM((2, 8, 2 * SPAN, QUERIES), BF16),
            pltpu.SemaphoreType.DMA((2,)),
        ],
        compiler_params=params,
    )(has_up, tok, up, chan_embed, w_query, w_key, w_value, xt, xut, qt, e_all, do_t, dd, dr1)
    below = passed_along(dxu, "band", -1)
    grad_tokens, g_embed = pl.pallas_call(
        finish_kernel,
        name="finish",
        out_shape=(shape((BLOCK_ROWS, ROW_POS, width), BF16), shape((3, width), F32)),
        in_specs=[vmem()] * 2,
        out_specs=(vmem(),) * 2,
        compiler_params=params,
    )(dx, below)

    def shared(grad):
        part = lax.psum_scatter(grad.astype(BF16), "band", scatter_dimension=0, tiled=True)
        return lax.psum(part.astype(F32), "grp")

    band_index = lax.axis_index("band")
    band_size = lax.axis_size("band")

    def share_of(full_sum, axis_dim):
        size = full_sum.shape[axis_dim] // band_size
        return lax.dynamic_slice_in_dim(full_sum, band_index * size, size, axis_dim)

    small_sum, bias_in_sum, embed_sum = lax.psum((small, g_bias_in, g_embed), ("band", "grp"))
    vector = lambda index: share_of(small_sum[index], 0)
    return (
        layer_out.reshape(tokens.shape),
        grad_tokens.reshape(tokens.shape),
        shared(g_query),
        shared(g_key),
        shared(g_value),
        shared(g_out),
        shared(g_in),
        share_of(bias_in_sum[0], 0),
        shared(g_back),
        vector(2),
        vector(3),
        vector(4),
        vector(0),
        vector(1),
        share_of(embed_sum, 1),
    )


def solution(mesh):
    tall = P("grp", "band", None, None)
    return jax.shard_map(
        shards,
        mesh=mesh,
        in_specs=(tall, P("grp", "band"), P("grp", "band"), tall) + (P(),) * 13,
        out_specs=(tall, tall)
        + (P("band", None),) * 5
        + (P("band"), P("band", None))
        + (P("band"),) * 5
        + (P(None, "band"),),
        check_vma=False,
    )
```

time: 834 us -> 594 us (0.71)
  local copies, waits for them, and re-layouts: 266 us -> 14.6 us
  matrix products: 176 us -> 0 us
  Pallas kernels: 0 us -> 169 us
  waiting for transfers between devices: 167 us -> 316 us
  other arithmetic: 141 us -> 12.5 us
  blocking collectives: 48.2 us -> 62.3 us
    reduce_scatter x0 -> x6, waiting for transfers between devices: none -> 316 us  [shared(): lax.psum_scatter(grad.astype(BF16), 'band', scatter_dimension=0, tiled=True)]
    dot_general x50 -> x0, matrix products: 176 us -> none  [the longest x4 30.3 us: attend_back(): jnp.einsum('rwqhe,rwkhe->rwhqk', d_out_heads, split_heads(value_pair), pr...]
    pallas_call x0 -> x4, Pallas kernels: none -> 169 us  [the longest x1 61.1 us: shards(): pl.pallas_call(feed_kernel, name='feed_forward_and_back', out_shape=(shap...]
    psum x1 -> x0, waiting for transfers between devices: 167 us -> none  [shards(): lax.psum((g_query, g_key, g_value, g_out, g_in, g_bias_in, g_back, g_bias...]
    unnamed x154 -> x24, local copies, waits for them, and re-layouts: 55.9 us -> 4.07 us
    dynamic_slice x37 -> x5, local copies, waits for them, and re-layouts: 43.3 us -> 2.92 us  [share_of(): return lax.dynamic_slice_in_dim(full_sum, band_index * size, size, axis_dim)]
    another operation x20 -> x0, local copies, waits for them, and re-layouts: 37.8 us -> none  [the longest x14 28.4 us: gather_windows(): jnp.stack(pieces, axis=1)]
    transpose x2 -> x0, local copies, waits for them, and re-layouts: 29.4 us -> none  [from_pairs(): merged = jnp.moveaxis(pairs, 0, 3)]
  transfers between devices with their start and end apart: 5 -> 8, of which waited for: 1 -> 6; matrix products, arithmetic and copies ran while one was open for 15% -> 4% of each run, Pallas kernels for 0% -> 1%
where the time goes in v1:
time: 594 us; the launch traced here: 593 us
  waiting for transfers between devices  316 us (53%)
  Pallas kernels  169 us (28%)
  blocking collectives  62.3 us (10%)
  between operations  15.5 us (3%)
  local copies, waits for them, and re-layouts  14.6 us (2%)
  other arithmetic  12.5 us (2%)
    reduce_scatter x6, waiting for transfers between devices, shared(): lax.psum_scatter(grad.astype(BF16), 'band', scatter_dimension=0, tiled=True)  316 us
    pallas_call x1, Pallas kernels, shards(): pl.pallas_call(feed_kernel, name='feed_forward_and_back', out_shape=(shap...  61.1 us
    pallas_call x1, Pallas kernels, shards(): pl.pallas_call(back_kernel, name='attend_backward', out_shape=(shape((wid...  53.7 us
    pallas_call x1, Pallas kernels, shards(): pl.pallas_call(attend_kernel, name='attend_forward', out_shape=(shape((wi...  49.6 us
    psum x1, blocking collectives, shards(): lax.psum((small, g_bias_in, g_embed), ('band', 'grp'))  40.7 us
    psum x1, blocking collectives, shared(): return lax.psum(part.astype(F32), 'grp')  21.6 us
    convert_element_type x6, other arithmetic, shared(): grad.astype(BF16)  12.5 us
  transfers between devices with their start and end apart: 8, of which 6 were waited for; matrix products, arithmetic and copies ran while one was open for 4% of the time, Pallas kernels for 1%

profile of v1, /device:TPU:0, one launch (start us, length us, event | category | flops | bytes accessed | tf_op | source)
XLA Modules:
  0.0 593.4 jit_solution(5394871980392214835)
XLA Ops:
  7.2 2.5 collective-permute-start
  11.0 1.3 reshape.75.bi_ref
  12.3 1.3 reshape.76.bb_ref
  13.5 1.3 reshape.77.g1_ref
  14.8 1.3 reshape.78.s1_ref
  16.1 1.3 reshape.79.g2_ref
  17.3 1.2 reshape.80.s2_ref
  19.7 49.6 %attend_forward.1 = (bf16[512,1536]{1,0:T(8,128)(2,1)}, bf16[512,1536]{1,0:T(8,128)(2,1)}, bf16[512,1536]{1,0:T(8,128)(2,1)}, bf16[512,1536]{1,0:T(8,128)(2,1)},...) custom-call(s32[1,1]{1,0:T(1,128)S(6)} %copy.44.place_ref, s32[1,1]{1,0:T(1,128)S(6)} %copy.45.width_ref, ...), custom_call_target="tpu_custom_call" | custom-call | tf_op jit(solution)/shard_map/attend_forward/pallas_call | solution.py:492
  69.3 61.1 %feed_forward_and_back.1 = (bf16[8,192,512]{2,1,0:T(8,128)(2,1)}, f32[512,1536]{1,0:T(8,128)}, bf16[512,1536]{1,0:T(8,128)(2,1)}, f32[8,1536]{1,0:T(8,128)}, f32...) custom-call(bf16[8,192,512]{2,1,0:T(8,128)(2,1)} %bitcast.19, ...), custom_call_target="tpu_custom_call" | custom-call | tf_op jit(solution)/shard_map/feed_forward_and_back/pallas_call | solution.py:521
  130.3 53.7 %attend_backward.1 = (f32[512,1536]{1,0:T(8,128)}, bf16[512,1536]{1,0:T(8,128)(2,1)}, f32[512,512]{1,0:T(8,128)}, f32[512,512]{1,0:T(8,128)}, f32[512,512]{1,0:T(8,128)}) custom-call(s32[1,1]{1,0:T(1,128)} %bitcast.2.has_ref, bf16[8,192,512]{2,1,0:T(8,128)(2,1)} %bitcast.20, bf16[8,192,512]{2,1,0:T(8,128)(2,1)} %copy-done, bf16[3,512]{1,0:T(4,128)(2,1)} %embed_ref.5, ...), custom_call_target="tpu_custom_call" | custom-call | tf_op jit(solution)/shard_map/attend_backward/pallas_call | solution.py:560
  184.1 2.2 convert_element_type.37
  189.5 3.9 convert_element_type.45
  193.5 3.8 convert_element_type.47
  197.3 1.4 copy-done.11
  198.7 1.3 collective-permute-start.1
  200.0 60.2 %reduce-scatter.7.cloned.1.call-done = bf16[32,512]{1,0:T(8,128)(2,1)} async-done(((bf16[512,512]{1,0:T(8,128)(2,1)}), bf16[32,512]{1,0:T(8,128)(2,1)}) %reduce-scatter.7.cloned.1.call-update) | async-done | bytes 32784 | tf_op jit(solution)/shard_map/reduce_scatter | solution.py:600
  260.1 58.8 %reduce-scatter.9.cloned.1.call-done = bf16[32,512]{1,0:T(8,128)(2,1)} async-done(((bf16[512,512]{1,0:T(8,128)(2,1)}), bf16[32,512]{1,0:T(8,128)(2,1)}) %reduce-scatter.9.cloned.1.call-update) | async-done | bytes 32784 | tf_op jit(solution)/shard_map/reduce_scatter | solution.py:600
  318.9 58.4 %reduce-scatter.11.cloned.1.call-done = bf16[32,512]{1,0:T(8,128)(2,1)} async-done(((bf16[512,512]{1,0:T(8,128)(2,1)}), bf16[32,512]{1,0:T(8,128)(2,1)}) %reduce-scatter.11.cloned.1.call-update) | async-done | bytes 32784 | tf_op jit(solution)/shard_map/reduce_scatter | solution.py:600
  377.3 58.6 %reduce-scatter.13.cloned.1.call-done = bf16[32,512]{1,0:T(8,128)(2,1)} async-done(((bf16[512,512]{1,0:T(8,128)(2,1)}), bf16[32,512]{1,0:T(8,128)(2,1)}) %reduce-scatter.13.cloned.1.call-update) | async-done | bytes 32784 | tf_op jit(solution)/shard_map/reduce_scatter | solution.py:600
  437.1 4.3 finish.1
  441.5 40.7 %all-reduce = (f32[1,2048]{1,0:T(1,128)S(1)}, f32[5,512]{1,0:T(8,128)S(1)}, f32[3,512]{1,0:T(4,128)S(1)}) all-reduce(f32[1,2048]{1,0:T(1,128)S(1)} %copy-done.10, f32[5,512]{1,0:T(8,128)S(1)} %copy-done.9, f32[3,512]{1,0:T(4,128)} %get-tuple-element.58), channel_id=1, replica_groups=mesh['band'=16,'grp'=2] {'band','grp'}, use_global_device_ids=true, to_apply=%region_10.0 | all-reduce | flops 6144 | bytes 49152 | tf_op jit(solution)/shard_map/psum | solution.py:610
  485.1 15.1 %reduce-scatter.15.cloned.1.call-done = bf16[32,2048]{1,0:T(8,128)(2,1)} async-done(((bf16[512,2048]{1,0:T(8,128)(2,1)}), bf16[32,2048]{1,0:T(8,128)(2,1)}) %reduce-scatter.15.cloned.1.call-update) | async-done | bytes 131088 | tf_op jit(solution)/shard_map/reduce_scatter | solution.py:600
  500.3 64.6 %reduce-scatter.17.cloned.1.call-done = bf16[128,512]{1,0:T(8,128)(2,1)} async-done(((bf16[2048,512]{1,0:T(8,128)(2,1)}), bf16[128,512]{1,0:T(8,128)(2,1)}) %reduce-scatter.17.cloned.1.call-update) | async-done | bytes 131088 | tf_op jit(solution)/shard_map/reduce_scatter | solution.py:600
  564.9 21.6 %all-reduce.3 = (f32[32,512]{1,0:T(8,128)}, f32[32,512]{1,0:T(8,128)}, f32[32,512]{1,0:T(8,128)}, f32[32,512]{1,0:T(8,128)}, f32[32,2048]{1,0:T(8,128)}, /*index=5*/f32[128,512]{1,0:T(8,128)}) all-reduce(bf16[32,512]{1,0:T(8,128)(2,1)S(1)} %copy-done.5, bf16[32,512]{1,0:T(8,128)(2,1)S(1)} %copy-done.6, ...), channel_id=1, replica_groups=mesh['band'=16,'grp'=2] {'grp'}, use_global_device_ids=true, to_apply=%region_1.0 | all-reduce | flops 196608 | bytes 1179648 | tf_op jit(solution)/shard_map/psum | solution.py:601
  (46 shorter events, 8.6 us)
Async XLA Ops:
  7.2 253.0 %reduce-scatter.7.cloned.1.call-start = ((), (), s32[]{:S(2)}) async-start(), calls=%async_computation.6 | async-start | bytes 557056 | tf_op jit(solution)/shard_map/reduce_scatter | solution.py:600
  7.2 11.3 %collective-permute-start = (bf16[8,192,512]{2,1,0:T(8,128)(2,1)}, bf16[8,192,512]{2,1,0:T(8,128)(2,1)S(1)}, u32[]{:S(2)}, u32[]{:S(2)}) collective-permute-start(bf16[8,192,512]{2,1,0:T(8,128)(2,1)} %bitcast.17), channel_id=1, source_target_pairs={{0,2},{2,4},{4,6},{6,8},{8,10},{10,12},{12,14},{14,16},{16,18},{18... | collective-permute-start | bytes 4718600 | tf_op jit(solution)/shard_map/ppermute | solution.py:477
  18.6 1.1 copy-start
  184.0 2.3 copy-start.4
  186.2 1.4 copy-start.3
  186.3 132.7 %reduce-scatter.9.cloned.1.call-start = ((), (), s32[]{:S(2)}) async-start(), calls=%async_computation.7 | async-start | bytes 557056 | tf_op jit(solution)/shard_map/reduce_scatter | solution.py:600
  187.2 1.4 copy-start.2
  187.2 190.1 %reduce-scatter.11.cloned.1.call-start = ((), (), s32[]{:S(2)}) async-start(), calls=%async_computation.8 | async-start | bytes 557056 | tf_op jit(solution)/shard_map/reduce_scatter | solution.py:600
  188.5 247.4 %reduce-scatter.13.cloned.1.call-start = ((), (), s32[]{:S(2)}) async-start(), calls=%async_computation.9 | async-start | bytes 557056 | tf_op jit(solution)/shard_map/reduce_scatter | solution.py:600
  189.5 310.8 %reduce-scatter.15.cloned.1.call-start = ((), (), s32[]{:S(2)}) async-start(), calls=%async_computation.10 | async-start | bytes 2228224 | tf_op jit(solution)/shard_map/reduce_scatter | solution.py:600
  193.4 371.5 %reduce-scatter.17.cloned.1.call-start = ((), (), s32[]{:S(2)}) async-start(), calls=%async_computation.11 | async-start | bytes 2228224 | tf_op jit(solution)/shard_map/reduce_scatter | solution.py:600
  197.3 1.4 copy-start.11
  198.7 237.3 %collective-permute-start.1 = (bf16[512,1536]{1,0:T(8,128)(2,1)S(1)}, bf16[512,1536]{1,0:T(8,128)(2,1)S(1)}, u32[]{:S(2)}, u32[]{:S(2)}) collective-permute-start(bf16[512,1536]{1,0:T(8,128)(2,1)S(1)} %copy-done.11), channel_id=1, source_target_pairs={{2,0},{4,2},{6,4},{8,6},{10,8},{12,10},{14,12},{16,14},{18,16},{20... | collective-permute-start | bytes 4718600 | tf_op jit(solution)/shard_map/ppermute | solution.py:477
  435.9 1.2 copy-start.1
  437.1 4.4 copy-start.9
  437.1 4.4 copy-start.10
  437.1 127.8 %copy-start.5 = (bf16[32,512]{1,0:T(8,128)(2,1)S(1)}, bf16[32,512]{1,0:T(8,128)(2,1)}, u32[]{:S(2)}) copy-start(bf16[32,512]{1,0:T(8,128)(2,1)} %reduce-scatter.7.cloned.1.call-done) | copy-start | bytes 98308
  437.1 127.8 %copy-start.6 = (bf16[32,512]{1,0:T(8,128)(2,1)S(1)}, bf16[32,512]{1,0:T(8,128)(2,1)}, u32[]{:S(2)}) copy-start(bf16[32,512]{1,0:T(8,128)(2,1)} %reduce-scatter.9.cloned.1.call-done) | copy-start | bytes 98308
  437.1 127.8 %copy-start.7 = (bf16[32,512]{1,0:T(8,128)(2,1)S(1)}, bf16[32,512]{1,0:T(8,128)(2,1)}, u32[]{:S(2)}) copy-start(bf16[32,512]{1,0:T(8,128)(2,1)} %reduce-scatter.11.cloned.1.call-done) | copy-start | bytes 98308
  437.1 127.8 %copy-start.8 = (bf16[32,512]{1,0:T(8,128)(2,1)S(1)}, bf16[32,512]{1,0:T(8,128)(2,1)}, u32[]{:S(2)}) copy-start(bf16[32,512]{1,0:T(8,128)(2,1)} %reduce-scatter.13.cloned.1.call-done) | copy-start | bytes 98308
Sparse Core Ops, SparseCore 0:
  186.4 73.7 reduce-scatter.6
  264.1 54.7 reduce-scatter.8
  322.5 54.7 reduce-scatter.10
  381.1 54.7 reduce-scatter.12
  439.5 60.6 reduce-scatter.14
  504.3 60.5 reduce-scatter.16

commit v2 on v1

--- a/solution.py
+++ b/solution.py
@@ -162,6 +162,134 @@
     pad = jnp.zeros((ref.shape[0], TILE), ref.dtype)
     ref[:, 0:TILE] = pad
     ref[:, PADDED - TILE : PADDED] = pad
+
+
+def reversed_bits(index, count):
+    place, bit = 0, 1
+    while bit < count:
+        place = place + (index // bit) % 2 * (count // (2 * bit))
+        bit *= 2
+    return place
+
+
+def levels(count):
+    return count.bit_length() - 1
+
+
+class Reduction:
+    def __init__(self, buf, recv, across, send_sem, recv_sem, band, grp, size, groups):
+        self.buf, self.recv, self.across = buf, recv, across
+        self.send_sem, self.recv_sem = send_sem, recv_sem
+        self.band, self.grp, self.size, self.groups = band, grp, size, groups
+        self.levels = levels(size)
+
+    def region(self, stage):
+        start = 0
+        for level in range(stage):
+            start = start + (self.band // (1 << level)) % 2 * (self.size >> (level + 1))
+        return start
+
+    def copies(self, stage):
+        if stage < self.levels:
+            half = self.size >> (stage + 1)
+            bit = (self.band // (1 << stage)) % 2
+            source = self.region(stage) + (1 - bit) * half
+            return [
+                pltpu.make_async_remote_copy(
+                    src_ref=self.buf.at[pl.ds(source, half)],
+                    dst_ref=self.recv.at[pl.ds(half, half)],
+                    send_sem=self.send_sem(stage),
+                    recv_sem=self.recv_sem(stage),
+                    device_id=(self.band + (1 << stage) * (1 - 2 * bit), self.grp),
+                    device_id_type=pl.DeviceIdType.MESH,
+                )
+            ]
+        return [
+            pltpu.make_async_remote_copy(
+                src_ref=self.buf.at[self.region(self.levels)],
+                dst_ref=self.across.at[step],
+                send_sem=self.send_sem(self.levels + step - 1),
+                recv_sem=self.recv_sem(self.levels + step - 1),
+                device_id=(self.band, (self.grp + step) % self.groups),
+                device_id_type=pl.DeviceIdType.MESH,
+            )
+            for step in range(1, self.groups)
+        ]
+
+    def start(self, stage):
+        for copy in self.copies(stage):
+            copy.start()
+
+    def advance(self, stage):
+        for copy in self.copies(stage):
+            copy.wait()
+        half = self.size >> (stage + 1)
+        keep = self.region(stage + 1)
+
+        @pl.loop(0, half)
+        def _(index):
+            total = self.buf[keep + index].astype(F32) + self.recv[half + index].astype(F32)
+            self.buf[keep + index] = total.astype(BF16)
+
+        self.start(stage + 1)
+
+    def finish(self):
+        for copy in self.copies(self.levels):
+            copy.wait()
+        self.across[0] = self.buf[self.region(self.levels)]
+        total = 0.0
+        for member in range(self.groups):
+            total = total + self.across[(self.grp + self.groups - member) % self.groups].astype(F32)
+        return total
+
+
+class SmallSum:
+    def __init__(self, buf, recv, send_sem, recv_sem, band, grp, size, groups):
+        self.buf, self.recv, self.send_sem, self.recv_sem = buf, recv, send_sem, recv_sem
+        self.band, self.grp, self.size, self.groups = band, grp, size, groups
+        self.levels = levels(size)
+
+    def copies(self, stage):
+        if stage < self.levels:
+            bit = (self.band // (1 << stage)) % 2
+            partners = [(stage, (self.band + (1 << stage) * (1 - 2 * bit), self.grp))]
+        else:
+            partners = [
+                (self.levels + step - 1, (self.band, (self.grp + step) % self.groups))
+                for step in range(1, self.groups)
+            ]
+        return [
+            pltpu.make_async_remote_copy(
+                src_ref=self.buf.at[stage],
+                dst_ref=self.recv.at[slot],
+                send_sem=self.send_sem.at[slot],
+                recv_sem=self.recv_sem.at[slot],
+                device_id=partner,
+                device_id_type=pl.DeviceIdType.MESH,
+            )
+            for slot, partner in partners
+        ]
+
+    def start(self, stage):
+        for copy in self.copies(stage):
+            copy.start()
+
+    def advance(self, stage):
+        for copy in self.copies(stage):
+            copy.wait()
+        self.buf[stage + 1] = self.buf[stage] + self.recv[stage]
+        self.start(stage + 1)
+
+    def finish(self):
+        for copy in self.copies(self.levels):
+            copy.wait()
+        mine = self.buf[self.levels]
+        total = 0.0
+        for member in range(self.groups):
+            step = (self.grp + self.groups - member) % self.groups
+            slot = jnp.where(step == 0, 0, self.levels + step - 1)
+            total = total + jnp.where(step == 0, mine, self.recv[slot])
+        return total
 
 
 def attend_kernel(
@@ -257,9 +385,8 @@
 
 
 def feed_kernel(
-    tok_ref, cot_ref, embed_ref, ot_ref, inv_ref, wo_ref, wi_ref, bi_ref, wb_ref, bb_ref,
-    g1_ref, s1_ref, g2_ref, s2_ref,
-    out_ref, dr1_ref, dot_ref, dd_ref, gout_ref, gin_ref, gback_ref, small_ref, gbi_ref,
+    tok_ref, cot_ref, embed_ref, ot_ref, inv_ref, wo_ref, wi_ref, wb_ref, vec_ref,
+    out_ref, dr1_ref, dot_ref, dd_ref, gin_ref, gbo_ref, small_ref,
     embed_rows, wot, wit, wbt, cols, bi_col, acc, acc_bi, n1_buf, y1_buf, slope, yl, df, da, hl, dh,
 ):
     eye = identity(256)
@@ -267,12 +394,14 @@
     wot[...] = transposed(eye, wo_ref[...])
     wit[...] = transposed(eye, wi_ref[...])
     wbt[...] = transposed(eye, wb_ref[...])
-    for index, ref in enumerate((bb_ref, g1_ref, s1_ref, g2_ref, s2_ref)):
-        cols[index] = column(eye, ref[...])
-    bi_col[...] = column(eye, bi_ref[...])
+    ff = wi_ref.shape[1]
+    width = wi_ref.shape[0]
+    for index in range(5):
+        at = ff + index * width
+        cols[index] = column(eye, vec_ref[:, at : at + width])
+    bi_col[...] = column(eye, vec_ref[:, 0:ff])
     acc[...] = jnp.zeros_like(acc)
     acc_bi[...] = jnp.zeros_like(acc_bi)
-    ff = wi_ref.shape[1]
     part = 512
 
     @pl.loop(0, WINDOWS)
@@ -353,122 +482,310 @@
                 jnp.sum(product[rows], axis=0, keepdims=True) * inverse
             )
 
+    count, back_rows, share = gin_ref.shape[0], ff // gin_ref.shape[0], gin_ref.shape[1]
+
     @pl.loop(0, ff // 256)
     def _(index):
         rows = pl.ds(pl.multiple_of(index * 256, 256), 256)
-        gback_ref[rows, :] = dot_nt(hl[rows, :], df[...])
-        gin_ref[:, rows] = dot_nt(yl[...], dh[rows, :])
-
-    gout_ref[...] = dot_nt(ot_ref[...], da[...])
+        back = dot_nt(hl[rows, :], df[...]).astype(BF16)
+        shares = 256 // back_rows
+        for part in range(shares):
+            gbo_ref[reversed_bits(index * shares + part, count), 0:back_rows, :] = back[
+                part * back_rows : part * back_rows + back_rows
+            ]
+        into = dot_nt(yl[...], dh[rows, :]).astype(BF16)
+        for owner in range(count):
+            gin_ref[reversed_bits(owner, count), :, rows] = into[owner * share : owner * share + share]
+
+    out = dot_nt(ot_ref[...], da[...]).astype(BF16)
+    for owner in range(count):
+        gbo_ref[reversed_bits(owner, count), back_rows:, :] = out[
+            owner * share : owner * share + share
+        ]
+    small_ref[...] = jnp.zeros_like(small_ref)
     for index in range(5):
         small_ref[index : index + 1, :] = lane_sums(acc[index])[0:1]
-    gbi_ref[...] = lane_sums(acc_bi[...])[0:1]
+    bias = lane_sums(acc_bi[...])[0:1]
+    for index in range(ff // width):
+        small_ref[5 + index : 6 + index, :] = bias[:, index * width : (index + 1) * width]
 
 
 def back_kernel(
-    has_ref, tok_ref, up_ref, embed_ref, wq_ref, wk_ref, wv_ref, xt_ref, xut_ref, qt_ref,
-    e_ref, dot_ref, dd_ref, dr1_ref,
-    dx_ref, dxu_ref, gq_ref, gk_ref, gv_ref,
-    embed_rows, wkt, vals, vals_up, kt, kt_up, dqt, dkt, dvt, dkt_up, dvt_up, e_buf, e_sem,
+    tok_ref, embed_ref, wq_ref, wk_ref, wv_ref, xt_ref, xut_ref, qt_ref, dot_ref, dd_ref, dr1_ref,
+    small_in, e_ref, gin_hbm, gbo_hbm,
+    gt_ref, qkv_ref, gin_ref, gbo_ref, small_ref,
+    wkt, vals, vals_up, kt, kt_up, dq_up, dqt, dkt, dvt, dkt_up, dvt_up, dk_acc, dv_acc,
+    dxu, below, e_buf, e_sem, load_sem,
+    gin_buf, gin_recv, gin_across, gbo_buf, gbo_recv, gbo_across, qkv_buf, qkv_recv, qkv_across,
+    small_buf, small_recv,
+    in_ss, in_rs, bo_ss, bo_rs, qkv_ss, qkv_rs, small_ss, small_rs, halo_ss, halo_rs,
+    *, size, groups,
 ):
+    band, grp = lax.axis_index("band"), lax.axis_index("grp")
+    depth = levels(size)
+    MESH = pl.DeviceIdType.MESH
+    barrier = pltpu.get_barrier_semaphore()
+    for level in range(depth):
+        bit = (band // (1 << level)) % 2
+        pl.semaphore_signal(
+            barrier, inc=1, device_id=(band + (1 << level) * (1 - 2 * bit), grp), device_id_type=MESH
+        )
+    for step in range(1, groups):
+        pl.semaphore_signal(
+            barrier, inc=1, device_id=(band, (grp + step) % groups), device_id_type=MESH
+        )
+
+    @pl.when((band % 2 == 1) & (band < size - 1))
+    def _():
+        pl.semaphore_signal(barrier, inc=1, device_id=(band + 1, grp), device_id_type=MESH)
+
+    load_in = pltpu.make_async_copy(gin_hbm, gin_buf, load_sem.at[0])
+    load_bo = pltpu.make_async_copy(gbo_hbm, gbo_buf, load_sem.at[1])
+    load_bo.start()
+    load_in.start()
+    above = jnp.where((band % 2 == 0) & (band > 0), 1, 0)
+    pl.semaphore_wait(barrier, depth + groups - 1 + above)
+
+    def reduction(buf, recv, across, ss, rs):
+        return Reduction(buf, recv, across, ss, rs, band, grp, size, groups)
+
+    sum_in = reduction(gin_buf, gin_recv, gin_across, lambda k: in_ss.at[k], lambda k: in_rs.at[k])
+    sum_bo = reduction(gbo_buf, gbo_recv, gbo_across, lambda k: bo_ss.at[k], lambda k: bo_rs.at[k])
+
+    def sum_qkv(pair):
+        return reduction(
+            qkv_buf.at[pair], qkv_recv.at[pair], qkv_across.at[pair],
+            lambda k: qkv_ss.at[pair, k], lambda k: qkv_rs.at[pair, k],
+        )
+
+    sum_small = SmallSum(
+        small_buf, small_recv, small_ss, small_rs, band, grp, size, groups
+    )
+    halo = pltpu.make_async_remote_copy(
+        src_ref=dxu, dst_ref=below, send_sem=halo_ss, recv_sem=halo_rs,
+        device_id=(jnp.maximum(band - 1, 0), grp), device_id_type=MESH,
+    )
+
+    def e_copy(step, slot, part):
+        pair, window = step // WINDOWS, step % WINDOWS
+        return pltpu.make_async_copy(
+            e_ref.at[window, pl.ds(2 * pair, 2), pl.ds(part * SPAN, SPAN)],
+            e_buf.at[slot],
+            e_sem.at[slot],
+        )
+
+    slots = e_buf.shape[0]
+    steps = 4 * WINDOWS
+    for step in range(slots - 1):
+        e_copy(step, step, 0).start()
+
     eye = identity(256)
-    fill_embed(embed_ref, embed_rows)
     wkt[...] = transposed(eye, wk_ref[...])
     clear_pads_rows(vals)
     clear_pads_rows(vals_up)
     clear_pads_lanes(kt)
     clear_pads_lanes(kt_up)
-    for ref in (dkt, dvt, dkt_up, dvt_up):
-        ref[...] = jnp.zeros_like(ref)
-    has_up = has_ref[0, 0].astype(F32)
-
-    def e_copy(window, slot):
-        return pltpu.make_async_copy(e_ref.at[window], e_buf.at[slot], e_sem.at[slot])
-
-    e_copy(0, 0).start()
+    load_bo.wait()
+    sum_bo.start(0)
 
     @pl.loop(0, WINDOWS)
     def _(window):
         here = pl.ds(pl.multiple_of(window * QUERIES, QUERIES), QUERIES)
         padded_at = pl.multiple_of(window * QUERIES + TILE, TILE)
-        low = start_window(tok_ref, embed_rows, window).astype(BF16)
+        low = transposed(eye, xt_ref[:, here])
         store_pairs(vals, padded_at, dot(low, wv_ref[...]).astype(BF16))
         kt[:, pl.ds(padded_at, QUERIES)] = dot(wkt[...], xt_ref[:, here]).astype(BF16)
-        upper = (start_window(up_ref, embed_rows, window) * has_up).astype(BF16)
+        upper = transposed(eye, xut_ref[:, here])
         store_pairs(vals_up, padded_at, dot(upper, wv_ref[...]).astype(BF16))
         kt_up[:, pl.ds(padded_at, QUERIES)] = dot(wkt[...], xut_ref[:, here]).astype(BF16)
 
+    load_in.wait()
+    sum_in.start(0)
+
+    def half_step(step, part, v_rows, k_cols):
+        pair, window = step // WINDOWS, step % WINDOWS
+        at = pl.multiple_of(window * QUERIES, QUERIES)
+        here, span = pl.ds(at, QUERIES), pl.ds(at, SPAN)
+        slot = step % slots
+        ahead = step + slots - 1
+
+        @pl.when(ahead < steps)
+        def _():
+            e_copy(ahead, ahead % slots, part).start()
+
+        @pl.when(window == 0)
+        def _():
+            dk_acc[...] = jnp.zeros_like(dk_acc)
+            dv_acc[...] = jnp.zeros_like(dv_acc)
+
+        e_copy(step, slot, part).wait()
+        feats = pl.ds(pl.multiple_of(pair * 128, 128), 128)
+        do_pair = dot_ref[feats, here]
+        values = v_rows[pair, span, :]
+        for half in range(2):
+            head = 2 * pair + half
+            mine = pl.ds(pl.multiple_of(pair * 128 + half * HEAD_DIM, HEAD_DIM), HEAD_DIM)
+            rows = pl.ds(half * HEAD_DIM, HEAD_DIM)
+            inner = dd_ref[pl.ds(head, 1), here]
+            e = e_buf[slot, half]
+            ds = (e.astype(F32) * (dot(values, head_of_pair(do_pair, half)) - inner)).astype(BF16)
+            dq = dot(k_cols[mine, span], ds)
+            if part == 0:
+                dq_up[mine, here] = dq
+            else:
+                dqt[mine, here] = ((dq + dq_up[mine, here]) * 0.125).astype(BF16)
+            dk_acc[rows, span] += dot_nt(qt_ref[mine, here], ds)
+            dv_acc[rows, span] += dot_nt(dot_ref[mine, here], e)
+
+    @pl.loop(0, steps)
+    def _(step):
+        half_step(step, 0, vals_up, kt_up)
+
+        @pl.when(step % WINDOWS == WINDOWS - 1)
+        def _():
+            feats = pl.ds(pl.multiple_of(step // WINDOWS * 128, 128), 128)
+            dkt_up[feats, :] = dk_acc[:, TILE : PADDED - TILE].astype(BF16)
+            dvt_up[feats, :] = dv_acc[:, TILE : PADDED - TILE].astype(BF16)
+
+        @pl.when(step == 1)
+        def _():
+            sum_bo.advance(0)
+            sum_in.advance(0)
+
+        @pl.when(step == 14)
+        def _():
+            sum_bo.advance(1)
+
+        @pl.when(step == 23)
+        def _():
+            sum_bo.advance(2)
+
+    for step in range(slots - 1):
+        e_copy(step, step, 1).start()
+
+    dxu[...] = (dot(wk_ref[...], dkt_up[...]) + dot(wv_ref[...], dvt_up[...])).astype(BF16)
+
+    @pl.when(band > 0)
+    def _():
+        halo.start()
+
+    @pl.loop(0, steps)
+    def _(step):
+        half_step(step, 1, vals, kt)
+        pair, window = step // WINDOWS, step % WINDOWS
+
+        for stage in range(depth):
+
+            @pl.when((pair > 0) & (window == stage + 5 - depth))
+            def _(stage=stage):
+                sum_qkv(pair - 1).advance(stage)
+
+        @pl.when((pair > 0) & (window == 5))
+        def _():
+            qkv_ref[pair - 1] = sum_qkv(pair - 1).finish()
+
+        @pl.when(window == WINDOWS - 1)
+        def _():
+            feats = pl.ds(pl.multiple_of(pair * 128, 128), 128)
+            dkt[feats, :] = dk_acc[:, TILE : PADDED - TILE].astype(BF16)
+            dvt[feats, :] = dv_acc[:, TILE : PADDED - TILE].astype(BF16)
+            xt, xut = xt_ref[...], xut_ref[...]
+            grads = (
+                dot_nt(xt, dqt[feats, :]),
+                dot_nt(xt, dkt[feats, :]) + dot_nt(xut, dkt_up[feats, :]),
+                dot_nt(xt, dvt[feats, :]) + dot_nt(xut, dvt_up[feats, :]),
+            )
+            share = qkv_buf.shape[2]
+            for index, grad in enumerate(grads):
+                low = grad.astype(BF16)
+                for owner in range(size):
+                    qkv_buf[pair, reversed_bits(owner, size), :, index * 128 : index * 128 + 128] = (
+                        low[owner * share : owner * share + share]
+                    )
+            sum_qkv(pair).start(0)
+
+        @pl.when(step == 2)
+        def _():
+            sum_in.advance(1)
+
+        @pl.when(step == 5)
+        def _():
+            sum_bo.advance(3)
+
+        @pl.when(step == 9)
+        def _():
+            sum_in.advance(2)
+
+        @pl.when(step == 10)
+        def _():
+            gbo_ref[...] = sum_bo.finish()
+
+        @pl.when(step == 15)
+        def _():
+            sum_in.advance(3)
+
+        @pl.when(step == 20)
+        def _():
+            gin_ref[...] = sum_in.finish()
+
+    shape = (16, LEN)
+    channel = (iota(shape, 1) // TILE + iota(shape, 1) % FLANK_COLS) % 3
+    chosen = jnp.where(channel + 9 == iota(shape, 0), 1.0, 0.0).astype(BF16)
+
+    def split(value):
+        high = value.astype(BF16)
+        return high, (value - high.astype(F32)).astype(BF16)
+
+    sums = jnp.zeros((16, dr1_ref.shape[0]), F32)
+    for piece in split(dr1_ref[...]):
+        sums += dot_nt(chosen, piece)
+    for grads, weight in ((dqt, wq_ref), (dkt, wk_ref), (dvt, wv_ref)):
+        for piece in split(dot_nt(chosen, grads[...])):
+            sums += dot_nt(piece, weight[...])
+    sums += dot_nt(chosen, dxu[...]) * jnp.where(band > 0, 1.0, 0.0)
+    small_buf[0] = small_in[...] + sums
+    sum_small.start(0)
+
+    @pl.when(band < size - 1)
+    def _():
+        halo.wait_recv()
+
+    @pl.when(band > 0)
+    def _():
+        halo.wait_send()
+
+    @pl.when(band == size - 1)
+    def _():
+        below[...] = jnp.zeros_like(below)
+
     @pl.loop(0, WINDOWS)
     def _(window):
-        at = pl.multiple_of(window * QUERIES, QUERIES)
-        here = pl.ds(at, QUERIES)
-        span = pl.ds(at, SPAN)
-        slot = lax.rem(window, 2)
-
-        @pl.when(window + 1 < WINDOWS)
-        def _():
-            e_copy(window + 1, 1 - slot).start()
-
-        e_copy(window, slot).wait()
-
-        @pl.loop(0, 4)
-        def _(pair):
-            feats = pl.ds(pl.multiple_of(pair * 128, 128), 128)
-            do_pair = dot_ref[feats, here]
-            v_low = vals[pair, span, :]
-            v_up = vals_up[pair, span, :]
-            for half in range(2):
-                head = 2 * pair + half
-                mine = pl.ds(pl.multiple_of(pair * 128 + half * HEAD_DIM, HEAD_DIM), HEAD_DIM)
-                do_head = head_of_pair(do_pair, half)
-                inner = dd_ref[pl.ds(head, 1), here]
-                e_up = e_buf[slot, head, 0:SPAN, :]
-                e_low = e_buf[slot, head, SPAN : 2 * SPAN, :]
-                ds_up = (e_up.astype(F32) * (dot(v_up, do_head) - inner)).astype(BF16)
-                ds_low = (e_low.astype(F32) * (dot(v_low, do_head) - inner)).astype(BF16)
-                dq = dot(kt_up[mine, span], ds_up) + dot(kt[mine, span], ds_low)
-                dqt[mine, here] = (dq * 0.125).astype(BF16)
-                q_head = qt_ref[mine, here]
-                do_mine = dot_ref[mine, here]
-                dkt[mine, span] += dot_nt(q_head, ds_low)
-                dkt_up[mine, span] += dot_nt(q_head, ds_up)
-                dvt[mine, span] += dot_nt(do_mine, e_low)
-                dvt_up[mine, span] += dot_nt(do_mine, e_up)
-
-    inner = slice(TILE, PADDED - TILE)
-    xt, xut = xt_ref[...], xut_ref[...]
-    gq_ref[...] = dot_nt(xt, dqt[...])
-    dk_low, dv_low = dkt[:, inner].astype(BF16), dvt[:, inner].astype(BF16)
-    dk_up, dv_up = dkt_up[:, inner].astype(BF16), dvt_up[:, inner].astype(BF16)
-    gk_ref[...] = dot_nt(xt, dk_low) + dot_nt(xut, dk_up)
-    gv_ref[...] = dot_nt(xt, dv_low) + dot_nt(xut, dv_up)
-    dxu_ref[...] = (dot(wk_ref[...], dk_up) + dot(wv_ref[...], dv_up)).astype(BF16)
-    dx_ref[...] = (
-        dr1_ref[...] + dot(wq_ref[...], dqt[...]) + dot(wk_ref[...], dk_low) + dot(wv_ref[...], dv_low)
-    )
-
-
-def finish_kernel(dx_ref, below_ref, gt_ref, ge_ref):
-    eye = identity(256)
-    sums = [0.0, 0.0, 0.0]
-    for window in range(WINDOWS):
-        here = slice(window * QUERIES, window * QUERIES + QUERIES)
-        dx = dx_ref[:, here] + below_ref[:, here].astype(F32)
-        for half in range(2):
-            kind = (2 * window + half) % 3
-            sums[kind] = sums[kind] + dx[:, half * TILE : half * TILE + TILE]
+        here = pl.ds(pl.multiple_of(window * QUERIES, QUERIES), QUERIES)
+        dx = (
+            dr1_ref[:, here]
+            + dot(wq_ref[...], dqt[:, here])
+            + dot(wk_ref[...], dkt[:, here])
+            + dot(wv_ref[...], dvt[:, here])
+            + below[:, here].astype(F32)
+        )
         rows = dot_nt(eye, dx.astype(BF16)).astype(BF16)
         for half in range(2):
-            at = (2 * window + half) * FLANK_COLS
-            gt_ref[:, at : at + FLANK_COLS, :] = rows[half * TILE : half * TILE + TILE].reshape(
+            at = pl.multiple_of((2 * window + half) * FLANK_COLS, FLANK_COLS)
+            gt_ref[:, pl.ds(at, FLANK_COLS), :] = rows[half * TILE : half * TILE + TILE].reshape(
                 BLOCK_ROWS, FLANK_COLS, -1
             )
-    lane = iota(sums[0].shape, 1) % FLANK_COLS
-    for channel in range(3):
-        total = 0.0
-        for kind in range(3):
-            total = total + jnp.where((lane + kind) % 3 == channel, sums[kind], 0.0)
-        ge_ref[channel : channel + 1, :] = lane_sums(total)[0:1]
+
+        for stage in range(depth):
+
+            @pl.when(window == stage + 5 - depth)
+            def _(stage=stage):
+                sum_qkv(3).advance(stage)
+                sum_small.advance(stage)
+
+        @pl.when(window == 5)
+        def _():
+            qkv_ref[3] = sum_qkv(3).finish()
+            small_ref[...] = sum_small.finish()
 
 
 def passed_along(value, axis, steps):
@@ -517,8 +834,12 @@
         ],
         compiler_params=params,
     )(row_place, row_width, has_up, tok, up, chan_embed, w_query, w_key, w_value)
-    row = lambda value: value.reshape(1, -1)
-    layer_out, dr1, do_t, dd, g_out, g_in, g_back, small, g_bias_in = pl.pallas_call(
+    size, groups = lax.axis_size("band"), lax.axis_size("grp")
+    share, back_share = width // size, ff // size
+    vectors = jnp.concatenate(
+        [bias_in, bias_back, gain_first, shift_first, gain_second, shift_second]
+    ).reshape(1, -1)
+    layer_out, dr1, do_t, dd, g_in, g_bo, small = pl.pallas_call(
         feed_kernel,
         name="feed_forward_and_back",
         out_shape=(
@@ -526,14 +847,12 @@
             shape((width, LEN), F32),
             shape((width, LEN), BF16),
             shape((8, LEN), F32),
-            shape((width, width), F32),
-            shape((width, ff), F32),
-            shape((ff, width), F32),
-            shape((5, width), F32),
-            shape((1, ff), F32),
+            shape((size, share, ff), BF16),
+            shape((size, back_share + share, width), BF16),
+            shape((16, width), F32),
         ),
-        in_specs=[vmem()] * 14,
-        out_specs=(vmem(),) * 9,
+        in_specs=[vmem()] * 9,
+        out_specs=(vmem(),) * 7,
         scratch_shapes=[
             pltpu.VMEM((ROW_POS, width), F32),
             pltpu.VMEM((width, width), BF16),
@@ -553,78 +872,90 @@
             pltpu.VMEM((ff, LEN), BF16),
         ],
         compiler_params=params,
-    )(
-        tok, cot, chan_embed, ot, inv, w_out, w_in, row(bias_in), w_back, row(bias_back),
-        row(gain_first), row(shift_first), row(gain_second), row(shift_second),
-    )
-    dx, dxu, g_query, g_key, g_value = pl.pallas_call(
-        back_kernel,
+    )(tok, cot, chan_embed, ot, inv, w_out, w_in, w_back, vectors)
+    dma = pltpu.SemaphoreType.DMA
+    stages = levels(size) + groups - 1
+    grad_tokens, g_qkv, g_in, g_bo, small = pl.pallas_call(
+        functools.partial(back_kernel, size=size, groups=groups),
         name="attend_backward",
         out_shape=(
-            shape((width, LEN), F32),
-            shape((width, LEN), BF16),
-            shape((width, width), F32),
-            shape((width, width), F32),
-            shape((width, width), F32),
+            shape((BLOCK_ROWS, ROW_POS, width), BF16),
+            shape((4, share, 384), F32),
+            shape((share, ff), F32),
+            shape((back_share + share, width), F32),
+            shape((16, width), F32),
         ),
-        in_specs=[smem()] + [vmem()] * 9 + [hbm()] + [vmem()] * 3,
+        in_specs=[vmem()] * 12 + [hbm()] * 3,
         out_specs=(vmem(),) * 5,
         scratch_shapes=[
-            pltpu.VMEM((ROW_POS, width), F32),
             pltpu.VMEM((width, width), BF16),
             pltpu.VMEM((4, PADDED, 128), BF16),
             pltpu.VMEM((4, PADDED, 128), BF16),
             pltpu.VMEM((width, PADDED), BF16),
             pltpu.VMEM((width, PADDED), BF16),
+            pltpu.VMEM((width, LEN), F32),
             pltpu.VMEM((width, LEN), BF16),
-            pltpu.VMEM((width, PADDED), F32),
-            pltpu.VMEM((width, PADDED), F32),
-            pltpu.VMEM((width, PADDED), F32),
-            pltpu.VMEM((width, PADDED), F32),
-            pltpu.VMEM((2, 8, 2 * SPAN, QUERIES), BF16),
-            pltpu.SemaphoreType.DMA((2,)),
+            pltpu.VMEM((width, LEN), BF16),
+            pltpu.VMEM((width, LEN), BF16),
+            pltpu.VMEM((width, LEN), BF16),
+            pltpu.VMEM((width, LEN), BF16),
+            pltpu.VMEM((128, PADDED), F32),
+            pltpu.VMEM((128, PADDED), F32),
+            pltpu.VMEM((width, LEN), BF16),
+            pltpu.VMEM((width, LEN), BF16),
+            pltpu.VMEM((4, 2, SPAN, QUERIES), BF16),
+            dma((4,)),
+            dma((2,)),
+            pltpu.VMEM((size, share, ff), BF16),
+            pltpu.VMEM((size, share, ff), BF16),
+            pltpu.VMEM((groups, share, ff), BF16),
+            pltpu.VMEM((size, back_share + share, width), BF16),
+            pltpu.VMEM((size, back_share + share, width), BF16),
+            pltpu.VMEM((groups, back_share + share, width), BF16),
+            pltpu.VMEM((4, size, share, 384), BF16),
+            pltpu.VMEM((4, size, share, 384), BF16),
+            pltpu.VMEM((4, groups, share, 384), BF16),
+            pltpu.VMEM((levels(size) + 1, 16, width), F32),
+            pltpu.VMEM((stages, 16, width), F32),
+            dma((stages,)),
+            dma((stages,)),
+            dma((stages,)),
+            dma((stages,)),
+            dma((4, stages)),
+            dma((4, stages)),
+            dma((stages,)),
+            dma((stages,)),
+            dma,
+            dma,
         ],
-        compiler_params=params,
-    )(has_up, tok, up, chan_embed, w_query, w_key, w_value, xt, xut, qt, e_all, do_t, dd, dr1)
-    below = passed_along(dxu, "band", -1)
-    grad_tokens, g_embed = pl.pallas_call(
-        finish_kernel,
-        name="finish",
-        out_shape=(shape((BLOCK_ROWS, ROW_POS, width), BF16), shape((3, width), F32)),
-        in_specs=[vmem()] * 2,
-        out_specs=(vmem(),) * 2,
-        compiler_params=params,
-    )(dx, below)
-
-    def shared(grad):
-        part = lax.psum_scatter(grad.astype(BF16), "band", scatter_dimension=0, tiled=True)
-        return lax.psum(part.astype(F32), "grp")
-
-    band_index = lax.axis_index("band")
-    band_size = lax.axis_size("band")
-
-    def share_of(full_sum, axis_dim):
-        size = full_sum.shape[axis_dim] // band_size
-        return lax.dynamic_slice_in_dim(full_sum, band_index * size, size, axis_dim)
-
-    small_sum, bias_in_sum, embed_sum = lax.psum((small, g_bias_in, g_embed), ("band", "grp"))
-    vector = lambda index: share_of(small_sum[index], 0)
+        compiler_params=pltpu.CompilerParams(
+            vmem_limit_bytes=LIMIT, collective_id=0, has_side_effects=True
+        ),
+    )(
+        tok, chan_embed, w_query, w_key, w_value, xt, xut, qt, do_t, dd, dr1, small, e_all, g_in, g_bo,
+    )
+    band = lax.axis_index("band")
+    qkv = g_qkv.reshape(4, share, 3, 128).transpose(2, 1, 0, 3).reshape(3, share, width)
+    mine = lax.dynamic_slice_in_dim(small, band * share, share, 1)
+    bias_in_sum = lax.dynamic_slice_in_dim(
+        small[5 : 5 + ff // width].reshape(ff), band * back_share, back_share, 0
+    )
     return (
         layer_out.reshape(tokens.shape),
         grad_tokens.reshape(tokens.shape),
-        shared(g_query),
-        shared(g_key),
-        shared(g_value),
-        shared(g_out),
-        shared(g_in),
-        share_of(bias_in_sum[0], 0),
-        shared(g_back),
-        vector(2),
-        vector(3),
-        vector(4),
-        vector(0),
-        vector(1),
-        share_of(embed_sum, 1),
+        qkv[0],
+        qkv[1],
+        qkv[2],
+        g_bo[back_share:],
+        g_in,
+        bias_in_sum,
+        g_bo[:back_share],
+        mine[2],
+        mine[3],
+        mine[4],
+        mine[0],
+        mine[1],
+        mine[9:12],
     )
 
 

time: 594 us -> 288 us (0.48)
  waiting for transfers between devices: 316 us -> 0.01 us
  Pallas kernels: 169 us -> 264 us
  blocking collectives: 62.3 us -> 0 us
  between operations: 15.5 us -> 2.01 us
  other arithmetic: 12.5 us -> 0 us
    reduce_scatter x6 -> x0, waiting for transfers between devices: 316 us -> none  [shared(): lax.psum_scatter(grad.astype(BF16), 'band', scatter_dimension=0, tiled=True)]
    pallas_call x2 -> x1, Pallas kernels: 58 us -> 154 us  [shards(): pl.pallas_call(functools.partial(back_kernel, size=size, groups=groups),...]
    psum x2 -> x0, blocking collectives: 62.3 us -> none  [the longest x1 40.7 us: shards(): lax.psum((small, g_bias_in, g_embed), ('band', 'grp'))]
    convert_element_type x6 -> x0, other arithmetic: 12.5 us -> none  [shared(): grad.astype(BF16)]
    reshape x6 -> x2, local copies, waits for them, and re-layouts: 7.57 us -> 1.62 us  [the longest x1 1 us: shards(): g_qkv.reshape(4, share, 3, 128).transpose(2, 1, 0, 3)]
  transfers between devices with their start and end apart: 8 -> 1, of which waited for: 6 -> 0; matrix products, arithmetic and copies ran while one was open for 4% -> 2% of each run, Pallas kernels for 1% -> 0%
where the time goes in v2:
time: 288 us; the launch traced here: 287 us
  Pallas kernels  264 us (92%)
  local copies, waits for them, and re-layouts  18.4 us (6%)
    pallas_call x1, Pallas kernels, shards(): pl.pallas_call(functools.partial(back_kernel, size=size, groups=groups),...  154 us
    pallas_call x1, Pallas kernels, shards(): pl.pallas_call(feed_kernel, name='feed_forward_and_back', out_shape=(shap...  60.1 us
    pallas_call x1, Pallas kernels, shards(): pl.pallas_call(attend_kernel, name='attend_forward', out_shape=(shape((wi...  49.6 us
    unnamed x16, local copies, waits for them, and re-layouts  8.52 us
  transfers between devices with their start and end apart: 1, of which 0 were waited for; matrix products, arithmetic and copies ran while one was open for 2% of the time, Pallas kernels for 0%

profile of v2, /device:TPU:0, one launch (start us, length us, event | category | flops | bytes accessed | tf_op | source)
XLA Modules:
  0.0 287.1 jit_solution(2223421505185151846)
XLA Ops:
  0.6 2.5 collective-permute-start
  4.4 0.7 constant_dynamic-update-slice_fusion.1
  5.1 0.9 dynamic-update-slice.1
  6.0 0.9 dynamic-update-slice.2
  6.8 0.9 dynamic-update-slice.3
  7.7 0.9 dynamic-update-slice.4
  8.5 0.7 constant_dynamic-update-slice_fusion
  9.2 0.6 reshape.67.vec_ref
  9.8 1.1 copy-done.1
  11.0 49.6 %attend_forward.1 = (bf16[512,1536]{1,0:T(8,128)(2,1)}, bf16[512,1536]{1,0:T(8,128)(2,1)}, bf16[512,1536]{1,0:T(8,128)(2,1)}, bf16[512,1536]{1,0:T(8,128)(2,1)},...) custom-call(s32[1,1]{1,0:T(1,128)S(6)} %copy.53.place_ref, s32[1,1]{1,0:T(1,128)S(6)} %copy.54.width_ref, ...), custom_call_target="tpu_custom_call" | custom-call | tf_op jit(solution)/shard_map/attend_forward/pallas_call | solution.py:809
  60.6 60.1 %feed_forward_and_back.1 = (bf16[8,192,512]{2,1,0:T(8,128)(2,1)}, f32[512,1536]{1,0:T(8,128)}, bf16[512,1536]{1,0:T(8,128)(2,1)}, f32[8,1536]{1,0:T(8,128)}, bf1...) custom-call(bf16[8,192,512]{2,1,0:T(8,128)(2,1)} %bitcast.34, ...), custom_call_target="tpu_custom_call" | custom-call | tf_op jit(solution)/shard_map/feed_forward_and_back/pallas_call | solution.py:842
  120.7 154.5 %attend_backward.1 = (bf16[8,192,512]{2,1,0:T(8,128)(2,1)}, f32[4,32,384]{2,1,0:T(8,128)}, f32[32,2048]{1,0:T(8,128)}, f32[160,512]{1,0:T(8,128)}, f32[16,512]{1,0:T(8,128)}) custom-call(bf16[8,192,512]{2,1,0:T(8,128)(2,1)} %bitcast.35, bf16[3,512]{1,0:T(4,128)(2,1)} %embed_ref.5, bf16[512,512]{1,0:T(8,128)(2,1)} %wq_ref.3, bf16[512,512]{1,0:T(8,128)(2,1)} %wk_ref.3, ...), custom_call_target="tpu_custom_call" | custom-call | tf_op jit(solution)/shard_map/attend_backward/pallas_call | solution.py:878
  275.2 1.6 slice.42
  276.8 1.7 slice.44
  278.5 1.0 reshape.70
  279.5 0.1 fusion
  279.7 0.6 copy.45
  280.4 0.8 slice_bitcast_fusion
  281.2 0.7 copy_bitcast_fusion
  281.8 0.6 dynamic_slice.6
  282.4 1.3 dynamic-slice.5
  283.8 1.5 dynamic-slice_bitcast_fusion
  285.2 1.1 copy.55
  286.4 0.7 copy.56
  (10 shorter events, 0.2 us)
Async XLA Ops:
  0.6 9.2 %collective-permute-start = (bf16[8,192,512]{2,1,0:T(8,128)(2,1)}, bf16[8,192,512]{2,1,0:T(8,128)(2,1)S(1)}, u32[]{:S(2)}, u32[]{:S(2)}) collective-permute-start(bf16[8,192,512]{2,1,0:T(8,128)(2,1)} %bitcast.32), channel_id=1, source_target_pairs={{0,2},{2,4},{4,6},{6,8},{8,10},{10,12},{12,14},{14,16},{16,18},{18... | collective-permute-start | bytes 4718600 | tf_op jit(solution)/shard_map/ppermute | solution.py:794
  9.8 1.1 copy-start.1
  275.2 10.0 %copy-start = (bf16[8,192,512]{2,1,0:T(8,128)(2,1)S(1)}, bf16[8,192,512]{2,1,0:T(8,128)(2,1)}, u32[]{:S(2)}) copy-start(bf16[8,192,512]{2,1,0:T(8,128)(2,1)} %get-tuple-element.46) | copy-start | bytes 4718596
  285.2 1.1 copy-start.2

commit v3 on v2

v3 whole, which is shorter than its diff:
```python
import functools

import jax
import jax.numpy as jnp
from jax import lax
from jax.experimental import pallas as pl
from jax.experimental.pallas import tpu as pltpu
from jax.sharding import PartitionSpec as P

HEAD_DIM = 64
ROW_POS = 192
BLOCK_ROWS = 8
BLOCK_COLS = 32
FLANK_COLS = 16
WINDOWS = ROW_POS // BLOCK_COLS
BLOCKS = ROW_POS // FLANK_COLS
TILE = BLOCK_ROWS * FLANK_COLS
QUERIES = 2 * TILE
SPAN = 4 * TILE
LEN = BLOCK_ROWS * ROW_POS
PADDED = LEN + 2 * TILE

norm_eps = 1e-06
big_negative = -1e30
F32 = jnp.float32
BF16 = jnp.bfloat16
LOG2_E = 1.4426950408889634
GELU_SCALE = 0.7978845608028654
GELU_CUBE = 0.044715


def dot(left, right):
    return jnp.dot(left, right, preferred_element_type=F32)


def dot_nt(left, right):
    return lax.dot_general(left, right, (((1,), (1,)), ((), ())), preferred_element_type=F32)


def iota(shape, dim):
    return lax.broadcasted_iota(jnp.int32, shape, dim)


def identity(size):
    return jnp.where(iota((size, size), 0) == iota((size, size), 1), 1.0, 0.0).astype(BF16)


def lanes(start, size):
    return pl.ds(pl.multiple_of(start, 128), size)


def transposed(eye, value):
    step = eye.shape[0]
    parts = [
        dot_nt(eye, value[:, at : at + step]).astype(BF16) for at in range(0, value.shape[1], step)
    ]
    return jnp.concatenate(parts, axis=0)


def column(eye, row):
    step = eye.shape[0]
    ones = jnp.ones((128, step), BF16)
    parts = [
        dot_nt(jnp.where(eye > 0, row[:, at : at + step], 0).astype(BF16), ones)
        for at in range(0, row.shape[1], step)
    ]
    return jnp.concatenate(parts, axis=0)


def wide(value):
    return jnp.concatenate([value, value], axis=1)


def halves(value):
    return value[:, :128] + value[:, 128:]


def lane_sums(value):
    ones = jnp.ones((8, 128), BF16)
    high = value.astype(BF16)
    rest = value - high.astype(F32)
    middle = rest.astype(BF16)
    low = (rest - middle.astype(F32)).astype(BF16)
    return dot_nt(ones, high) + dot_nt(ones, middle) + dot_nt(ones, low)


def fill_embed(embed_ref, rows_ref):
    embed = embed_ref[...].astype(F32)
    channel = lax.rem(iota(rows_ref.shape, 0), 3)
    rows_ref[...] = jnp.where(
        channel == 0, embed[0:1], jnp.where(channel == 1, embed[1:2], embed[2:3])
    )


def block_rows(rows_ref, block):
    return rows_ref[:, pl.ds(pl.multiple_of(block * FLANK_COLS, FLANK_COLS), FLANK_COLS), :]


def raw_window(rows_ref, window):
    parts = [block_rows(rows_ref, 2 * window + half).reshape(TILE, -1) for half in range(2)]
    return jnp.concatenate(parts, axis=0)


def embed_window(embed_rows, window):
    parts = []
    for half in range(2):
        at = pl.multiple_of((2 * window + half) * FLANK_COLS, FLANK_COLS)
        part = embed_rows[pl.ds(at, FLANK_COLS), :][None]
        parts.append(jnp.broadcast_to(part, (BLOCK_ROWS,) + part.shape[1:]).reshape(TILE, -1))
    return jnp.concatenate(parts, axis=0)


def start_window(rows_ref, embed_rows, window):
    return raw_window(rows_ref, window).astype(F32) + embed_window(embed_rows, window)


def norm_stats(value):
    center = value - jnp.mean(value, axis=0, keepdims=True)
    spread = jnp.mean(center * center, axis=0, keepdims=True)
    inverse = lax.rsqrt(spread + norm_eps)
    return center * inverse, inverse


def norm_back(normed, inverse, grad, gain):
    scaled = grad * gain
    first = jnp.mean(scaled, axis=0, keepdims=True)
    second = jnp.mean(scaled * normed, axis=0, keepdims=True)
    return (scaled - first - normed * second) * inverse


def vmem():
    return pl.BlockSpec(memory_space=pltpu.VMEM)


def smem():
    return pl.BlockSpec(memory_space=pltpu.SMEM)


def hbm():
    return pl.BlockSpec(memory_space=pl.ANY)


LIMIT = 60 * 1024 * 1024


def head_of_pair(value, half):
    keep = (iota(value.shape, 0) // HEAD_DIM) == half
    return jnp.where(keep, value, jnp.zeros_like(value))


def store_pairs(ref, at, value):
    for pair in range(value.shape[1] // 128):
        ref[pair, pl.ds(at, value.shape[0]), :] = value[:, pair * 128 : (pair + 1) * 128]


def clear_pads_rows(ref):
    pad = jnp.zeros((ref.shape[0], TILE, ref.shape[2]), ref.dtype)
    ref[:, 0:TILE, :] = pad
    ref[:, PADDED - TILE : PADDED, :] = pad


def clear_pads_lanes(ref):
    pad = jnp.zeros((ref.shape[0], TILE), ref.dtype)
    ref[:, 0:TILE] = pad
    ref[:, PADDED - TILE : PADDED] = pad


def reversed_bits(index, count):
    place, bit = 0, 1
    while bit < count:
        place = place + (index // bit) % 2 * (count // (2 * bit))
        bit *= 2
    return place


def levels(count):
    return count.bit_length() - 1


class Reduction:
    def __init__(self, buf, recv, across, gathered, send_sem, recv_sem, band, grp, size, groups):
        self.buf, self.recv, self.across, self.gathered = buf, recv, across, gathered
        self.send_sem, self.recv_sem = send_sem, recv_sem
        self.band, self.grp, self.size, self.groups = band, grp, size, groups
        depth = levels(size)
        bits = [("bit", level) for level in range(depth)]
        if gathered is None:
            self.stages = bits + [("sum", depth)]
        else:
            self.stages = bits[:1] + [("split", 1)] + bits[1:] + [("gather", depth)]
        self.depth = depth
        self.part = buf.shape[2] // groups

    def start_of(self, bits):
        start = 0
        for level in range(bits):
            start = start + (self.band // (1 << level)) % 2 * (self.size >> (level + 1))
        return start

    def columns_of(self, member):
        return pl.ds(pl.multiple_of(member * self.part, 128), self.part)

    def columns(self, stage):
        split = [kind for kind, _ in self.stages[:stage]].count("split")
        return self.columns_of(self.grp) if split else slice(None)

    def view(self, ref, first, count, columns):
        rows = pl.ds(first, count)
        return ref.at[rows] if columns == slice(None) else ref.at[rows, :, columns]

    def copies(self, stage):
        kind, bits = self.stages[stage]
        columns = self.columns(stage)
        pieces = []
        if kind == "bit":
            half = self.size >> (bits + 1)
            bit = (self.band // (1 << bits)) % 2
            pieces.append(
                (
                    self.view(self.buf, self.start_of(bits) + (1 - bit) * half, half, columns),
                    self.view(self.recv, half, half, columns),
                    bits,
                    (self.band + (1 << bits) * (1 - 2 * bit), self.grp),
                )
            )
        for step in range(1, self.groups):
            partner = (self.grp + step) % self.groups
            place = (self.band, partner)
            if kind == "sum":
                source, target = self.buf.at[self.start_of(bits)], self.across.at[step]
                pieces.append((source, target, self.depth + step - 1, place))
            if kind == "split":
                source = self.view(
                    self.buf, self.start_of(bits), self.size >> bits, self.columns_of(partner)
                )
                pieces.append((source, self.across.at[step - 1], self.depth + step - 1, place))
            if kind == "gather":
                source, target = self.gathered.at[0], self.gathered.at[step]
                pieces.append((source, target, self.depth + self.groups + step - 2, place))
        return [
            pltpu.make_async_remote_copy(
                src_ref=source,
                dst_ref=target,
                send_sem=self.send_sem(sem),
                recv_sem=self.recv_sem(sem),
                device_id=place,
                device_id_type=pl.DeviceIdType.MESH,
            )
            for source, target, sem, place in pieces
        ]

    def start(self, stage):
        for copy in self.copies(stage):
            copy.start()

    def advance(self, stage):
        for copy in self.copies(stage):
            copy.wait()
        kind, bits = self.stages[stage]
        if kind == "bit":
            columns = self.columns(stage)
            half, keep = self.size >> (bits + 1), self.start_of(bits + 1)

            @pl.loop(0, half)
            def _(index):
                total = self.buf[keep + index, :, columns].astype(F32)
                total = total + self.recv[half + index, :, columns].astype(F32)
                self.buf[keep + index, :, columns] = total.astype(BF16)
        else:
            columns = self.columns_of(self.grp)
            keep = self.start_of(bits)

            @pl.loop(0, self.size >> bits)
            def _(index):
                total = self.buf[keep + index, :, columns].astype(F32)
                for step in range(self.groups - 1):
                    total = total + self.across[step, index].astype(F32)
                self.buf[keep + index, :, columns] = total.astype(BF16)

        if self.stages[stage + 1][0] == "gather":
            self.gathered[0] = self.buf[self.start_of(self.depth), :, self.columns_of(self.grp)].astype(
                F32
            )
        self.start(stage + 1)

    def finish(self, out):
        last = len(self.stages) - 1
        for copy in self.copies(last):
            copy.wait()
        if self.stages[last][0] == "sum":
            self.across[0] = self.buf[self.start_of(self.depth)]
            total = 0.0
            for member in range(self.groups):
                step = (self.grp + self.groups - member) % self.groups
                total = total + self.across[step].astype(F32)
            out(total)
        else:
            for step in range(self.groups):
                member = (self.grp + self.groups - step) % self.groups
                out(self.gathered[step], self.columns_of(member))


class SmallSum:
    def __init__(self, buf, recv, send_sem, recv_sem, band, grp, size, groups):
        self.buf, self.recv, self.send_sem, self.recv_sem = buf, recv, send_sem, recv_sem
        self.band, self.grp, self.size, self.groups = band, grp, size, groups
        self.levels = levels(size)

    def copies(self, stage):
        if stage < self.levels:
            bit = (self.band // (1 << stage)) % 2
            partners = [(stage, (self.band + (1 << stage) * (1 - 2 * bit), self.grp))]
        else:
            partners = [
                (self.levels + step - 1, (self.band, (self.grp + step) % self.groups))
                for step in range(1, self.groups)
            ]
        return [
            pltpu.make_async_remote_copy(
                src_ref=self.buf.at[stage],
                dst_ref=self.recv.at[slot],
                send_sem=self.send_sem.at[slot],
                recv_sem=self.recv_sem.at[slot],
                device_id=partner,
                device_id_type=pl.DeviceIdType.MESH,
            )
            for slot, partner in partners
        ]

    def start(self, stage):
        for copy in self.copies(stage):
            copy.start()

    def advance(self, stage):
        for copy in self.copies(stage):
            copy.wait()
        self.buf[stage + 1] = self.buf[stage] + self.recv[stage]
        self.start(stage + 1)

    def finish(self):
        for copy in self.copies(self.levels):
            copy.wait()
        mine = self.buf[self.levels]
        total = 0.0
        for member in range(self.groups):
            step = (self.grp + self.groups - member) % self.groups
            slot = jnp.where(step == 0, 0, self.levels + step - 1)
            total = total + jnp.where(step == 0, mine, self.recv[slot])
        return total


def attend_kernel(
    place_ref, width_ref, tok_ref, embed_ref, wq_ref, wk_ref, wv_ref,
    xt_ref, xut_ref, qt_ref, ot_ref, inv_ref, e_ref,
    embed_rows, up, wqt, wvt, qs, keys, keys_up, vt, vt_up, bias_low, bias_up, ones_row,
    e_buf, e_sem, up_ss, up_rs,
    *, size,
):
    band, grp = lax.axis_index("band"), lax.axis_index("grp")
    barrier = pltpu.get_barrier_semaphore()

    @pl.when(band > 0)
    def _():
        pl.semaphore_signal(
            barrier, inc=1, device_id=(band - 1, grp), device_id_type=pl.DeviceIdType.MESH
        )

    def up_copy(window):
        cols = pl.ds(pl.multiple_of(window * BLOCK_COLS, BLOCK_COLS), BLOCK_COLS)
        return pltpu.make_async_remote_copy(
            src_ref=tok_ref.at[:, cols, :],
            dst_ref=up.at[:, cols, :],
            send_sem=up_ss.at[window],
            recv_sem=up_rs.at[window],
            device_id=(jnp.minimum(band + 1, size - 1), grp),
            device_id_type=pl.DeviceIdType.MESH,
        )

    @pl.when(band < size - 1)
    def _():
        pl.semaphore_wait(barrier, 1)
        for window in range(WINDOWS):
            up_copy(window).start()

    @pl.when(band == 0)
    def _():
        up[...] = jnp.zeros_like(up)

    eye = identity(256)
    fill_embed(embed_ref, embed_rows)
    wqt[...] = transposed(eye, wq_ref[...])
    wvt[...] = transposed(eye, wv_ref[...])
    clear_pads_rows(keys)
    clear_pads_rows(keys_up)
    vt[...] = jnp.zeros_like(vt)
    vt_up[...] = jnp.zeros_like(vt_up)
    sums = jnp.where(iota((16, PADDED), 0) == 0, 1.0, 0.0).astype(BF16)
    for head in range(8):
        vt[head, HEAD_DIM:, :] = sums
        vt_up[head, HEAD_DIM:, :] = sums
    ones_row[...] = jnp.where(iota(ones_row.shape, 0) == 0, 1.0, 0.0).astype(BF16)
    has_up = jnp.where(band > 0, 1.0, 0.0)
    def store_heads(ref, at, value):
        for head in range(8):
            ref[head, 0:HEAD_DIM, pl.ds(at, QUERIES)] = value[
                head * HEAD_DIM : head * HEAD_DIM + HEAD_DIM
            ]

    @pl.loop(0, WINDOWS)
    def _(window):
        at = pl.multiple_of(window * QUERIES, QUERIES)
        padded_at = pl.multiple_of(window * QUERIES + TILE, TILE)
        low = start_window(tok_ref, embed_rows, window).astype(BF16)
        low_t = transposed(eye, low)
        xt_ref[:, pl.ds(at, QUERIES)] = low_t
        q_low = dot(wqt[...], low_t).astype(BF16)
        qt_ref[:, pl.ds(at, QUERIES)] = q_low * BF16(0.125)
        qs[:, pl.ds(at, QUERIES)] = (q_low.astype(F32) * (0.125 * LOG2_E)).astype(BF16)
        store_pairs(keys, padded_at, dot(low, wk_ref[...]).astype(BF16))
        store_heads(vt, padded_at, dot(wvt[...], low_t).astype(BF16))

    def prepare_upper(window):
        @pl.when(band > 0)
        def _():
            up_copy(window).wait_recv()

        at = pl.multiple_of(window * QUERIES, QUERIES)
        padded_at = pl.multiple_of(window * QUERIES + TILE, TILE)
        upper = (start_window(up, embed_rows, window) * has_up).astype(BF16)
        upper_t = transposed(eye, upper)
        xut_ref[:, pl.ds(at, QUERIES)] = upper_t
        store_pairs(keys_up, padded_at, dot(upper, wk_ref[...]).astype(BF16))
        store_heads(vt_up, padded_at, dot(wvt[...], upper_t).astype(BF16))

    place = place_ref[0, 0]
    width = width_ref[0, 0]
    shape = (SPAN, QUERIES)
    memory, query = iota(shape, 0), iota(shape, 1)
    memory_col = (memory // TILE) * FLANK_COLS + memory % FLANK_COLS - FLANK_COLS
    query_col = (query // TILE) * FLANK_COLS + query % FLANK_COLS
    memory_row = (memory % TILE) // FLANK_COLS
    query_row = (query % TILE) // FLANK_COLS

    def prepare_masks(window):
        column_at = memory_col + window * BLOCK_COLS
        inside = (column_at >= 0) & (column_at < width)
        earlier = (memory_row < query_row) | ((memory_row == query_row) & (memory_col <= query_col))
        itself = (memory_row == query_row) & (memory_col == query_col)
        bias_low[...] = jnp.where((inside & earlier) | itself, 0.0, big_negative)
        first = iota(bias_up.shape, 1) == 0
        closed = jnp.where(inside[:, 0:128] & (place > 0), 0.0, big_negative)
        bias_up[...] = jnp.where(first, closed, 0.0).astype(BF16)

    def e_copy(window):
        slot = window % 2
        return pltpu.make_async_copy(e_buf.at[slot], e_ref.at[window], e_sem.at[slot])

    prepare_upper(0)

    @pl.loop(0, WINDOWS)
    def _(window):
        @pl.when(window < WINDOWS - 1)
        def _():
            prepare_upper(window + 1)

        prepare_masks(window)

        @pl.when(window > 1)
        def _():
            e_copy(window - 2).wait()

        slot = window % 2
        at = pl.multiple_of(window * QUERIES, QUERIES)
        here, span = pl.ds(at, QUERIES), pl.ds(at, SPAN)

        def scores(head):
            pair = head // 2
            q_head = head_of_pair(qs[pair * 128 : pair * 128 + 128, here], head % 2)
            upper = dot(
                jnp.concatenate([keys_up[pair, span, :], bias_up[...]], axis=1),
                jnp.concatenate([q_head, ones_row[...]], axis=0),
            )
            lower = dot(keys[pair, span, :], q_head) + bias_low[...]
            shape = (SPAN // 8, 8, QUERIES)
            top = jnp.maximum(
                jnp.max(upper.reshape(shape), axis=0), jnp.max(lower.reshape(shape), axis=0)
            )
            return upper, lower, jnp.max(top, axis=0, keepdims=True)

        def mix(head, e_up, e_low):
            mixed = dot(vt_up[head, :, span], e_up) + dot(vt[head, :, span], e_low)
            inverse = 1.0 / mixed[HEAD_DIM : HEAD_DIM + 1]
            rows = slice(head * HEAD_DIM, head * HEAD_DIM + HEAD_DIM)
            ot_ref[rows, here] = (mixed[0:HEAD_DIM] * inverse).astype(BF16)
            inv_ref[head : head + 1, here] = inverse

        current, raised = scores(0), None
        for head in range(8):
            upcoming = scores(head + 1) if head < 7 else None
            upper, lower, peak = current
            e_up = jnp.exp2(upper - peak).astype(BF16)
            e_low = jnp.exp2(lower - peak).astype(BF16)
            e_buf[slot, head, 0:SPAN, :] = e_up
            e_buf[slot, head, SPAN : 2 * SPAN, :] = e_low
            if head > 0:
                mix(head - 1, *raised)
            raised = (e_up, e_low)
            current = upcoming
        mix(7, *raised)
        e_copy(window).start()

    for window in range(WINDOWS - 2, WINDOWS):
        e_copy(window).wait()

    @pl.when(band < size - 1)
    def _():
        for window in range(WINDOWS):
            up_copy(window).wait_send()


def feed_kernel(
    tok_ref, cot_ref, embed_ref, ot_ref, inv_ref, wo_ref, wi_ref, wb_ref, vec_ref,
    out_ref, dr1_ref, dot_ref, dd_ref, gin_ref, gbo_ref, small_ref,
    embed_rows, wot, wit, wbt, cols, bi_col, acc, acc_bi, n1_buf, y1_buf, slope, yl, df, da, hl, dh,
):
    eye = identity(256)
    fill_embed(embed_ref, embed_rows)
    wot[...] = transposed(eye, wo_ref[...])
    wit[...] = transposed(eye, wi_ref[...])
    wbt[...] = transposed(eye, wb_ref[...])
    ff = wi_ref.shape[1]
    width = wi_ref.shape[0]
    for index in range(5):
        at = ff + index * width
        cols[index] = column(eye, vec_ref[:, at : at + width])
    bi_col[...] = column(eye, vec_ref[:, 0:ff])
    acc[...] = jnp.zeros_like(acc)
    acc_bi[...] = jnp.zeros_like(acc_bi)
    part = 256

    @pl.loop(0, WINDOWS)
    def _(window):
        here = pl.ds(pl.multiple_of(window * QUERIES, QUERIES), QUERIES)
        raw = raw_window(tok_ref, window)
        embed = embed_window(embed_rows, window).astype(BF16)
        start = jnp.concatenate(
            [
                dot_nt(eye, raw[:, half * 256 : half * 256 + 256])
                + dot_nt(eye, embed[:, half * 256 : half * 256 + 256])
                for half in range(2)
            ],
            axis=0,
        )
        n1, inv1 = norm_stats(start + dot(wot[...], ot_ref[:, here]))
        y1 = n1 * wide(cols[1]) + wide(cols[2])
        low = y1.astype(BF16)
        n1_buf[...] = n1
        y1_buf[...] = y1
        yl[:, here] = low

        for index in range(ff // part):
            rows = pl.ds(index * part, part)
            u = dot(wit[rows, :], low) + wide(bi_col[rows, :])
            square = u * u
            t = jnp.tanh(GELU_SCALE * u * (1.0 + GELU_CUBE * square))
            half_up = 0.5 * (1.0 + t)
            hl[rows, here] = (u * half_up).astype(BF16)
            slope[rows, :] = half_up + (0.5 * GELU_SCALE) * u * (1.0 - t * t) * (
                1.0 + 3.0 * GELU_CUBE * square
            )

        f = dot(wbt[...], hl[:, here]) + wide(cols[0])
        n2, inv2 = norm_stats(y1_buf[...] + f)
        g2 = wide(cols[3])
        result = (n2 * g2 + wide(cols[4])).astype(BF16)
        result = dot_nt(eye, result).astype(BF16)
        for half in range(2):
            at = pl.multiple_of((2 * window + half) * FLANK_COLS, FLANK_COLS)
            out_ref[:, pl.ds(at, FLANK_COLS), :] = result[half * TILE : half * TILE + TILE].reshape(
                BLOCK_ROWS, FLANK_COLS, -1
            )
        raw_cot = raw_window(cot_ref, window)
        cot = jnp.concatenate(
            [dot_nt(eye, raw_cot[:, half * 256 : half * 256 + 256]) for half in range(2)], axis=0
        )
        acc[0] += halves(cot * n2)
        acc[1] += halves(cot)
        dr2 = norm_back(n2, inv2, cot, g2)
        df_low = dr2.astype(BF16)
        acc[2] += halves(df_low.astype(F32))
        df[:, here] = df_low

        for index in range(ff // part):
            rows = pl.ds(index * part, part)
            dh_low = (dot(wb_ref[rows, :], df_low) * slope[rows, :]).astype(BF16)
            dh[rows, here] = dh_low
            acc_bi[rows, :] += halves(dh_low.astype(F32))

        dy1 = dr2 + dot(wi_ref[...], dh[:, here])
        n1 = n1_buf[...]
        acc[3] += halves(dy1 * n1)
        acc[4] += halves(dy1)
        dr1 = norm_back(n1, inv1, dy1, wide(cols[1]))
        dr1_ref[:, here] = dr1
        da_low = dr1.astype(BF16)
        da[:, here] = da_low
        d_o = dot(wo_ref[...], da_low)
        product = d_o * ot_ref[:, here].astype(F32)
        for head in range(8):
            rows = slice(head * HEAD_DIM, head * HEAD_DIM + HEAD_DIM)
            inverse = inv_ref[head : head + 1, here]
            dot_ref[rows, here] = (d_o[rows] * inverse).astype(BF16)
            dd_ref[head : head + 1, here] = (
                jnp.sum(product[rows], axis=0, keepdims=True) * inverse
            )

    count, back_rows, share = gin_ref.shape[0], ff // gin_ref.shape[0], gin_ref.shape[1]

    @pl.loop(0, ff // 256)
    def _(index):
        rows = pl.ds(pl.multiple_of(index * 256, 256), 256)
        back = dot_nt(hl[rows, :], df[...]).astype(BF16)
        shares = 256 // back_rows
        for part in range(shares):
            gbo_ref[reversed_bits(index * shares + part, count), 0:back_rows, :] = back[
                part * back_rows : part * back_rows + back_rows
            ]
        into = dot_nt(yl[...], dh[rows, :]).astype(BF16)
        for owner in range(count):
            gin_ref[reversed_bits(owner, count), :, rows] = into[owner * share : owner * share + share]

    out = dot_nt(ot_ref[...], da[...]).astype(BF16)
    for owner in range(count):
        gbo_ref[reversed_bits(owner, count), back_rows:, :] = out[
            owner * share : owner * share + share
        ]
    small_ref[...] = jnp.zeros_like(small_ref)
    for index in range(5):
        small_ref[index : index + 1, :] = lane_sums(acc[index])[0:1]
    bias = lane_sums(acc_bi[...])[0:1]
    for index in range(ff // width):
        small_ref[5 + index : 6 + index, :] = bias[:, index * width : (index + 1) * width]


def back_kernel(
    wq_ref, wk_ref, wv_ref, xt_ref, xut_ref, qt_ref, dot_ref, dd_ref, dr1_ref,
    small_in, e_ref, gin_hbm, gbo_hbm,
    gt_ref, qkv_ref, gin_ref, gbo_ref, small_ref,
    wkt, w3, w2, vals, vals_up, kt, kt_up, dq_up, d3, d2, dk_acc, dv_acc,
    dxu, below, e_buf, e_sem, load_sem,
    gin_buf, gin_recv, gin_across, gin_parts, gbo_buf, gbo_recv, gbo_across,
    qkv_buf, qkv_recv, qkv_across, small_buf, small_recv,
    in_ss, in_rs, bo_ss, bo_rs, qkv_ss, qkv_rs, small_ss, small_rs, halo_ss, halo_rs,
    *, size, groups,
):
    band, grp = lax.axis_index("band"), lax.axis_index("grp")
    depth = levels(size)
    MESH = pl.DeviceIdType.MESH
    barrier = pltpu.get_barrier_semaphore()
    for level in range(depth):
        bit = (band // (1 << level)) % 2
        pl.semaphore_signal(
            barrier, inc=1, device_id=(band + (1 << level) * (1 - 2 * bit), grp), device_id_type=MESH
        )
    for step in range(1, groups):
        pl.semaphore_signal(
            barrier, inc=1, device_id=(band, (grp + step) % groups), device_id_type=MESH
        )

    @pl.when((band % 2 == 1) & (band < size - 1))
    def _():
        pl.semaphore_signal(barrier, inc=1, device_id=(band + 1, grp), device_id_type=MESH)

    load_in = pltpu.make_async_copy(gin_hbm, gin_buf, load_sem.at[0])
    load_bo = pltpu.make_async_copy(gbo_hbm, gbo_buf, load_sem.at[1])
    load_bo.start()
    load_in.start()

    def e_copies(pair, part):
        return [
            pltpu.make_async_copy(
                e_ref.at[window, pl.ds(2 * pair, 2), pl.ds(part * SPAN, SPAN)],
                e_buf.at[pair % 2, window],
                e_sem.at[pair % 2, window],
            )
            for window in range(WINDOWS)
        ]

    for copy in e_copies(0, 0):
        copy.start()
    above = jnp.where((band % 2 == 0) & (band > 0), 1, 0)
    pl.semaphore_wait(barrier, depth + groups - 1 + above)

    sum_in = Reduction(
        gin_buf, gin_recv, gin_across, gin_parts,
        lambda k: in_ss.at[k], lambda k: in_rs.at[k], band, grp, size, groups,
    )
    sum_bo = Reduction(
        gbo_buf, gbo_recv, gbo_across, None,
        lambda k: bo_ss.at[k], lambda k: bo_rs.at[k], band, grp, size, groups,
    )

    def sum_qkv(pair):
        return Reduction(
            qkv_buf.at[pair], qkv_recv.at[pair], qkv_across.at[pair], None,
            lambda k: qkv_ss.at[pair, k], lambda k: qkv_rs.at[pair, k], band, grp, size, groups,
        )

    sum_small = SmallSum(small_buf, small_recv, small_ss, small_rs, band, grp, size, groups)

    def halo(window):
        here = pl.ds(pl.multiple_of(window * QUERIES, QUERIES), QUERIES)
        return pltpu.make_async_remote_copy(
            src_ref=dxu.at[:, here], dst_ref=below.at[:, here],
            send_sem=halo_ss.at[window], recv_sem=halo_rs.at[window],
            device_id=(jnp.maximum(band - 1, 0), grp), device_id_type=MESH,
        )

    def write_in(value, columns):
        gin_ref[:, columns] = value

    def write_bo(value):
        gbo_ref[...] = value

    def write_qkv(pair):
        def write(value):
            qkv_ref[pair] = value

        return write

    eye = identity(256)
    wkt[...] = transposed(eye, wk_ref[...])
    for pair in range(4):
        cols = slice(pair * 128, pair * 128 + 128)
        for index, ref in enumerate((wq_ref, wk_ref, wv_ref)):
            w3[:, pair * 384 + index * 128 : pair * 384 + index * 128 + 128] = ref[:, cols]
        for index, ref in enumerate((wk_ref, wv_ref)):
            w2[:, pair * 256 + index * 128 : pair * 256 + index * 128 + 128] = ref[:, cols]
    clear_pads_rows(vals)
    clear_pads_rows(vals_up)
    clear_pads_lanes(kt)
    clear_pads_lanes(kt_up)
    load_bo.wait()
    sum_bo.start(0)
    load_in.wait()
    sum_in.start(0)

    @pl.loop(0, WINDOWS)
    def _(window):
        here = pl.ds(pl.multiple_of(window * QUERIES, QUERIES), QUERIES)
        padded_at = pl.multiple_of(window * QUERIES + TILE, TILE)
        low = transposed(eye, xt_ref[:, here])
        upper = transposed(eye, xut_ref[:, here])
        store_pairs(vals, padded_at, dot(low, wv_ref[...]).astype(BF16))
        kt[:, pl.ds(padded_at, QUERIES)] = dot(wkt[...], xt_ref[:, here]).astype(BF16)
        store_pairs(vals_up, padded_at, dot(upper, wv_ref[...]).astype(BF16))
        kt_up[:, pl.ds(padded_at, QUERIES)] = dot(wkt[...], xut_ref[:, here]).astype(BF16)

    sum_bo.advance(0)
    sum_in.advance(0)

    def pass_over(pair, part, v_rows, k_cols):
        for copy in e_copies(pair, part):
            copy.wait()
        dk_acc[...] = jnp.zeros_like(dk_acc)
        dv_acc[...] = jnp.zeros_like(dv_acc)
        feats = pl.ds(pl.multiple_of(pair * 128, 128), 128)
        items = [(window, half) for window in range(WINDOWS) for half in range(2)]

        def limits(window):
            first = TILE if window == 0 else 0
            last = SPAN - TILE if window == WINDOWS - 1 else SPAN
            return first, last

        def grad_probs(window, half):
            first, last = limits(window)
            here = slice(window * QUERIES, window * QUERIES + QUERIES)
            rows = slice(window * QUERIES + first, window * QUERIES + last)
            return dot(v_rows[pair, rows, :], head_of_pair(dot_ref[feats, here], half))

        upcoming = grad_probs(*items[0])
        for index, (window, half) in enumerate(items):
            current = upcoming
            if index + 1 < len(items):
                upcoming = grad_probs(*items[index + 1])
            first, last = limits(window)
            here = slice(window * QUERIES, window * QUERIES + QUERIES)
            span = slice(window * QUERIES + first, window * QUERIES + last)
            mine = pl.ds(pl.multiple_of(pair * 128 + half * HEAD_DIM, HEAD_DIM), HEAD_DIM)
            rows = slice(half * HEAD_DIM, half * HEAD_DIM + HEAD_DIM)
            e = e_buf[pair % 2, window, half, first:last, :]
            inner = dd_ref[pl.ds(2 * pair + half, 1), here]
            ds = (e.astype(F32) * (current - inner)).astype(BF16)
            dq = dot(k_cols[mine, span], ds)
            if part == 0:
                dq_up[mine, here] = dq
            else:
                at = pl.multiple_of(pair * 384 + half * HEAD_DIM, HEAD_DIM)
                d3[pl.ds(at, HEAD_DIM), here] = ((dq + dq_up[mine, here]) * 0.125).astype(BF16)
            dk_acc[rows, span] += dot_nt(qt_ref[mine, here], ds)
            dv_acc[rows, span] += dot_nt(dot_ref[mine, here], e)

    inside = slice(TILE, PADDED - TILE)

    @pl.loop(0, 4)
    def _(pair):
        @pl.when(pair < 3)
        def _():
            for copy in e_copies(pair + 1, 0):
                copy.start()

        @pl.when(pair == 3)
        def _():
            for copy in e_copies(0, 1):
                copy.start()

        pass_over(pair, 0, vals_up, kt_up)
        at = pl.multiple_of(pair * 256, 256)
        d2[pl.ds(at, 128), :] = dk_acc[:, inside].astype(BF16)
        d2[pl.ds(at + 128, 128), :] = dv_acc[:, inside].astype(BF16)

        @pl.when(pair == 2)
        def _():
            sum_in.advance(1)

    sum_bo.advance(1)
    for window in range(WINDOWS):
        here = slice(window * QUERIES, window * QUERIES + QUERIES)
        dxu[:, here] = dot(w2[...], d2[:, here]).astype(BF16)

        @pl.when(band > 0)
        def _(window=window):
            halo(window).start()

    @pl.loop(0, 4)
    def _(pair):
        @pl.when(pair < 3)
        def _():
            for copy in e_copies(pair + 1, 1):
                copy.start()

        pass_over(pair, 1, vals, kt)

        @pl.when(pair == 0)
        def _():
            sum_bo.advance(2)
            sum_in.advance(2)

        @pl.when(pair == 1)
        def _():
            sum_bo.advance(3)
            sum_in.advance(3)

        @pl.when(pair == 2)
        def _():
            sum_bo.finish(write_bo)
            sum_in.advance(4)

        @pl.when(pair == 3)
        def _():
            sum_in.finish(write_in)

        for earlier in range(3):
            for stage in range(3 - earlier):

                @pl.when(pair == earlier + 1 + stage)
                def _(earlier=earlier, stage=stage):
                    sum_qkv(earlier).advance(stage)

        at = pl.multiple_of(pair * 384, 128)
        d3[pl.ds(at + 128, 128), :] = dk_acc[:, inside].astype(BF16)
        d3[pl.ds(at + 256, 128), :] = dv_acc[:, inside].astype(BF16)
        grads = dot_nt(xt_ref[...], d3[pl.ds(at, 384), :])
        grads_up = dot_nt(xut_ref[...], d2[pl.ds(pl.multiple_of(pair * 256, 256), 256), :])
        share = qkv_buf.shape[2]
        low_q = grads[:, 0:128].astype(BF16)
        low_kv = (grads[:, 128:384] + grads_up).astype(BF16)
        for owner in range(size):
            rows = slice(owner * share, owner * share + share)
            qkv_buf[pair, reversed_bits(owner, size), :, 0:128] = low_q[rows]
            qkv_buf[pair, reversed_bits(owner, size), :, 128:384] = low_kv[rows]
        sum_qkv(pair).start(0)

    shape = (16, LEN)
    channel = (iota(shape, 1) // TILE + iota(shape, 1) % FLANK_COLS) % 3
    chosen = jnp.where(channel + 9 == iota(shape, 0), 1.0, 0.0).astype(BF16)
    sums = dot_nt(chosen, dr1_ref[...].astype(BF16))
    totals = dot_nt(chosen, d3[...])
    high = totals.astype(BF16)
    sums += dot_nt(high, w3[...]) + dot_nt((totals - high.astype(F32)).astype(BF16), w3[...])
    sums += dot_nt(chosen, dxu[...]) * jnp.where(band > 0, 1.0, 0.0)
    small_buf[0] = small_in[...] + sums
    sum_small.start(0)

    @pl.when(band == size - 1)
    def _():
        below[...] = jnp.zeros_like(below)

    chains = [(sum_qkv(pair), write_qkv(pair), 3 - pair) for pair in range(4)]

    @pl.loop(0, WINDOWS)
    def _(window):
        @pl.when(band < size - 1)
        def _():
            halo(window).wait_recv()

        here = pl.ds(pl.multiple_of(window * QUERIES, QUERIES), QUERIES)
        dx = dr1_ref[:, here] + dot(w3[...], d3[:, here]) + below[:, here].astype(F32)
        rows = dot_nt(eye, dx.astype(BF16)).astype(BF16)
        for half in range(2):
            at = pl.multiple_of((2 * window + half) * FLANK_COLS, FLANK_COLS)
            gt_ref[:, pl.ds(at, FLANK_COLS), :] = rows[half * TILE : half * TILE + TILE].reshape(
                BLOCK_ROWS, FLANK_COLS, -1
            )

        for turn in range(depth + 1):

            @pl.when(window == turn + 5 - depth)
            def _(turn=turn):
                for chain, write, done in chains:
                    stage = done + turn
                    if stage < depth:
                        chain.advance(stage)
                    if stage == depth:
                        chain.finish(write)
                if turn < depth:
                    sum_small.advance(turn)
                else:
                    small_ref[...] = sum_small.finish()

    @pl.when(band > 0)
    def _():
        for window in range(WINDOWS):
            halo(window).wait_send()


def emit_kernel(
    qkv_ref, gin_ref, gbo_ref, small_ref,
    gq, gk, gv, gout, gin, gbi, gback, gbb, gg1, gs1, gg2, gs2, gemb,
    *, size,
):
    for pair in range(4):
        for index, ref in enumerate((gq, gk, gv)):
            ref[:, pair * 128 : pair * 128 + 128] = qkv_ref[pair, :, index * 128 : index * 128 + 128]
    back_share = gback.shape[0]
    gback[...] = gbo_ref[0:back_share]
    gout[...] = gbo_ref[back_share:]
    gin[...] = gin_ref[...]
    band = lax.axis_index("band")
    share = gout.shape[0]
    mine = 0.0
    for owner in range(size):
        mine = mine + jnp.where(band == owner, small_ref[:, owner * share : owner * share + share], 0.0)
    for row, ref in ((2, gbb), (3, gg1), (4, gs1), (0, gg2), (1, gs2)):
        ref[...] = mine[row : row + 1]
    gemb[...] = mine[9:12]
    per_row = small_ref.shape[1] // back_share
    bias = 0.0
    for owner in range(size):
        at = owner % per_row * back_share
        row = small_ref[5 + owner // per_row : 6 + owner // per_row, at : at + back_share]
        bias = bias + jnp.where(band == owner, row, 0.0)
    gbi[...] = bias


def shards(
    tokens, row_place, row_width, cotangent, chan_embed, w_query, w_key, w_value, w_out, w_in,
    bias_in, w_back, bias_back, gain_first, shift_first, gain_second, shift_second,
):
    width = tokens.shape[3]
    ff = w_in.shape[1]
    tok = tokens.reshape(BLOCK_ROWS, ROW_POS, width)
    cot = cotangent.reshape(BLOCK_ROWS, ROW_POS, width)
    shape = jax.ShapeDtypeStruct
    size, groups = lax.axis_size("band"), lax.axis_size("grp")
    dma = pltpu.SemaphoreType.DMA
    params = pltpu.CompilerParams(vmem_limit_bytes=LIMIT)
    xt, xut, qt, ot, inv, e_all = pl.pallas_call(
        functools.partial(attend_kernel, size=size),
        name="attend_forward",
        out_shape=(
            shape((width, LEN), BF16),
            shape((width, LEN), BF16),
            shape((width, LEN), BF16),
            shape((width, LEN), BF16),
            shape((8, LEN), F32),
            shape((WINDOWS, 8, 2 * SPAN, QUERIES), BF16),
        ),
        in_specs=[smem()] * 2 + [vmem()] * 5,
        out_specs=(vmem(), vmem(), vmem(), vmem(), vmem(), hbm()),
        scratch_shapes=[
            pltpu.VMEM((ROW_POS, width), F32),
            pltpu.VMEM((BLOCK_ROWS, ROW_POS, width), BF16),
            pltpu.VMEM((width, width), BF16),
            pltpu.VMEM((width, width), BF16),
            pltpu.VMEM((width, LEN), BF16),
            pltpu.VMEM((4, PADDED, 128), BF16),
            pltpu.VMEM((4, PADDED, 128), BF16),
            pltpu.VMEM((8, HEAD_DIM + 16, PADDED), BF16),
            pltpu.VMEM((8, HEAD_DIM + 16, PADDED), BF16),
            pltpu.VMEM((SPAN, QUERIES), F32),
            pltpu.VMEM((SPAN, 128), BF16),
            pltpu.VMEM((128, QUERIES), BF16),
            pltpu.VMEM((2, 8, 2 * SPAN, QUERIES), BF16),
            dma((2,)),
            dma((WINDOWS,)),
            dma((WINDOWS,)),
        ],
        compiler_params=pltpu.CompilerParams(
            vmem_limit_bytes=LIMIT, collective_id=1, has_side_effects=True
        ),
    )(row_place, row_width, tok, chan_embed, w_query, w_key, w_value)
    share, back_share = width // size, ff // size
    vectors = jnp.concatenate(
        [bias_in, bias_back, gain_first, shift_first, gain_second, shift_second]
    ).reshape(1, -1)
    layer_out, dr1, do_t, dd, g_in, g_bo, small = pl.pallas_call(
        feed_kernel,
        name="feed_forward_and_back",
        out_shape=(
            shape((BLOCK_ROWS, ROW_POS, width), BF16),
            shape((width, LEN), F32),
            shape((width, LEN), BF16),
            shape((8, LEN), F32),
            shape((size, share, ff), BF16),
            shape((size, back_share + share, width), BF16),
            shape((16, width), F32),
        ),
        in_specs=[vmem()] * 9,
        out_specs=(vmem(),) * 7,
        scratch_shapes=[
            pltpu.VMEM((ROW_POS, width), F32),
            pltpu.VMEM((width, width), BF16),
            pltpu.VMEM((ff, width), BF16),
            pltpu.VMEM((width, ff), BF16),
            pltpu.VMEM((5, width, 128), F32),
            pltpu.VMEM((ff, 128), F32),
            pltpu.VMEM((5, width, 128), F32),
            pltpu.VMEM((ff, 128), F32),
            pltpu.VMEM((width, QUERIES), F32),
            pltpu.VMEM((width, QUERIES), F32),
            pltpu.VMEM((ff, QUERIES), F32),
            pltpu.VMEM((width, LEN), BF16),
            pltpu.VMEM((width, LEN), BF16),
            pltpu.VMEM((width, LEN), BF16),
            pltpu.VMEM((ff, LEN), BF16),
            pltpu.VMEM((ff, LEN), BF16),
        ],
        compiler_params=params,
    )(tok, cot, chan_embed, ot, inv, w_out, w_in, w_back, vectors)
    stages = levels(size) + 2 * (groups - 1)
    grad_tokens, g_qkv, g_in, g_bo, small = pl.pallas_call(
        functools.partial(back_kernel, size=size, groups=groups),
        name="attend_backward",
        out_shape=(
            shape((BLOCK_ROWS, ROW_POS, width), BF16),
            shape((4, share, 384), F32),
            shape((share, ff), F32),
            shape((back_share + share, width), F32),
            shape((16, width), F32),
        ),
        in_specs=[vmem()] * 10 + [hbm()] * 3,
        out_specs=(vmem(),) * 5,
        scratch_shapes=[
            pltpu.VMEM((width, width), BF16),
            pltpu.VMEM((width, 3 * width), BF16),
            pltpu.VMEM((width, 2 * width), BF16),
            pltpu.VMEM((4, PADDED, 128), BF16),
            pltpu.VMEM((4, PADDED, 128), BF16),
            pltpu.VMEM((width, PADDED), BF16),
            pltpu.VMEM((width, PADDED), BF16),
            pltpu.VMEM((width, LEN), F32),
            pltpu.VMEM((3 * width, LEN), BF16),
            pltpu.VMEM((2 * width, LEN), BF16),
            pltpu.VMEM((128, PADDED), F32),
            pltpu.VMEM((128, PADDED), F32),
            pltpu.VMEM((width, LEN), BF16),
            pltpu.VMEM((width, LEN), BF16),
            pltpu.VMEM((2, WINDOWS, 2, SPAN, QUERIES), BF16),
            dma((2, WINDOWS)),
            dma((2,)),
            pltpu.VMEM((size, share, ff), BF16),
            pltpu.VMEM((size, share, ff), BF16),
            pltpu.VMEM((groups - 1, size // 2, share, ff // groups), BF16),
            pltpu.VMEM((groups, share, ff // groups), F32),
            pltpu.VMEM((size, back_share + share, width), BF16),
            pltpu.VMEM((size, back_share + share, width), BF16),
            pltpu.VMEM((groups, back_share + share, width), BF16),
            pltpu.VMEM((4, size, share, 384), BF16),
            pltpu.VMEM((4, size, share, 384), BF16),
            pltpu.VMEM((4, groups, share, 384), BF16),
            pltpu.VMEM((levels(size) + 1, 16, width), F32),
            pltpu.VMEM((levels(size) + groups - 1, 16, width), F32),
            dma((stages,)),
            dma((stages,)),
            dma((stages,)),
            dma((stages,)),
            dma((4, stages)),
            dma((4, stages)),
            dma((stages,)),
            dma((stages,)),
            dma((WINDOWS,)),
            dma((WINDOWS,)),
        ],
        compiler_params=pltpu.CompilerParams(
            vmem_limit_bytes=LIMIT, collective_id=0, has_side_effects=True
        ),
    )(w_query, w_key, w_value, xt, xut, qt, do_t, dd, dr1, small, e_all, g_in, g_bo)
    vector = shape((1, share), F32)
    square = shape((share, width), F32)
    gq, gk, gv, gout, gin, gbi, gback, gbb, gg1, gs1, gg2, gs2, gemb = pl.pallas_call(
        functools.partial(emit_kernel, size=size),
        name="emit_shares",
        out_shape=(
            square, square, square, square, shape((share, ff), F32), shape((1, back_share), F32),
            shape((back_share, width), F32), vector, vector, vector, vector, vector,
            shape((3, share), F32),
        ),
        in_specs=[vmem()] * 4,
        out_specs=(vmem(),) * 13,
        compiler_params=pltpu.CompilerParams(vmem_limit_bytes=16 * 1024 * 1024),
    )(g_qkv, g_in, g_bo, small)
    return (
        layer_out.reshape(tokens.shape),
        grad_tokens.reshape(tokens.shape),
        gq, gk, gv, gout, gin, gbi.reshape(-1), gback,
        gbb.reshape(-1), gg1.reshape(-1), gs1.reshape(-1), gg2.reshape(-1), gs2.reshape(-1), gemb,
    )


def solution(mesh):
    tall = P("grp", "band", None, None)
    return jax.shard_map(
        shards,
        mesh=mesh,
        in_specs=(tall, P("grp", "band"), P("grp", "band"), tall) + (P(),) * 13,
        out_specs=(tall, tall)
        + (P("band", None),) * 5
        + (P("band"), P("band", None))
        + (P("band"),) * 5
        + (P(None, "band"),),
        check_vma=False,
    )
```

time: 288 us -> 197 us (0.68)
  Pallas kernels: 264 us -> 186 us
  local copies, waits for them, and re-layouts: 18.4 us -> 7.81 us
    pallas_call x1, Pallas kernels: 154 us -> 98.9 us  [shards(): pl.pallas_call(functools.partial(back_kernel, size=size, groups=groups),...]
    pallas_call x1 -> x2, Pallas kernels: 49.6 us -> 37.7 us  [the longest x1 36.8 us: shards(): pl.pallas_call(functools.partial(attend_kernel, size=size), name='attend_...]
    pallas_call x1, Pallas kernels: 60.1 us -> 49.9 us  [shards(): pl.pallas_call(feed_kernel, name='feed_forward_and_back', out_shape=(shap...]
    slice x7 -> x0, local copies, waits for them, and re-layouts: 4.88 us -> none  [the longest x1 1.67 us: shards(): g_bo[:back_share]]
    unnamed x16 -> x26, local copies, waits for them, and re-layouts: 8.52 us -> 7.18 us
  transfers between devices with their start and end apart: 1 -> 0, of which waited for: 0 -> 0; matrix products, arithmetic and copies ran while one was open for 2% -> 0% of each run, Pallas kernels for 0% -> 0%
where the time goes in v3:
time: 197 us; the launch traced here: 196 us
  Pallas kernels  186 us (94%)
  local copies, waits for them, and re-layouts  7.81 us (4%)
  between operations  2.04 us (1%)
    pallas_call x1, Pallas kernels, shards(): pl.pallas_call(functools.partial(back_kernel, size=size, groups=groups),...  98.9 us
    pallas_call x1, Pallas kernels, shards(): pl.pallas_call(feed_kernel, name='feed_forward_and_back', out_shape=(shap...  49.9 us
    pallas_call x1, Pallas kernels, shards(): pl.pallas_call(functools.partial(attend_kernel, size=size), name='attend_...  36.8 us
    unnamed x26, local copies, waits for them, and re-layouts  7.18 us

profile of v3, /device:TPU:0, one launch (start us, length us, event | category | flops | bytes accessed | tf_op | source)
XLA Modules:
  0.0 196.3 jit_solution(11466703459321102765)
XLA Ops:
  1.9 0.0 copy-start.4
  1.9 0.0 copy-start.6
  2.0 0.0 copy-start.7
  2.0 0.0 copy-start.8
  2.0 0.0 copy-start.9
  2.0 0.0 copy-start.5
  2.0 36.8 %attend_forward.1 = (bf16[512,1536]{1,0:T(8,128)(2,1)}, bf16[512,1536]{1,0:T(8,128)(2,1)}, bf16[512,1536]{1,0:T(8,128)(2,1)}, bf16[512,1536]{1,0:T(8,128)(2,1)},...) custom-call(s32[1,1]{1,0:T(1,128)S(6)} %copy.38.place_ref, s32[1,1]{1,0:T(1,128)S(6)} %copy.39.width_ref, ...), custom_call_target="tpu_custom_call" | custom-call | tf_op jit(solution)/shard_map/attend_forward/pallas_call | solution.py:978
  38.8 0.0 copy-done.4
  38.8 0.0 copy-done.6
  38.8 0.3 dynamic-update-slice.1
  39.1 0.0 copy-done.7
  39.1 0.2 dynamic-update-slice.2
  39.3 0.0 copy-done.8
  39.3 0.2 dynamic-update-slice.3
  39.5 0.2 dynamic-update-slice.4
  39.7 0.6 reshape.65.vec_ref
  40.4 49.9 %feed_forward_and_back.1 = (bf16[8,192,512]{2,1,0:T(8,128)(2,1)}, f32[512,1536]{1,0:T(8,128)}, bf16[512,1536]{1,0:T(8,128)(2,1)}, f32[8,1536]{1,0:T(8,128)}, bf1...) custom-call(bf16[8,192,512]{2,1,0:T(8,128)(2,1)} %bitcast.11, ...), custom_call_target="tpu_custom_call" | custom-call | tf_op jit(solution)/shard_map/feed_forward_and_back/pallas_call | solution.py:1017
  90.2 98.9 %attend_backward.1 = (bf16[8,192,512]{2,1,0:T(8,128)(2,1)}, f32[4,32,384]{2,1,0:T(8,128)}, f32[32,2048]{1,0:T(8,128)}, f32[160,512]{1,0:T(8,128)}, f32[16,512]{1,0:T(8,128)}) custom-call(bf16[512,512]{1,0:T(8,128)(2,1)} %wq_ref.3, bf16[512,512]{1,0:T(8,128)(2,1)} %wk_ref.3, bf16[512,512]{1,0:T(8,128)(2,1)} %wv_ref.3, ...), custom_call_target="tpu_custom_call" | custom-call | tf_op jit(solution)/shard_map/attend_backward/pallas_call | solution.py:1052
  189.1 1.0 copy-done
  190.1 0.9 copy-done.1
  191.1 0.9 copy-done.2
  192.0 0.8 copy-done.3
  192.7 0.9 emit_shares.1
  193.7 2.7 %copy.40 = bf16[1,1,1536,512]{3,2,1,0:T(8,128)(2,1)} copy(bf16[1,1,1536,512]{3,2,1,0:T(8,128)(2,1)} %bitcast.13) | data formatting | bytes 3145728
  (8 shorter events, 0.0 us)
Async XLA Ops:
  1.9 36.9 %copy-start.4 = (bf16[2048]{0:T(1024)(128)(2,1)S(1)}, bf16[2048]{0:T(1024)(128)(2,1)}, u32[]{:S(2)}) copy-start(bf16[2048]{0:T(1024)(128)(2,1)} %param.27) | copy-start | bytes 12292
  1.9 36.9 %copy-start.6 = (bf16[512]{0:T(512)(128)(2,1)S(1)}, bf16[512]{0:T(512)(128)(2,1)}, u32[]{:S(2)}) copy-start(bf16[512]{0:T(512)(128)(2,1)} %param.29) | copy-start | bytes 3076
  2.0 37.1 %copy-start.7 = (bf16[512]{0:T(512)(128)(2,1)S(1)}, bf16[512]{0:T(512)(128)(2,1)}, u32[]{:S(2)}) copy-start(bf16[512]{0:T(512)(128)(2,1)} %param.30) | copy-start | bytes 3076
  2.0 37.3 %copy-start.8 = (bf16[512]{0:T(512)(128)(2,1)S(1)}, bf16[512]{0:T(512)(128)(2,1)}, u32[]{:S(2)}) copy-start(bf16[512]{0:T(512)(128)(2,1)} %param.31) | copy-start | bytes 3076
  2.0 37.5 %copy-start.9 = (bf16[512]{0:T(512)(128)(2,1)S(1)}, bf16[512]{0:T(512)(128)(2,1)}, u32[]{:S(2)}) copy-start(bf16[512]{0:T(512)(128)(2,1)} %param.32) | copy-start | bytes 3076
  2.0 37.8 %copy-start.5 = (bf16[512]{0:T(512)(128)(2,1)S(1)}, bf16[512]{0:T(512)(128)(2,1)}, u32[]{:S(2)}) copy-start(bf16[512]{0:T(512)(128)(2,1)} %param.33) | copy-start | bytes 3076
  189.1 1.0 copy-start
  190.1 0.9 copy-start.1
  191.1 0.9 copy-start.2
  192.0 0.8 copy-start.3

commit v4 on v3

v4 whole, which is shorter than its diff:
```python
import functools

import jax
import jax.numpy as jnp
from jax import lax
from jax.experimental import pallas as pl
from jax.experimental.pallas import tpu as pltpu
from jax.sharding import PartitionSpec as P

HEAD_DIM = 64
ROW_POS = 192
BLOCK_ROWS = 8
BLOCK_COLS = 32
FLANK_COLS = 16
WINDOWS = ROW_POS // BLOCK_COLS
BLOCKS = ROW_POS // FLANK_COLS
TILE = BLOCK_ROWS * FLANK_COLS
QUERIES = 2 * TILE
SPAN = 4 * TILE
LEN = BLOCK_ROWS * ROW_POS
PADDED = LEN + 2 * TILE

norm_eps = 1e-06
big_negative = -1e30
F32 = jnp.float32
BF16 = jnp.bfloat16
LOG2_E = 1.4426950408889634
GELU_SCALE = 0.7978845608028654
GELU_CUBE = 0.044715


def dot(left, right):
    return jnp.dot(left, right, preferred_element_type=F32)


def dot_nt(left, right):
    return lax.dot_general(left, right, (((1,), (1,)), ((), ())), preferred_element_type=F32)


def iota(shape, dim):
    return lax.broadcasted_iota(jnp.int32, shape, dim)


def identity(size):
    return jnp.where(iota((size, size), 0) == iota((size, size), 1), 1.0, 0.0).astype(BF16)


def transposed(eye, value):
    step = eye.shape[0]
    parts = [
        dot_nt(eye, value[:, at : at + step]).astype(BF16) for at in range(0, value.shape[1], step)
    ]
    return jnp.concatenate(parts, axis=0)


def column(eye, row):
    step = eye.shape[0]
    ones = jnp.ones((128, step), BF16)
    parts = [
        dot_nt(jnp.where(eye > 0, row[:, at : at + step], 0).astype(BF16), ones)
        for at in range(0, row.shape[1], step)
    ]
    return jnp.concatenate(parts, axis=0)


def wide(value):
    return jnp.concatenate([value, value], axis=1)


def halves(value):
    return value[:, :128] + value[:, 128:]


def fill_embed(embed_ref, rows_ref):
    embed = embed_ref[...].astype(F32)
    channel = lax.rem(iota(rows_ref.shape, 0), 3)
    rows_ref[...] = jnp.where(
        channel == 0, embed[0:1], jnp.where(channel == 1, embed[1:2], embed[2:3])
    ).astype(BF16)


def block_rows(rows_ref, block):
    return rows_ref[:, pl.ds(pl.multiple_of(block * FLANK_COLS, FLANK_COLS), FLANK_COLS), :]


def raw_window(rows_ref, window):
    parts = [block_rows(rows_ref, 2 * window + half).reshape(TILE, -1) for half in range(2)]
    return jnp.concatenate(parts, axis=0)


def embed_window(embed_rows, window):
    parts = []
    for half in range(2):
        at = pl.multiple_of((2 * window + half) * FLANK_COLS, FLANK_COLS)
        part = embed_rows[pl.ds(at, FLANK_COLS), :][None]
        parts.append(jnp.broadcast_to(part, (BLOCK_ROWS,) + part.shape[1:]).reshape(TILE, -1))
    return jnp.concatenate(parts, axis=0)


def start_window(rows_ref, embed_rows, window):
    return raw_window(rows_ref, window).astype(F32) + embed_window(embed_rows, window).astype(F32)


def norm_stats(value):
    center = value - jnp.mean(value, axis=0, keepdims=True)
    spread = jnp.mean(center * center, axis=0, keepdims=True)
    inverse = lax.rsqrt(spread + norm_eps)
    return center * inverse, inverse


def norm_back(normed, inverse, grad, gain):
    scaled = grad * gain
    first = jnp.mean(scaled, axis=0, keepdims=True)
    second = jnp.mean(scaled * normed, axis=0, keepdims=True)
    return (scaled - first - normed * second) * inverse


def vmem():
    return pl.BlockSpec(memory_space=pltpu.VMEM)


def smem():
    return pl.BlockSpec(memory_space=pltpu.SMEM)


def hbm():
    return pl.BlockSpec(memory_space=pl.ANY)


LIMIT = 62 * 1024 * 1024


def head_of_pair(value, half):
    keep = (iota(value.shape, 0) // HEAD_DIM) == half
    return jnp.where(keep, value, jnp.zeros_like(value))


def clear_pads_rows(ref):
    pad = jnp.zeros((ref.shape[0], TILE, ref.shape[2]), ref.dtype)
    ref[:, 0:TILE, :] = pad
    ref[:, PADDED - TILE : PADDED, :] = pad


def reversed_bits(index, count):
    place, bit = 0, 1
    while bit < count:
        place = place + (index // bit) % 2 * (count // (2 * bit))
        bit *= 2
    return place


def levels(count):
    return count.bit_length() - 1


def first_share(band, bits, count):
    start = 0
    for level in range(bits):
        start = start + (band // (1 << level)) % 2 * (count >> (level + 1))
    return start


class Reduction:
    def __init__(self, buf, shape, recv, later, across, gathered, send_sem, recv_sem, place):
        self.buf, self.recv, self.later = buf, recv, later
        self.across, self.gathered = across, gathered
        self.send_sem, self.recv_sem = send_sem, recv_sem
        self.band, self.grp, self.size, self.groups = place
        self.depth = depth = levels(self.size)
        self.rows = shape[0] // self.size
        self.stages = [("halve", 0)]
        if gathered is None:
            self.stages += [("direct", 1), ("sum", depth)]
        else:
            self.stages += [("split", 1)] + [("halve", bit) for bit in range(1, depth)]
            self.stages += [("gather", depth)]
        self.part = shape[1] // self.groups

    def start_of(self, bits):
        return first_share(self.band, bits, self.size)

    def columns_of(self, member):
        return pl.ds(pl.multiple_of(member * self.part, 128), self.part)

    def columns(self, stage):
        split = [kind for kind, _ in self.stages[:stage]].count("split")
        return self.columns_of(self.grp) if split else slice(None)

    def shares(self, first, count=1):
        return pl.ds(pl.multiple_of(first * self.rows, self.rows), count * self.rows)

    def landing(self, bits):
        return self.later if bits else self.recv

    def landing_rows(self, bits, index, count):
        return self.shares(index + (self.size >> (bits + 1) if bits else 0), count)

    def copies(self, stage):
        kind, bits = self.stages[stage]
        columns = self.columns(stage)
        pieces = []
        if kind == "halve":
            half = self.size >> (bits + 1)
            bit = (self.band // (1 << bits)) % 2
            pieces.append(
                (
                    self.buf.at[self.shares(self.start_of(bits) + (1 - bit) * half, half), columns],
                    self.landing(bits).at[self.landing_rows(bits, 0, half)],
                    bits,
                    (self.band + (1 << bits) * (1 - 2 * bit), self.grp),
                )
            )
        if kind == "direct":
            for step in range(1, self.size // 2):
                partner = (self.band + 2 * step) % self.size
                source = self.buf.at[self.shares(reversed_bits(partner, self.size))]
                place = (partner, self.grp)
                pieces.append((source, self.later.at[self.shares(step)], step, place))
        for step in range(1, self.groups):
            partner = (self.grp + step) % self.groups
            place = (self.band, partner)
            if kind == "sum":
                source, target = self.buf.at[self.shares(self.start_of(bits))], self.across.at[step]
                pieces.append((source, target, self.size // 2 + step - 1, place))
            if kind == "split":
                rows = self.shares(self.start_of(bits), self.size >> bits)
                source = self.buf.at[rows, self.columns_of(partner)]
                pieces.append((source, self.across.at[step - 1], self.depth + step - 1, place))
            if kind == "gather":
                source, target = self.gathered.at[0], self.gathered.at[step]
                pieces.append((source, target, self.depth + self.groups + step - 2, place))
        return [
            pltpu.make_async_remote_copy(
                src_ref=source,
                dst_ref=target,
                send_sem=self.send_sem(sem),
                recv_sem=self.recv_sem(sem),
                device_id=place,
                device_id_type=pl.DeviceIdType.MESH,
            )
            for source, target, sem, place in pieces
        ]

    def start(self, stage):
        for copy in self.copies(stage):
            copy.start()

    def advance(self, stage):
        for copy in self.copies(stage):
            copy.wait()
        kind, bits = self.stages[stage]
        if kind == "halve":
            columns = self.columns(stage)
            half, keep = self.size >> (bits + 1), self.start_of(bits + 1)

            @pl.loop(0, half)
            def _(index):
                mine = self.shares(keep + index)
                total = self.buf[mine, columns].astype(F32)
                total = total + self.landing(bits)[self.landing_rows(bits, index, 1), :].astype(F32)
                self.buf[mine, columns] = total.astype(BF16)
        elif kind == "direct":
            mine = self.shares(self.start_of(self.depth))
            total = self.buf[mine, :].astype(F32)
            for step in range(1, self.size // 2):
                total = total + self.later[step * self.rows : (step + 1) * self.rows, :].astype(F32)
            self.buf[mine, :] = total.astype(BF16)
        else:
            columns = self.columns_of(self.grp)
            keep = self.start_of(bits)

            @pl.loop(0, self.size >> bits)
            def _(index):
                mine = self.shares(keep + index)
                total = self.buf[mine, columns].astype(F32)
                for step in range(self.groups - 1):
                    total = total + self.across[step, self.shares(index), :].astype(F32)
                self.buf[mine, columns] = total.astype(BF16)

        if self.stages[stage + 1][0] == "gather":
            mine = self.shares(self.start_of(self.depth))
            self.gathered[0] = self.buf[mine, self.columns_of(self.grp)].astype(F32)
        self.start(stage + 1)

    def finish(self, out):
        last = len(self.stages) - 1
        for copy in self.copies(last):
            copy.wait()
        if self.stages[last][0] == "sum":
            self.across[0] = self.buf[self.shares(self.start_of(self.depth)), :]
            total = 0.0
            for member in range(self.groups):
                step = (self.grp + self.groups - member) % self.groups
                total = total + self.across[step].astype(F32)
            out(total)
        else:
            for step in range(self.groups):
                member = (self.grp + self.groups - step) % self.groups
                out(self.gathered[step], self.columns_of(member))


class SmallSum:
    def __init__(self, buf, recv, send_sem, recv_sem, place):
        self.buf, self.recv, self.send_sem, self.recv_sem = buf, recv, send_sem, recv_sem
        self.band, self.grp, self.size, self.groups = place

    def copies(self, stage):
        half = self.size // 2
        if stage == 0:
            partners = [(0, (self.band + 1 - 2 * (self.band % 2), self.grp))]
        elif stage == 1:
            partners = [
                (step, ((self.band + 2 * step) % self.size, self.grp)) for step in range(1, half)
            ]
        else:
            partners = [
                (half + step - 1, (self.band, (self.grp + step) % self.groups))
                for step in range(1, self.groups)
            ]
        return [
            pltpu.make_async_remote_copy(
                src_ref=self.buf.at[stage],
                dst_ref=self.recv.at[slot],
                send_sem=self.send_sem.at[slot],
                recv_sem=self.recv_sem.at[slot],
                device_id=partner,
                device_id_type=pl.DeviceIdType.MESH,
            )
            for slot, partner in partners
        ]

    def start(self, stage):
        for copy in self.copies(stage):
            copy.start()

    def advance(self, stage):
        for copy in self.copies(stage):
            copy.wait()
        total = self.buf[stage]
        for slot in (0,) if stage == 0 else range(1, self.size // 2):
            total = total + self.recv[slot]
        self.buf[stage + 1] = total
        self.start(stage + 1)

    def finish(self):
        for copy in self.copies(2):
            copy.wait()
        mine = self.buf[2]
        total = 0.0
        for member in range(self.groups):
            step = (self.grp + self.groups - member) % self.groups
            slot = jnp.where(step == 0, 0, self.size // 2 + step - 1)
            total = total + jnp.where(step == 0, mine, self.recv[slot])
        return total


def store_pairs(ref, at, value):
    for pair in range(value.shape[1] // 128):
        ref[pair, pl.ds(at, value.shape[0]), :] = value[:, pair * 128 : (pair + 1) * 128]


def store_heads(ref, at, value):
    for head in range(value.shape[0] // HEAD_DIM):
        rows = slice(head * HEAD_DIM, head * HEAD_DIM + HEAD_DIM)
        ref[head, 0:HEAD_DIM, pl.ds(at, value.shape[1])] = value[rows]


def clear_pads_lanes(ref):
    pad = jnp.zeros(ref.shape[:2] + (TILE,), ref.dtype)
    ref[:, :, 0:TILE] = pad
    ref[:, :, PADDED - TILE : PADDED] = pad


def gelu_and_slope(u):
    square = u * u
    cube = (GELU_SCALE * GELU_CUBE) * square
    h = 0.5 * jnp.tanh(u * (GELU_SCALE + cube)) + 0.5
    g = u * (2.0 * GELU_SCALE + 6.0 * cube)
    return u * h, h * (1.0 + (1.0 - h) * g)


class Steps:
    def __init__(self, reduction, write):
        self.reduction, self.write, self.stage = reduction, write, 0

    def __call__(self):
        if self.stage < len(self.reduction.stages) - 1:
            self.reduction.advance(self.stage)
            self.stage += 1

    def last(self):
        while self.stage < len(self.reduction.stages) - 1:
            self()
        self.reduction.finish(self.write)


def layer_kernel(
    place_ref, width_ref, embed_ref, bi_ref, bb_ref, g1_ref, s1_ref, g2_ref, s2_ref, tok_h, cot_h, wq_h, wk_h, wv_h, wo_h, wi_h, wb_h,
    out_h, gt_h, e_h, qkv_ref, gin_ref, gback_ref, gout_ref, small_ref,
    tok, side, w4, wta, wtb, ww, wt, xt, xut, qt, ot, da, rows_a, rows_b, cols_a, cols_b, hd,
    bias_low, bias_up, ones_row, embed_rows, cols, bi_col, n1_buf, d_o, acc, below,
    inv, dd,
    in_recv, in_later, in_across, in_parts, back_recv, back_later, back_across, back_parts,
    out_recv, out_later, out_across,
    qkv_recv, qkv_later, qkv_across, small_buf, small_recv, totals,
    load_sem, e_out_sem, e_in_sem, out_sem, up_ss, up_rs, halo_ss, halo_rs,
    in_ss, in_rs, back_ss, back_rs, go_ss, go_rs, qkv_ss, qkv_rs, small_ss, small_rs,
    *, size, groups, in_split, back_split,
):
    band, grp = lax.axis_index("band"), lax.axis_index("grp")
    place = (band, grp, size, groups)
    depth = levels(size)
    MESH = pl.DeviceIdType.MESH
    wq, wk, wv, wo = (w4.at[index] for index in range(4))
    wit, wb, wi, wbt = ww.at[0], ww.at[1], wt.at[0], wt.at[1]
    width, ff = wi_h.shape

    sources = (tok_h, wq_h, wk_h, wv_h, wo_h, wi_h, wb_h, cot_h)
    targets = (tok, wq, wk, wv, wo, wi, wb, side)
    loads = [
        pltpu.make_async_copy(source, target, load_sem.at[index])
        for index, (source, target) in enumerate(zip(sources, targets))
    ]
    for load in loads[:7]:
        load.start()
    barrier = pltpu.get_barrier_semaphore()
    odd = band % 2
    pl.semaphore_signal(barrier, inc=1, device_id=(band + 1 - 2 * odd, grp), device_id_type=MESH)
    for step in range(1, size // 2):
        pl.semaphore_signal(
            barrier, inc=1, device_id=((band + 2 * step) % size, grp), device_id_type=MESH
        )
    for step in range(1, groups):
        pl.semaphore_signal(
            barrier, inc=1, device_id=(band, (grp + step) % groups), device_id_type=MESH
        )
    beyond = (odd == 1) & (band < size - 1) | (odd == 0) & (band > 0)

    @pl.when(beyond)
    def _():
        pl.semaphore_signal(
            barrier, inc=1, device_id=(band + 2 * odd - 1, grp), device_id_type=MESH
        )

    pl.semaphore_wait(barrier, size // 2 + groups - 1 + jnp.where(beyond, 1, 0))

    def up_copy(window):
        columns = pl.ds(pl.multiple_of(window * BLOCK_COLS, BLOCK_COLS), BLOCK_COLS)
        return pltpu.make_async_remote_copy(
            src_ref=tok_h.at[:, columns, :], dst_ref=side.at[:, columns, :],
            send_sem=up_ss.at[window], recv_sem=up_rs.at[window],
            device_id=(jnp.minimum(band + 1, size - 1), grp), device_id_type=MESH,
        )

    def halo(window):
        here = pl.ds(pl.multiple_of(window * QUERIES, QUERIES), QUERIES)
        return pltpu.make_async_remote_copy(
            src_ref=dxu.at[:, here], dst_ref=below.at[:, here],
            send_sem=halo_ss.at[window], recv_sem=halo_rs.at[window],
            device_id=(jnp.maximum(band - 1, 0), grp), device_id_type=MESH,
        )

    @pl.when(band < size - 1)
    def _():
        for window in range(WINDOWS):
            up_copy(window).start()

    @pl.when(band == 0)
    def _():
        side[...] = jnp.zeros_like(side)

    keys, keys_up, vt, vt_up, qs = rows_a, rows_b, cols_a, cols_b, da
    eye = identity(256)
    fill_embed(embed_ref, embed_rows)
    clear_pads_rows(keys)
    clear_pads_rows(keys_up)
    clear_pads_lanes(vt)
    clear_pads_lanes(vt_up)
    sums = jnp.where(iota((16, PADDED), 0) == 0, 1.0, 0.0).astype(BF16)
    for head in range(8):
        vt[head, HEAD_DIM:, :] = sums
        vt_up[head, HEAD_DIM:, :] = sums
    ones_row[...] = jnp.where(iota(ones_row.shape, 0) == 0, 1.0, 0.0).astype(BF16)
    for load in loads[:4]:
        load.wait()
    wta[...] = transposed(eye, wq[...])
    wtb[...] = transposed(eye, wv[...])
    has_up = jnp.where(band > 0, 1.0, 0.0)

    @pl.loop(0, WINDOWS)
    def _(window):
        at = pl.multiple_of(window * QUERIES, QUERIES)
        padded_at = pl.multiple_of(window * QUERIES + TILE, TILE)
        low = start_window(tok, embed_rows, window).astype(BF16)
        low_t = transposed(eye, low)
        xt[:, pl.ds(at, QUERIES)] = low_t
        q_low = dot(wta[...], low_t).astype(BF16)
        store_pairs(keys, padded_at, dot(low, wk[...]).astype(BF16))
        store_heads(vt, padded_at, dot(wtb[...], low_t).astype(BF16))
        qt[:, pl.ds(at, QUERIES)] = q_low * BF16(0.125)
        qs[:, pl.ds(at, QUERIES)] = (q_low.astype(F32) * (0.125 * LOG2_E)).astype(BF16)

    def prepare_upper(window):
        @pl.when(band > 0)
        def _():
            up_copy(window).wait_recv()

        at = pl.multiple_of(window * QUERIES, QUERIES)
        padded_at = pl.multiple_of(window * QUERIES + TILE, TILE)
        upper = (start_window(side, embed_rows, window) * has_up).astype(BF16)
        upper_t = transposed(eye, upper)
        xut[:, pl.ds(at, QUERIES)] = upper_t
        store_pairs(keys_up, padded_at, dot(upper, wk[...]).astype(BF16))
        store_heads(vt_up, padded_at, dot(wtb[...], upper_t).astype(BF16))

    first_block = place_ref[0, 0] > 0
    row_limit = width_ref[0, 0]
    mask_shape = (SPAN, QUERIES)
    memory, query = iota(mask_shape, 0), iota(mask_shape, 1)
    memory_col = (memory // TILE) * FLANK_COLS + memory % FLANK_COLS - FLANK_COLS
    query_col = (query // TILE) * FLANK_COLS + query % FLANK_COLS
    memory_row = (memory % TILE) // FLANK_COLS
    query_row = (query % TILE) // FLANK_COLS

    def prepare_masks(window):
        column_at = memory_col + window * BLOCK_COLS
        inside = (column_at >= 0) & (column_at < row_limit)
        earlier = (memory_row < query_row) | ((memory_row == query_row) & (memory_col <= query_col))
        itself = (memory_row == query_row) & (memory_col == query_col)
        bias_low[...] = jnp.where((inside & earlier) | itself, 0.0, big_negative)
        first = iota(bias_up.shape, 1) == 0
        closed = jnp.where(inside[:, 0:128] & first_block, 0.0, big_negative)
        bias_up[...] = jnp.where(first, closed, 0.0).astype(BF16)

    def e_out(window, half):
        slot = window % 2
        return pltpu.make_async_copy(
            hd.at[slot, pl.ds(half * 2 * SPAN, 2 * SPAN), pl.ds(0, 4 * QUERIES)],
            e_h.at[window, half],
            e_out_sem.at[slot, half],
        )

    prepare_upper(0)

    @pl.loop(0, WINDOWS)
    def _(window):
        @pl.when(window < WINDOWS - 1)
        def _():
            prepare_upper(window + 1)

        prepare_masks(window)

        @pl.when(window > 1)
        def _():
            for half in range(2):
                e_out(window - 2, half).wait()

        slot = window % 2
        at = pl.multiple_of(window * QUERIES, QUERIES)
        here, span = pl.ds(at, QUERIES), pl.ds(at, SPAN)

        def scores(head):
            pair = head // 2
            q_head = head_of_pair(qs[pair * 128 : pair * 128 + 128, here], head % 2)
            upper = dot(
                jnp.concatenate([keys_up[pair, span, :], bias_up[...]], axis=1),
                jnp.concatenate([q_head, ones_row[...]], axis=0),
            )
            lower = dot(keys[pair, span, :], q_head) + bias_low[...]
            shape = (SPAN // 8, 8, QUERIES)
            top = jnp.maximum(
                jnp.max(upper.reshape(shape), axis=0), jnp.max(lower.reshape(shape), axis=0)
            )
            return upper, lower, jnp.max(top, axis=0, keepdims=True)

        def mix(head, e_up, e_low):
            mixed = dot(vt_up[head, :, span], e_up) + dot(vt[head, :, span], e_low)
            inverse = 1.0 / mixed[HEAD_DIM : HEAD_DIM + 1]
            rows = slice(head * HEAD_DIM, head * HEAD_DIM + HEAD_DIM)
            ot[rows, here] = (mixed[0:HEAD_DIM] * inverse).astype(BF16)
            inv[head : head + 1, here] = inverse

        current, raised = scores(0), None
        for head in range(8):
            upcoming = scores(head + 1) if head < 7 else None
            upper, lower, peak = current
            e_up = jnp.exp2(upper - peak).astype(BF16)
            e_low = jnp.exp2(lower - peak).astype(BF16)
            at_row, at_lane = head % 2 * 2 * SPAN, head // 2 * QUERIES
            hd[slot, at_row : at_row + SPAN, at_lane : at_lane + QUERIES] = e_up
            hd[slot, at_row + SPAN : at_row + 2 * SPAN, at_lane : at_lane + QUERIES] = e_low
            if head > 0:
                mix(head - 1, *raised)
            raised = (e_up, e_low)
            current = upcoming
        mix(7, *raised)
        for half in range(2):
            e_out(window, half).start()

    loads[7].start()
    for load in loads[4:7]:
        load.wait()
    wta[...] = transposed(eye, wo[...])
    wit[...] = transposed(eye, wi[...])
    wbt[...] = transposed(eye, wb[...])
    for index, ref in enumerate((bb_ref, g1_ref, s1_ref, g2_ref, s2_ref)):
        cols[index] = column(eye, ref[...].reshape(1, -1)).astype(BF16)
    bi_col[...] = column(eye, bi_ref[...].reshape(1, -1)).astype(BF16)
    acc[...] = jnp.zeros_like(acc)
    for window in range(WINDOWS - 2, WINDOWS):
        for half in range(2):
            e_out(window, half).wait()
    loads[7].wait()
    hl, dh = hd.at[0], hd.at[1]
    heads = width // HEAD_DIM

    def broadcast(index):
        return wide(cols[index].astype(F32))

    def gather(index, value):
        blocks = pl.ds(index * width // 128, width // 128)
        acc[blocks] += halves(value).reshape(width // 128, 128, 128)

    def out_copy(window):
        columns = pl.ds(pl.multiple_of(window * BLOCK_COLS, BLOCK_COLS), BLOCK_COLS)
        return pltpu.make_async_copy(
            tok.at[:, columns, :], out_h.at[:, columns, :], out_sem.at[window]
        )

    part = 256
    parts = [slice(at, at + part) for at in range(0, ff, part)]

    @pl.loop(0, WINDOWS)
    def _(window):
        here = pl.ds(pl.multiple_of(window * QUERIES, QUERIES), QUERIES)
        raw = raw_window(tok, window)
        embed = embed_window(embed_rows, window)
        start = jnp.concatenate(
            [
                dot_nt(eye, raw[:, half * 256 : half * 256 + 256])
                + dot_nt(eye, embed[:, half * 256 : half * 256 + 256])
                for half in range(2)
            ],
            axis=0,
        )
        n1, inv1 = norm_stats(start + dot(wta[...], ot[:, here]))
        y1 = n1 * broadcast(1) + broadcast(2)
        low = y1.astype(BF16)
        n1_buf[...] = n1
        cols_a[:, 0:HEAD_DIM, here] = low.reshape(heads, HEAD_DIM, QUERIES)

        upcoming = dot(wit[parts[0], :], low)
        for index, rows in enumerate(parts):
            u = upcoming + wide(bi_col[rows, :].astype(F32))
            if index + 1 < len(parts):
                upcoming = dot(wit[parts[index + 1], :], low)
            active, slope = gelu_and_slope(u)
            hl[rows, here] = active.astype(BF16)
            dh[rows, here] = slope.astype(BF16)

        f = dot(wbt[...], hl[:, here]) + broadcast(0)
        n2, inv2 = norm_stats(n1_buf[...] * broadcast(1) + broadcast(2) + f)
        g2 = broadcast(3)
        result = (n2 * g2 + broadcast(4)).astype(BF16)
        result = dot_nt(eye, result).astype(BF16)
        raw_cot = raw_window(side, window)
        for half in range(2):
            at = pl.multiple_of((2 * window + half) * FLANK_COLS, FLANK_COLS)
            tok[:, pl.ds(at, FLANK_COLS), :] = result[half * TILE : half * TILE + TILE].reshape(
                BLOCK_ROWS, FLANK_COLS, -1
            )
        cot = jnp.concatenate(
            [dot_nt(eye, raw_cot[:, half * 256 : half * 256 + 256]) for half in range(2)], axis=0
        )
        gather(0, cot * n2)
        gather(1, cot)
        dr2 = norm_back(n2, inv2, cot, g2)
        df_low = dr2.astype(BF16)
        cols_b[:, 0:HEAD_DIM, here] = df_low.reshape(heads, HEAD_DIM, QUERIES)

        upcoming = dot(wb[parts[0], :], df_low)
        for index, rows in enumerate(parts):
            current = upcoming
            if index + 1 < len(parts):
                upcoming = dot(wb[parts[index + 1], :], df_low)
            dh[rows, here] = (current * dh[rows, here].astype(F32)).astype(BF16)

        dy1 = dr2 + dot(wi[...], dh[:, here])
        n1 = n1_buf[...]
        gather(2, dy1 * n1)
        gather(3, dy1)
        dr1 = norm_back(n1, inv1, dy1, broadcast(1))
        da_low = dr1.astype(BF16)
        da[:, here] = da_low
        grad_o = dot(wo[...], da_low)
        product = grad_o * ot[:, here].astype(F32)
        for head in range(heads):
            rows = slice(head * HEAD_DIM, head * HEAD_DIM + HEAD_DIM)
            inverse = inv[head : head + 1, here]
            d_o[rows, here] = (grad_o[rows] * inverse).astype(BF16)
            dd[head : head + 1, here] = jnp.sum(product[rows], axis=0, keepdims=True) * inverse
        out_copy(window).start()

    small_buf[0] = jnp.zeros(small_buf.shape[1:], F32)
    ones = jnp.ones((8, 256), BF16)
    for index, row in enumerate((0, 1, 3, 4)):
        value = acc[pl.ds(index * width // 128, width // 128)].reshape(width, 128)
        high = value.astype(BF16)
        split = jnp.concatenate([high, (value - high.astype(F32)).astype(BF16)], axis=1)
        small_buf[0, row : row + 1, :] = dot_nt(ones, split)[0:1]

    def e_in(pair, part, window, half):
        if window < 4:
            target = ww.at[0, pl.ds(window * SPAN, SPAN), pl.ds(half * QUERIES, QUERIES)]
        else:
            at = (2 * (window - 4) + half) * QUERIES
            target = wt.at[1, :, pl.ds(at, QUERIES)]
        source = e_h.at[
            window, half, pl.ds(part * SPAN, SPAN), pl.ds(pl.multiple_of(pair * QUERIES, QUERIES), QUERIES)
        ]
        return pltpu.make_async_copy(source, target, e_in_sem.at[window, half])

    def e_tile(window, half, first, last):
        if window < 4:
            return ww[0, window * SPAN + first : window * SPAN + last, half * QUERIES : (half + 1) * QUERIES]
        at = (2 * (window - 4) + half) * QUERIES
        return wt[1, first:last, at : at + QUERIES]

    items = [(window, half) for window in range(WINDOWS) for half in range(2)]
    for window, half in items:
        e_in(0, 0, window, half).start()

    qkv_at = 3 * width
    gback, gin = ww.at[1], wt.at[0]
    gout = wt.at[1, :, pl.ds(4 * QUERIES, width)]
    sum_back = Reduction(
        gback, (ff, width), back_recv, back_later, back_across, back_parts if back_split else None,
        lambda k: back_ss.at[k], lambda k: back_rs.at[k], place,
    )
    sum_out = Reduction(
        gout, (width, width), out_recv, out_later, out_across, None,
        lambda k: go_ss.at[k], lambda k: go_rs.at[k], place,
    )
    sum_in = Reduction(
        gin, (width, ff), in_recv, in_later, in_across, in_parts if in_split else None,
        lambda k: in_ss.at[k], lambda k: in_rs.at[k], place,
    )

    def write_in(value, columns=slice(None)):
        gin_ref[:, columns] = value

    def write_back(value, columns=slice(None)):
        gback_ref[:, columns] = value

    def write_out(value):
        gout_ref[...] = value

    def write_qkv(pair):
        def write(value):
            qkv_ref[pair] = value

        return write

    def sum_qkv(pair):
        return Reduction(
            hd.at[1, pl.ds(qkv_at, width), pl.ds(pl.multiple_of(pair * 384, 128), 384)],
            (width, 384), qkv_recv.at[pair], qkv_later.at[pair], qkv_across.at[pair], None,
            lambda k: qkv_ss.at[pair, k], lambda k: qkv_rs.at[pair, k], place,
        )

    sum_small = SmallSum(small_buf, small_recv, small_ss, small_rs, place)
    share, back_share = width // size, ff // size
    ones_rows = jnp.where(iota((16, LEN), 0) == 0, 1.0, 0.0).astype(BF16)

    @pl.loop(0, ff // 256)
    def _(index):
        rows = pl.ds(pl.multiple_of(index * 256, 256), 256)
        df = cols_b[:, 0:HEAD_DIM, 0:LEN].reshape(width, LEN)
        grad = dot_nt(jnp.concatenate([hl[rows, :], ones_rows], axis=0), df)
        shares = 256 // back_share
        for piece in range(shares):
            at = reversed_bits(index * shares + piece, size) * back_share
            gback[pl.ds(pl.multiple_of(at, back_share), back_share), :] = grad[
                piece * back_share : (piece + 1) * back_share
            ].astype(BF16)
        small_buf[0, 2:3, :] = grad[256:257]

    sum_back.start(0)

    def scatter_shares(ref, grad, first_lane):
        low = grad.astype(BF16)
        for owner in range(size):
            at = pl.multiple_of(reversed_bits(owner, size) * share, share)
            ref[pl.ds(at, share), first_lane : first_lane + grad.shape[1]] = low[
                owner * share : owner * share + share
            ]

    scatter_shares(gout, dot_nt(ot[...], da[...]), 0)
    sum_out.start(0)
    step_back = Steps(sum_back, write_back)
    step_out = Steps(sum_out, write_out)
    step_in = Steps(sum_in, write_in)

    yl_rows = jnp.concatenate([cols_a[:, 0:HEAD_DIM, 0:LEN].reshape(width, LEN), ones_rows], axis=0)
    for index in range(ff // 256):
        at = index * 256
        grad = dot_nt(yl_rows, dh[at : at + 256, :])
        scatter_shares(gin, grad[0:width], at)
        row, lane = 5 + at // width, at % width
        small_buf[0, row : row + 1, lane : lane + 256] = grad[width : width + 1]
        if index == 1:
            step_back()
        if index == 3:
            step_out()
    sum_in.start(0)

    vals, vals_up, kt, kt_up = rows_a, rows_b, cols_a, cols_b
    w3 = ot
    d3, w2 = hd.at[0, pl.ds(0, 3 * width)], hd.at[0, pl.ds(3 * width, width), pl.ds(0, 2 * width)]
    d2, dxu = hd.at[1, pl.ds(0, 2 * width)], hd.at[1, pl.ds(2 * width, width)]
    wtb[...] = transposed(eye, wk[...])
    for pair in range(4):
        lanes = slice(pair * 128, pair * 128 + 128)
        for index, ref in enumerate((wq, wk, wv)):
            w3[:, pair * 384 + index * 128 : pair * 384 + index * 128 + 128] = ref[:, lanes]
        for index, ref in enumerate((wk, wv)):
            w2[:, pair * 256 + index * 128 : pair * 256 + index * 128 + 128] = ref[:, lanes]
    clear_pads_lanes(kt)
    clear_pads_lanes(kt_up)

    @pl.loop(0, WINDOWS)
    def _(window):
        @pl.when(window == 2)
        def _():
            step_in()

        here = pl.ds(pl.multiple_of(window * QUERIES, QUERIES), QUERIES)
        padded_at = pl.multiple_of(window * QUERIES + TILE, TILE)
        low = transposed(eye, xt[:, here])
        upper = transposed(eye, xut[:, here])
        store_pairs(vals, padded_at, dot(low, wv[...]).astype(BF16))
        store_heads(kt, padded_at, dot(wtb[...], xt[:, here]).astype(BF16))
        store_pairs(vals_up, padded_at, dot(upper, wv[...]).astype(BF16))
        store_heads(kt_up, padded_at, dot(wtb[...], xut[:, here]).astype(BF16))

    blocks = PADDED // 128

    shape = (8, LEN)
    channel = (iota(shape, 1) // TILE + iota(shape, 1) % FLANK_COLS) % 3
    chosen = jnp.where(channel == iota(shape, 0), 1.0, 0.0).astype(BF16)

    def pass_over(pair, part, v_rows, k_cols):
        for window, half in items:
            e_in(pair, part, window, half).wait()
        acc[...] = jnp.zeros_like(acc)
        feats = pl.ds(pl.multiple_of(pair * 128, 128), 128)
        follow = pair + 1
        next_pair, next_part = follow % 4, jnp.minimum(part + follow // 4, 1)

        def limits(window):
            first = TILE if window == 0 else 0
            last = SPAN - TILE if window == WINDOWS - 1 else SPAN
            return first, last

        def grad_probs(window, half):
            first, last = limits(window)
            here = slice(window * QUERIES, window * QUERIES + QUERIES)
            rows = slice(window * QUERIES + first, window * QUERIES + last)
            return dot(v_rows[pair, rows, :], head_of_pair(d_o[feats, here], half))

        def add_blocks(base, window, half, value):
            first, last = limits(window)
            rows = slice(half * HEAD_DIM, half * HEAD_DIM + HEAD_DIM)
            for at in range(first, last, 128):
                acc[base + (window * QUERIES + at) // 128, rows, :] += value[
                    :, at - first : at - first + 128
                ]

        upcoming = grad_probs(*items[0])
        for index, (window, half) in enumerate(items):
            current = upcoming
            if index + 1 < len(items):
                upcoming = grad_probs(*items[index + 1])
            first, last = limits(window)
            here = slice(window * QUERIES, window * QUERIES + QUERIES)
            span = slice(window * QUERIES + first, window * QUERIES + last)
            head = 2 * pair + half
            mine = pl.ds(pl.multiple_of(pair * 128 + half * HEAD_DIM, HEAD_DIM), HEAD_DIM)
            e = e_tile(window, half, first, last)
            ds = (e.astype(F32) * (current - dd[pl.ds(head, 1), here])).astype(BF16)
            dq = dot(k_cols[head, 0:HEAD_DIM, span], ds)
            at = pl.ds(pl.multiple_of(pair * 384 + half * HEAD_DIM, HEAD_DIM), HEAD_DIM)
            if part == 0:
                d3[at, here] = dq.astype(BF16)
            else:
                d3[at, here] = ((dq + d3[at, here].astype(F32)) * 0.125).astype(BF16)
            add_blocks(0, window, half, dot_nt(qt[mine, here], ds))
            add_blocks(blocks, window, half, dot_nt(d_o[mine, here], e))
            e_in(next_pair, next_part, window, half).start()

    def take_blocks(ref, at, base):
        for block in range(1, blocks - 1):
            ref[pl.ds(at, 128), block * 128 - 128 : block * 128] = acc[base + block].astype(BF16)

    @pl.loop(0, 4)
    def _(pair):
        pass_over(pair, 0, vals_up, kt_up)
        at = pl.multiple_of(pair * 256, 256)
        take_blocks(d2, at, 0)
        take_blocks(d2, at + 128, blocks)

        @pl.when(pair == 0)
        def _():
            step_back()
            step_out()

        @pl.when(pair == 2)
        def _():
            step_back()
            step_out()
            step_in()

        @pl.when(pair == 3)
        def _():
            step_back()

    for window in range(WINDOWS):
        here = slice(window * QUERIES, window * QUERIES + QUERIES)
        dxu[:, here] = dot(w2[...], d2[:, here]).astype(BF16)

        @pl.when(band > 0)
        def _(window=window):
            halo(window).start()

    @pl.loop(0, 4)
    def _(pair):
        pass_over(pair, 1, vals, kt)

        for turn in range(4):

            @pl.when(pair == turn)
            def _(turn=turn):
                if turn == 0:
                    step_back()
                if turn < 3:
                    step_in()
                if turn > 0:
                    sum_qkv(turn - 1).advance(0)

        at = pl.multiple_of(pair * 384, 128)
        take_blocks(d3, at + 128, 0)
        take_blocks(d3, at + 256, blocks)
        grads = dot_nt(xt[...], d3[pl.ds(at, 384), :])
        grads_up = dot_nt(xut[...], d2[pl.ds(pl.multiple_of(pair * 256, 256), 256), :])
        lanes = pl.ds(pl.multiple_of(pair * 384, 128), 128)
        low_q = grads[:, 0:128].astype(BF16)
        low_kv = (grads[:, 128:384] + grads_up).astype(BF16)
        for owner in range(size):
            rows = slice(owner * share, owner * share + share)
            to = pl.ds(pl.multiple_of(qkv_at + reversed_bits(owner, size) * share, share), share)
            hd[1, to, lanes] = low_q[rows]
            hd[1, to, pl.ds(pl.multiple_of(pair * 384 + 128, 128), 256)] = low_kv[rows]
        sum_qkv(pair).start(0)
        totals[pair] = dot_nt(chosen, d3[pl.ds(at, 384), :])

    small_buf[0, 9:12, :] = dot_nt(chosen, da[...])[0:3]
    small_buf[0, 12:15, :] = dot_nt(chosen, dxu[...])[0:3] * has_up
    for block in range(12):
        row, lane = 15 + block // 4 * 3, block % 4 * 128
        small_buf[0, row : row + 3, lane : lane + 128] = totals[
            block // 3, 0:3, block % 3 * 128 : block % 3 * 128 + 128
        ]
    sum_small.start(0)
    for window, half in items:
        e_in(0, 1, window, half).wait()

    @pl.when(band == size - 1)
    def _():
        below[...] = jnp.zeros_like(below)

    for window in range(WINDOWS):
        out_copy(window).wait()

    def gt_copy(window):
        columns = pl.ds(pl.multiple_of(window * BLOCK_COLS, BLOCK_COLS), BLOCK_COLS)
        return pltpu.make_async_copy(
            side.at[:, columns, :], gt_h.at[:, columns, :], out_sem.at[window]
        )

    @pl.loop(0, WINDOWS)
    def _(window):
        @pl.when(band < size - 1)
        def _():
            halo(window).wait_recv()

        here = pl.ds(pl.multiple_of(window * QUERIES, QUERIES), QUERIES)
        dx = da[:, here].astype(F32) + dot(w3[...], d3[:, here]) + below[:, here].astype(F32)
        rows = dot_nt(eye, dx.astype(BF16)).astype(BF16)
        for half in range(2):
            at = pl.multiple_of((2 * window + half) * FLANK_COLS, FLANK_COLS)
            side[:, pl.ds(at, FLANK_COLS), :] = rows[half * TILE : half * TILE + TILE].reshape(
                BLOCK_ROWS, FLANK_COLS, -1
            )
        gt_copy(window).start()

        @pl.when(window == 0)
        def _():
            sum_qkv(0).advance(1)

        @pl.when(window == 1)
        def _():
            sum_qkv(3).advance(0)
            sum_small.advance(0)

        @pl.when(window == 2)
        def _():
            sum_qkv(1).advance(1)

        @pl.when(window == 3)
        def _():
            sum_qkv(2).advance(1)
            step_back.last()

        @pl.when(window == 4)
        def _():
            step_out.last()
            step_in.last()
            sum_qkv(0).finish(write_qkv(0))

    sum_qkv(1).finish(write_qkv(1))
    sum_qkv(3).advance(1)
    sum_small.advance(1)
    sum_qkv(2).finish(write_qkv(2))
    sum_qkv(3).finish(write_qkv(3))
    small = sum_small.finish()
    small_ref[...] = small[0:16]
    own = w3[pl.ds(pl.multiple_of(band * share, share), share), :]
    parts = jnp.concatenate([small[15:18], small[18:21], small[21:24]], axis=1)
    high = parts.astype(BF16)
    low = (parts - high.astype(F32)).astype(BF16)
    embed = dot_nt(jnp.concatenate([high, low], axis=0), own)
    rest = small[9:12] + small[12:15]
    mine = 0.0
    for owner in range(size):
        mine = mine + jnp.where(band == owner, rest[:, owner * share : owner * share + share], 0.0)
    small_ref[9:12, 0:share] = mine + embed[0:3] + embed[3:6]

    for window in range(WINDOWS):
        gt_copy(window).wait()

    @pl.when(band > 0)
    def _():
        for window in range(WINDOWS):
            halo(window).wait_send()

    @pl.when(band < size - 1)
    def _():
        for window in range(WINDOWS):
            up_copy(window).wait_send()


def emit_kernel(
    out_in, gt_in, qkv_in, gin_in, gback_in, gout_in, small_in,
    out_h, gt_h, gq, gk, gv, gout, gin, gbi, gback, gbb, gg1, gs1, gg2, gs2, gemb,
    qkv, small, large, sems, large_sems,
    *, size,
):
    pairs = (
        (small_in, small), (qkv_in, qkv), (gback_in, gback), (gin_in, gin), (gout_in, gout),
    )
    moves = []
    for index, (source, target) in enumerate(((out_in, out_h), (gt_in, gt_h))):
        for row in range(0, BLOCK_ROWS, 2):
            rows, held = pl.ds(row, 2), large.at[index, pl.ds(row, 2)]
            sem = index * 4 + row // 2
            moves.append(
                (
                    pltpu.make_async_copy(source.at[rows], held, large_sems.at[0, sem]),
                    pltpu.make_async_copy(held, target.at[rows], large_sems.at[1, sem]),
                )
            )
    for load, _ in moves:
        load.start()
    copies = [
        pltpu.make_async_copy(source, target, sems.at[index])
        for index, (source, target) in enumerate(pairs)
    ]
    for copy in copies:
        copy.start()
    for load, store in moves:
        load.wait()
        store.start()
    copies[0].wait()
    band = lax.axis_index("band")
    share, back_share = gq.shape[0], gbi.shape[0]
    mine = 0.0
    for owner in range(size):
        mine = mine + jnp.where(band == owner, small[:, owner * share : owner * share + share], 0.0)
    for row, ref in ((2, gbb), (3, gg1), (4, gs1), (0, gg2), (1, gs2)):
        ref[...] = mine[row : row + 1].reshape(-1)
    gemb[...] = small[9:12, 0:share]
    per_row = small.shape[1] // back_share
    bias = 0.0
    for owner in range(size):
        at = owner % per_row * back_share
        row = small[5 + owner // per_row : 6 + owner // per_row, at : at + back_share]
        bias = bias + jnp.where(band == owner, row, 0.0)
    gbi[...] = bias.reshape(-1)
    copies[1].wait()
    for pair in range(4):
        for index, ref in enumerate((gq, gk, gv)):
            ref[:, pair * 128 : pair * 128 + 128] = qkv[pair, :, index * 128 : index * 128 + 128]
    for copy in copies[2:]:
        copy.wait()
    for _, store in moves:
        store.wait()


def shards(
    tokens, row_place, row_width, cotangent, chan_embed, w_query, w_key, w_value, w_out, w_in,
    bias_in, w_back, bias_back, gain_first, shift_first, gain_second, shift_second,
):
    width = tokens.shape[3]
    ff = w_in.shape[1]
    tok = tokens.reshape(BLOCK_ROWS, ROW_POS, width)
    cot = cotangent.reshape(BLOCK_ROWS, ROW_POS, width)
    shape = jax.ShapeDtypeStruct
    size, groups = lax.axis_size("band"), lax.axis_size("grp")
    dma = pltpu.SemaphoreType.DMA
    share, back_share = width // size, ff // size
    stages = size // 2 + 2 * groups
    in_split = ff // groups % 128 == 0
    back_split = width // groups % 128 == 0
    rows = shape((BLOCK_ROWS, ROW_POS, width), BF16)

    def later(split, total_rows, columns):
        return pltpu.VMEM((total_rows // 2, columns // groups if split else columns), BF16)

    def across(split, total_rows, columns):
        if split:
            return pltpu.VMEM((groups - 1, total_rows // 2, columns // groups), BF16)
        return pltpu.VMEM((groups, total_rows // size, columns), BF16)

    flat = pltpu.VMEM((width, LEN), BF16)
    out, gt, _, qkv, gin, gback, gout, small = pl.pallas_call(
        functools.partial(
            layer_kernel, size=size, groups=groups, in_split=in_split, back_split=back_split
        ),
        name="layer_forward_and_back",
        out_shape=(
            rows,
            rows,
            shape((WINDOWS, 2, 2 * SPAN, 4 * QUERIES), BF16),
            shape((4, share, 384), F32),
            shape((share, ff), F32),
            shape((back_share, width), F32),
            shape((share, width), F32),
            shape((16, width), F32),
        ),
        in_specs=[smem()] * 2 + [vmem()] * 7 + [hbm()] * 8,
        out_specs=(hbm(),) * 3 + (vmem(),) * 5,
        scratch_shapes=[
            pltpu.VMEM(rows.shape, BF16),
            pltpu.VMEM(rows.shape, BF16),
            pltpu.VMEM((4, width, width), BF16),
            pltpu.VMEM((width, width), BF16),
            pltpu.VMEM((width, width), BF16),
            pltpu.VMEM((2, ff, width), BF16),
            pltpu.VMEM((2, width, ff), BF16),
            flat,
            flat,
            flat,
            flat,
            flat,
            pltpu.VMEM((4, PADDED, 128), BF16),
            pltpu.VMEM((4, PADDED, 128), BF16),
            pltpu.VMEM((8, HEAD_DIM + 16, PADDED), BF16),
            pltpu.VMEM((8, HEAD_DIM + 16, PADDED), BF16),
            pltpu.VMEM((2, ff, LEN), BF16),
            pltpu.VMEM((SPAN, QUERIES), F32),
            pltpu.VMEM((SPAN, 128), BF16),
            pltpu.VMEM((128, QUERIES), BF16),
            pltpu.VMEM((ROW_POS, width), BF16),
            pltpu.VMEM((5, width, 128), BF16),
            pltpu.VMEM((ff, 128), BF16),
            pltpu.VMEM((width, QUERIES), F32),
            flat,
            pltpu.VMEM((2 * PADDED // 128, 128, 128), F32),
            flat,
            pltpu.VMEM((8, LEN), F32),
            pltpu.VMEM((8, LEN), F32),
            pltpu.VMEM((width // 2, ff), BF16),
            later(in_split, width, ff),
            across(in_split, width, ff),
            pltpu.VMEM((groups, share, ff // groups), F32),
            pltpu.VMEM((ff // 2, width), BF16),
            later(back_split, ff, width),
            across(back_split, ff, width),
            pltpu.VMEM((groups, back_share, width // groups), F32),
            pltpu.VMEM((width // 2, width), BF16),
            pltpu.VMEM((width // 2, width), BF16),
            pltpu.VMEM((groups, share, width), BF16),
            pltpu.VMEM((4, width // 2, 384), BF16),
            pltpu.VMEM((4, width // 2, 384), BF16),
            pltpu.VMEM((4, groups, share, 384), BF16),
            pltpu.VMEM((3, 24, width), F32),
            pltpu.VMEM((size // 2 + groups - 1, 24, width), F32),
            pltpu.VMEM((4, 8, 384), F32),
            dma((8,)),
            dma((2, 2)),
            dma((WINDOWS, 2)),
            dma((WINDOWS,)),
            dma((WINDOWS,)),
            dma((WINDOWS,)),
            dma((WINDOWS,)),
            dma((WINDOWS,)),
            dma((stages,)),
            dma((stages,)),
            dma((stages,)),
            dma((stages,)),
            dma((stages,)),
            dma((stages,)),
            dma((4, stages)),
            dma((4, stages)),
            dma((stages,)),
            dma((stages,)),
        ],
        compiler_params=pltpu.CompilerParams(
            vmem_limit_bytes=LIMIT, collective_id=0, has_side_effects=True
        ),
    )(
        row_place, row_width, chan_embed, bias_in, bias_back, gain_first, shift_first, gain_second,
        shift_second, tok, cot, w_query, w_key, w_value, w_out, w_in, w_back,
    )
    vector = shape((share,), F32)
    square = shape((share, width), F32)
    out, gt, gq, gk, gv, gout, gin, gbi, gback, gbb, gg1, gs1, gg2, gs2, gemb = pl.pallas_call(
        functools.partial(emit_kernel, size=size),
        name="emit_shares",
        out_shape=(
            rows, rows, square, square, square, square, shape((share, ff), F32),
            shape((back_share,), F32), shape((back_share, width), F32),
            vector, vector, vector, vector, vector, shape((3, share), F32),
        ),
        in_specs=[hbm()] * 7,
        out_specs=(hbm(),) * 2 + (vmem(),) * 3 + (vmem(), vmem(), vmem(), vmem()) + (vmem(),) * 6,
        scratch_shapes=[
            pltpu.VMEM((4, share, 384), F32),
            pltpu.VMEM((16, width), F32),
            pltpu.VMEM((2,) + rows.shape, BF16),
            dma((5,)),
            dma((2, 8)),
        ],
        compiler_params=pltpu.CompilerParams(vmem_limit_bytes=LIMIT),
    )(out, gt, qkv, gin, gback, gout, small)
    return (
        out.reshape(tokens.shape),
        gt.reshape(tokens.shape),
        gq, gk, gv, gout, gin, gbi, gback, gbb, gg1, gs1, gg2, gs2, gemb,
    )


def solution(mesh):
    tall = P("grp", "band", None, None)
    return jax.shard_map(
        shards,
        mesh=mesh,
        in_specs=(tall, P("grp", "band"), P("grp", "band"), tall) + (P(),) * 13,
        out_specs=(tall, tall)
        + (P("band", None),) * 5
        + (P("band"), P("band", None))
        + (P("band"),) * 5
        + (P(None, "band"),),
        check_vma=False,
    )
```

time: 197 us -> 175 us (0.89)
  Pallas kernels: 186 us -> 172 us
  local copies, waits for them, and re-layouts: 7.81 us -> 0 us
    pallas_call x3 -> x1, Pallas kernels: 186 us -> 168 us  [shards(): pl.pallas_call(functools.partial(layer_kernel, size=size, groups=groups,...]
    unnamed x26 -> x0, local copies, waits for them, and re-layouts: 7.18 us -> none
    pallas_call x1, Pallas kernels: 0.92 us -> 4.3 us  [shards(): pl.pallas_call(functools.partial(emit_kernel, size=size), name='emit_shar...]
where the time goes in v4:
time: 175 us; the launch traced here: 174 us
  Pallas kernels  172 us (98%)
  between operations  2.13 us (1%)
    pallas_call x1, Pallas kernels, shards(): pl.pallas_call(functools.partial(layer_kernel, size=size, groups=groups,...  168 us
    pallas_call x1, Pallas kernels, shards(): pl.pallas_call(functools.partial(emit_kernel, size=size), name='emit_shar...  4.3 us

profile of v4, /device:TPU:0, one launch (start us, length us, event | category | flops | bytes accessed | tf_op | source)
XLA Modules:
  0.0 174.2 jit_solution(17793645994739053124)
XLA Ops:
  1.9 167.7 %layer_forward_and_back.1 = (bf16[8,192,512]{2,1,0:T(8,128)(2,1)}, bf16[8,192,512]{2,1,0:T(8,128)(2,1)}, bf16[6,2,1024,1024]{3,2,1,0:T(8,128)(2,1)}, f32[4,32,38...) custom-call(s32[1,1]{1,0:T(1,128)S(6)} %copy.32.place_ref, ...), custom_call_target="tpu_custom_call" | custom-call | tf_op jit(solution)/shard_map/layer_forward_and_back/pallas_call | solution.py:1145
  169.7 4.3 %emit_shares.1 = (bf16[8,192,512]{2,1,0:T(8,128)(2,1)}, bf16[8,192,512]{2,1,0:T(8,128)(2,1)}, f32[32,512]{1,0:T(8,128)}, f32[32,512]{1,0:T(8,128)}, f32[32,512]{...) custom-call(bf16[8,192,512]{2,1,0:T(8,128)(2,1)} %get-tuple-element., ...), custom_call_target="tpu_custom_call" | custom-call | tf_op jit(solution)/shard_map/emit_shares/pallas_call | solution.py:1237

commit v5 on v4

--- a/solution.py
+++ b/solution.py
@@ -91,7 +91,7 @@
 def embed_window(embed_rows, window):
     parts = []
     for half in range(2):
-        at = pl.multiple_of((2 * window + half) * FLANK_COLS, FLANK_COLS)
+        at = pl.multiple_of((2 * window + half) % 3 * FLANK_COLS, FLANK_COLS)
         part = embed_rows[pl.ds(at, FLANK_COLS), :][None]
         parts.append(jnp.broadcast_to(part, (BLOCK_ROWS,) + part.shape[1:]).reshape(TILE, -1))
     return jnp.concatenate(parts, axis=0)
@@ -161,20 +161,25 @@
 
 
 class Reduction:
-    def __init__(self, buf, shape, recv, later, across, gathered, send_sem, recv_sem, place):
+    def __init__(
+        self, buf, shape, recv, later, across, gathered, send_sem, recv_sem, place, direct=False
+    ):
         self.buf, self.recv, self.later = buf, recv, later
         self.across, self.gathered = across, gathered
         self.send_sem, self.recv_sem = send_sem, recv_sem
         self.band, self.grp, self.size, self.groups = place
         self.depth = depth = levels(self.size)
         self.rows = shape[0] // self.size
+        halvings = [("halve", bit) for bit in range(1, depth)]
         self.stages = [("halve", 0)]
-        if gathered is None:
+        if gathered is not None:
+            self.stages += [("split", 1)] + halvings + [("gather", depth)]
+        elif direct:
             self.stages += [("direct", 1), ("sum", depth)]
         else:
-            self.stages += [("split", 1)] + [("halve", bit) for bit in range(1, depth)]
-            self.stages += [("gather", depth)]
+            self.stages += halvings + [("sum", depth)]
         self.part = shape[1] // self.groups
+        self.dtype = buf.dtype
 
     def start_of(self, bits):
         return first_share(self.band, bits, self.size)
@@ -258,13 +263,13 @@
                 mine = self.shares(keep + index)
                 total = self.buf[mine, columns].astype(F32)
                 total = total + self.landing(bits)[self.landing_rows(bits, index, 1), :].astype(F32)
-                self.buf[mine, columns] = total.astype(BF16)
+                self.buf[mine, columns] = total.astype(self.dtype)
         elif kind == "direct":
             mine = self.shares(self.start_of(self.depth))
             total = self.buf[mine, :].astype(F32)
             for step in range(1, self.size // 2):
                 total = total + self.later[step * self.rows : (step + 1) * self.rows, :].astype(F32)
-            self.buf[mine, :] = total.astype(BF16)
+            self.buf[mine, :] = total.astype(self.dtype)
         else:
             columns = self.columns_of(self.grp)
             keep = self.start_of(bits)
@@ -275,7 +280,7 @@
                 total = self.buf[mine, columns].astype(F32)
                 for step in range(self.groups - 1):
                     total = total + self.across[step, self.shares(index), :].astype(F32)
-                self.buf[mine, columns] = total.astype(BF16)
+                self.buf[mine, columns] = total.astype(self.dtype)
 
         if self.stages[stage + 1][0] == "gather":
             mine = self.shares(self.start_of(self.depth))
@@ -299,61 +304,6 @@
                 out(self.gathered[step], self.columns_of(member))
 
 
-class SmallSum:
-    def __init__(self, buf, recv, send_sem, recv_sem, place):
-        self.buf, self.recv, self.send_sem, self.recv_sem = buf, recv, send_sem, recv_sem
-        self.band, self.grp, self.size, self.groups = place
-
-    def copies(self, stage):
-        half = self.size // 2
-        if stage == 0:
-            partners = [(0, (self.band + 1 - 2 * (self.band % 2), self.grp))]
-        elif stage == 1:
-            partners = [
-                (step, ((self.band + 2 * step) % self.size, self.grp)) for step in range(1, half)
-            ]
-        else:
-            partners = [
-                (half + step - 1, (self.band, (self.grp + step) % self.groups))
-                for step in range(1, self.groups)
-            ]
-        return [
-            pltpu.make_async_remote_copy(
-                src_ref=self.buf.at[stage],
-                dst_ref=self.recv.at[slot],
-                send_sem=self.send_sem.at[slot],
-                recv_sem=self.recv_sem.at[slot],
-                device_id=partner,
-                device_id_type=pl.DeviceIdType.MESH,
-            )
-            for slot, partner in partners
-        ]
-
-    def start(self, stage):
-        for copy in self.copies(stage):
-            copy.start()
-
-    def advance(self, stage):
-        for copy in self.copies(stage):
-            copy.wait()
-        total = self.buf[stage]
-        for slot in (0,) if stage == 0 else range(1, self.size // 2):
-            total = total + self.recv[slot]
-        self.buf[stage + 1] = total
-        self.start(stage + 1)
-
-    def finish(self):
-        for copy in self.copies(2):
-            copy.wait()
-        mine = self.buf[2]
-        total = 0.0
-        for member in range(self.groups):
-            step = (self.grp + self.groups - member) % self.groups
-            slot = jnp.where(step == 0, 0, self.size // 2 + step - 1)
-            total = total + jnp.where(step == 0, mine, self.recv[slot])
-        return total
-
-
 def store_pairs(ref, at, value):
     for pair in range(value.shape[1] // 128):
         ref[pair, pl.ds(at, value.shape[0]), :] = value[:, pair * 128 : (pair + 1) * 128]
@@ -398,11 +348,11 @@
     place_ref, width_ref, embed_ref, bi_ref, bb_ref, g1_ref, s1_ref, g2_ref, s2_ref, tok_h, cot_h, wq_h, wk_h, wv_h, wo_h, wi_h, wb_h,
     out_h, gt_h, e_h, qkv_ref, gin_ref, gback_ref, gout_ref, small_ref,
     tok, side, w4, wta, wtb, ww, wt, xt, xut, qt, ot, da, rows_a, rows_b, cols_a, cols_b, hd,
-    bias_low, bias_up, ones_row, embed_rows, cols, bi_col, n1_buf, d_o, acc, below,
+    bias_low, embed_rows, cols, bi_col, n1_buf, inv_buf, d_o, acc, below,
     inv, dd,
     in_recv, in_later, in_across, in_parts, back_recv, back_later, back_across, back_parts,
     out_recv, out_later, out_across,
-    qkv_recv, qkv_later, qkv_across, small_buf, small_recv, totals,
+    qkv_recv, qkv_later, qkv_across, small, small_buf, small_recv, small_later, small_across, embed_sum,
     load_sem, e_out_sem, e_in_sem, out_sem, up_ss, up_rs, halo_ss, halo_rs,
     in_ss, in_rs, back_ss, back_rs, go_ss, go_rs, qkv_ss, qkv_rs, small_ss, small_rs,
     *, size, groups, in_split, back_split,
@@ -470,6 +420,7 @@
         side[...] = jnp.zeros_like(side)
 
     keys, keys_up, vt, vt_up, qs = rows_a, rows_b, cols_a, cols_b, da
+    bias_up, ones_row = d_o.at[:, pl.ds(0, 128)], d_o.at[pl.ds(0, 128), pl.ds(128, QUERIES)]
     eye = identity(256)
     fill_embed(embed_ref, embed_rows)
     clear_pads_rows(keys)
@@ -612,6 +563,7 @@
             e_out(window, half).wait()
     loads[7].wait()
     hl, dh = hd.at[0], hd.at[1]
+    dr2_buf = bias_low
     heads = width // HEAD_DIM
 
     def broadcast(index):
@@ -630,9 +582,10 @@
     part = 256
     parts = [slice(at, at + part) for at in range(0, ff, part)]
 
-    @pl.loop(0, WINDOWS)
-    def _(window):
-        here = pl.ds(pl.multiple_of(window * QUERIES, QUERIES), QUERIES)
+    def columns_at(window):
+        return pl.ds(pl.multiple_of(window * QUERIES, QUERIES), QUERIES)
+
+    def forward_start(window):
         raw = raw_window(tok, window)
         embed = embed_window(embed_rows, window)
         start = jnp.concatenate(
@@ -643,23 +596,23 @@
             ],
             axis=0,
         )
+        here = columns_at(window)
         n1, inv1 = norm_stats(start + dot(wta[...], ot[:, here]))
-        y1 = n1 * broadcast(1) + broadcast(2)
-        low = y1.astype(BF16)
-        n1_buf[...] = n1
+        low = (n1 * broadcast(1) + broadcast(2)).astype(BF16)
+        n1_buf[window % 2] = n1.astype(BF16)
+        inv_buf[window % 2, 0:1, :] = inv1
         cols_a[:, 0:HEAD_DIM, here] = low.reshape(heads, HEAD_DIM, QUERIES)
-
-        upcoming = dot(wit[parts[0], :], low)
-        for index, rows in enumerate(parts):
-            u = upcoming + wide(bi_col[rows, :].astype(F32))
-            if index + 1 < len(parts):
-                upcoming = dot(wit[parts[index + 1], :], low)
-            active, slope = gelu_and_slope(u)
-            hl[rows, here] = active.astype(BF16)
-            dh[rows, here] = slope.astype(BF16)
-
-        f = dot(wbt[...], hl[:, here]) + broadcast(0)
-        n2, inv2 = norm_stats(n1_buf[...] * broadcast(1) + broadcast(2) + f)
+        return low
+
+    def activate(window, index, product):
+        u = product + wide(bi_col[parts[index], :].astype(F32))
+        active, slope = gelu_and_slope(u)
+        hl[parts[index], columns_at(window)] = active.astype(BF16)
+        dh[parts[index], columns_at(window)] = slope.astype(BF16)
+
+    def forward_end(window, f):
+        y1 = n1_buf[window % 2].astype(F32) * broadcast(1) + broadcast(2)
+        n2, inv2 = norm_stats(y1 + f + broadcast(0))
         g2 = broadcast(3)
         result = (n2 * g2 + broadcast(4)).astype(BF16)
         result = dot_nt(eye, result).astype(BF16)
@@ -675,21 +628,26 @@
         gather(0, cot * n2)
         gather(1, cot)
         dr2 = norm_back(n2, inv2, cot, g2)
-        df_low = dr2.astype(BF16)
-        cols_b[:, 0:HEAD_DIM, here] = df_low.reshape(heads, HEAD_DIM, QUERIES)
-
-        upcoming = dot(wb[parts[0], :], df_low)
-        for index, rows in enumerate(parts):
-            current = upcoming
-            if index + 1 < len(parts):
-                upcoming = dot(wb[parts[index + 1], :], df_low)
-            dh[rows, here] = (current * dh[rows, here].astype(F32)).astype(BF16)
-
-        dy1 = dr2 + dot(wi[...], dh[:, here])
-        n1 = n1_buf[...]
+        dr2_buf[...] = dr2
+        cols_b[:, 0:HEAD_DIM, columns_at(window)] = dr2.astype(BF16).reshape(
+            heads, HEAD_DIM, QUERIES
+        )
+
+    def back_hidden(window, index, df_low):
+        here = columns_at(window)
+        slope = dh[parts[index], here].astype(F32)
+        dh[parts[index], here] = (dot(wb[parts[index], :], df_low) * slope).astype(BF16)
+
+    def back_input(window, quarter):
+        rows = slice(quarter * ff // 4, (quarter + 1) * ff // 4)
+        return dot(wi[:, rows], dh[rows, columns_at(window)])
+
+    def back_end(window, dy1):
+        here = columns_at(window)
+        n1 = n1_buf[window % 2].astype(F32)
         gather(2, dy1 * n1)
         gather(3, dy1)
-        dr1 = norm_back(n1, inv1, dy1, broadcast(1))
+        dr1 = norm_back(n1, inv_buf[window % 2, 0:1, :], dy1, broadcast(1))
         da_low = dr1.astype(BF16)
         da[:, here] = da_low
         grad_o = dot(wo[...], da_low)
@@ -699,15 +657,55 @@
             inverse = inv[head : head + 1, here]
             d_o[rows, here] = (grad_o[rows] * inverse).astype(BF16)
             dd[head : head + 1, here] = jnp.sum(product[rows], axis=0, keepdims=True) * inverse
-        out_copy(window).start()
-
-    small_buf[0] = jnp.zeros(small_buf.shape[1:], F32)
+
+    def step(back, ahead):
+        df_low, dy1 = None, None
+        if back is not None:
+            df_low = cols_b[:, 0:HEAD_DIM, columns_at(back)].reshape(width, QUERIES)
+            dy1 = dr2_buf[...]
+            for index in range(2):
+                back_hidden(back, index, df_low)
+        if ahead is not None:
+            low = forward_start(ahead)
+            upcoming = dot(wit[parts[0], :], low)
+        for index in range(len(parts)):
+            if ahead is not None:
+                current = upcoming
+                if index + 1 < len(parts):
+                    upcoming = dot(wit[parts[index + 1], :], low)
+            if back is not None:
+                if index < 3:
+                    back_hidden(back, 2 * index + 2, df_low)
+                    back_hidden(back, 2 * index + 3, df_low)
+                elif index < 7:
+                    dy1 = dy1 + back_input(back, index - 3)
+            if ahead is not None:
+                activate(ahead, index, current)
+        if ahead is not None:
+            f = dot(wbt[...], hl[:, columns_at(ahead)])
+        if back is not None:
+            back_end(back, dy1)
+        if ahead is not None:
+            forward_end(ahead, f)
+            out_copy(ahead).start()
+
+    assert len(parts) == 8
+    step(None, 0)
+
+    @pl.loop(0, WINDOWS - 1)
+    def _(window):
+        step(window, window + 1)
+
+    step(WINDOWS - 1, None)
+
+    small[...] = jnp.zeros_like(small)
+    small_buf[...] = jnp.zeros_like(small_buf)
     ones = jnp.ones((8, 256), BF16)
     for index, row in enumerate((0, 1, 3, 4)):
         value = acc[pl.ds(index * width // 128, width // 128)].reshape(width, 128)
         high = value.astype(BF16)
         split = jnp.concatenate([high, (value - high.astype(F32)).astype(BF16)], axis=1)
-        small_buf[0, row : row + 1, :] = dot_nt(ones, split)[0:1]
+        small[row : row + 1, :] = dot_nt(ones, split)[0:1]
 
     def e_in(pair, part, window, half):
         if window < 4:
@@ -765,25 +763,30 @@
         return Reduction(
             hd.at[1, pl.ds(qkv_at, width), pl.ds(pl.multiple_of(pair * 384, 128), 384)],
             (width, 384), qkv_recv.at[pair], qkv_later.at[pair], qkv_across.at[pair], None,
-            lambda k: qkv_ss.at[pair, k], lambda k: qkv_rs.at[pair, k], place,
+            lambda k: qkv_ss.at[pair, k], lambda k: qkv_rs.at[pair, k], place, True,
         )
 
-    sum_small = SmallSum(small_buf, small_recv, small_ss, small_rs, place)
+    sum_small = Reduction(
+        small_buf, (16 * size, 128), small_recv, small_later, small_across, None,
+        lambda k: small_ss.at[k], lambda k: small_rs.at[k], place, True,
+    )
     share, back_share = width // size, ff // size
     ones_rows = jnp.where(iota((16, LEN), 0) == 0, 1.0, 0.0).astype(BF16)
 
-    @pl.loop(0, ff // 256)
+    tall = 512
+
+    @pl.loop(0, ff // tall)
     def _(index):
-        rows = pl.ds(pl.multiple_of(index * 256, 256), 256)
+        rows = pl.ds(pl.multiple_of(index * tall, tall), tall)
         df = cols_b[:, 0:HEAD_DIM, 0:LEN].reshape(width, LEN)
         grad = dot_nt(jnp.concatenate([hl[rows, :], ones_rows], axis=0), df)
-        shares = 256 // back_share
+        shares = tall // back_share
         for piece in range(shares):
             at = reversed_bits(index * shares + piece, size) * back_share
             gback[pl.ds(pl.multiple_of(at, back_share), back_share), :] = grad[
                 piece * back_share : (piece + 1) * back_share
             ].astype(BF16)
-        small_buf[0, 2:3, :] = grad[256:257]
+        small[2:3, :] = grad[tall : tall + 1]
 
     sum_back.start(0)
 
@@ -807,7 +810,7 @@
         grad = dot_nt(yl_rows, dh[at : at + 256, :])
         scatter_shares(gin, grad[0:width], at)
         row, lane = 5 + at // width, at % width
-        small_buf[0, row : row + 1, lane : lane + 256] = grad[width : width + 1]
+        small[row : row + 1, lane : lane + 256] = grad[width : width + 1]
         if index == 1:
             step_back()
         if index == 3:
@@ -852,7 +855,6 @@
     def pass_over(pair, part, v_rows, k_cols):
         for window, half in items:
             e_in(pair, part, window, half).wait()
-        acc[...] = jnp.zeros_like(acc)
         feats = pl.ds(pl.multiple_of(pair * 128, 128), 128)
         follow = pair + 1
         next_pair, next_part = follow % 4, jnp.minimum(part + follow // 4, 1)
@@ -872,9 +874,11 @@
             first, last = limits(window)
             rows = slice(half * HEAD_DIM, half * HEAD_DIM + HEAD_DIM)
             for at in range(first, last, 128):
-                acc[base + (window * QUERIES + at) // 128, rows, :] += value[
-                    :, at - first : at - first + 128
-                ]
+                block = (window * QUERIES + at) // 128
+                piece = value[:, at - first : at - first + 128]
+                if window > 0 and at < SPAN - QUERIES:
+                    piece = piece + acc[base + block, rows, :]
+                acc[base + block, rows, :] = piece
 
         upcoming = grad_probs(*items[0])
         for index, (window, half) in enumerate(items):
@@ -923,14 +927,21 @@
         @pl.when(pair == 3)
         def _():
             step_back()
+            step_out()
+
+    def send_halo(window):
+        @pl.when(band > 0)
+        def _():
+            halo(window).start()
 
     for window in range(WINDOWS):
         here = slice(window * QUERIES, window * QUERIES + QUERIES)
         dxu[:, here] = dot(w2[...], d2[:, here]).astype(BF16)
-
-        @pl.when(band > 0)
-        def _(window=window):
-            halo(window).start()
+        if window < 2:
+            send_halo(window)
+
+    embed_sum[0:8, :] = dot_nt(chosen, da[...]) + dot_nt(chosen, dxu[...]) * has_up
+    embed_sum[8:16, :] = jnp.zeros((8, width), F32)
 
     @pl.loop(0, 4)
     def _(pair):
@@ -946,6 +957,9 @@
                     step_in()
                 if turn > 0:
                     sum_qkv(turn - 1).advance(0)
+                if turn < 2:
+                    send_halo(2 * turn + 2)
+                    send_halo(2 * turn + 3)
 
         at = pl.multiple_of(pair * 384, 128)
         take_blocks(d3, at + 128, 0)
@@ -961,15 +975,19 @@
             hd[1, to, lanes] = low_q[rows]
             hd[1, to, pl.ds(pl.multiple_of(pair * 384 + 128, 128), 256)] = low_kv[rows]
         sum_qkv(pair).start(0)
-        totals[pair] = dot_nt(chosen, d3[pl.ds(at, 384), :])
-
-    small_buf[0, 9:12, :] = dot_nt(chosen, da[...])[0:3]
-    small_buf[0, 12:15, :] = dot_nt(chosen, dxu[...])[0:3] * has_up
-    for block in range(12):
-        row, lane = 15 + block // 4 * 3, block % 4 * 128
-        small_buf[0, row : row + 3, lane : lane + 128] = totals[
-            block // 3, 0:3, block % 3 * 128 : block % 3 * 128 + 128
-        ]
+        totals = dot_nt(chosen, d3[pl.ds(at, 384), :])
+        high = totals.astype(BF16)
+        low = (totals - high.astype(F32)).astype(BF16)
+        embed_sum[...] += dot_nt(
+            jnp.concatenate([high, low], axis=0), w3[:, pl.ds(pl.multiple_of(pair * 384, 128), 384)]
+        )
+
+    rows = jnp.concatenate([small[0:8], embed_sum[0:8] + embed_sum[8:16]], axis=0)
+    for owner in range(size):
+        at = pl.multiple_of(reversed_bits(owner, size) * 16, 16)
+        small_buf[pl.ds(at, 16), 0:share] = rows[:, owner * share : owner * share + share]
+        row, lane = 5 + owner * back_share // width, owner * back_share % width
+        small_buf[pl.ds(at + 5, 1), 0:back_share] = small[row : row + 1, lane : lane + back_share]
     sum_small.start(0)
     for window, half in items:
         e_in(0, 1, window, half).wait()
@@ -1015,35 +1033,28 @@
         @pl.when(window == 2)
         def _():
             sum_qkv(1).advance(1)
+            step_back.last()
 
         @pl.when(window == 3)
         def _():
+            step_in.last()
+
+        @pl.when(window == 4)
+        def _():
+            step_out.last()
             sum_qkv(2).advance(1)
-            step_back.last()
-
-        @pl.when(window == 4)
-        def _():
-            step_out.last()
-            step_in.last()
             sum_qkv(0).finish(write_qkv(0))
 
-    sum_qkv(1).finish(write_qkv(1))
     sum_qkv(3).advance(1)
     sum_small.advance(1)
+    sum_qkv(1).finish(write_qkv(1))
     sum_qkv(2).finish(write_qkv(2))
+
+    def write_small(value):
+        small_ref[...] = value
+
     sum_qkv(3).finish(write_qkv(3))
-    small = sum_small.finish()
-    small_ref[...] = small[0:16]
-    own = w3[pl.ds(pl.multiple_of(band * share, share), share), :]
-    parts = jnp.concatenate([small[15:18], small[18:21], small[21:24]], axis=1)
-    high = parts.astype(BF16)
-    low = (parts - high.astype(F32)).astype(BF16)
-    embed = dot_nt(jnp.concatenate([high, low], axis=0), own)
-    rest = small[9:12] + small[12:15]
-    mine = 0.0
-    for owner in range(size):
-        mine = mine + jnp.where(band == owner, rest[:, owner * share : owner * share + share], 0.0)
-    small_ref[9:12, 0:share] = mine + embed[0:3] + embed[3:6]
+    sum_small.finish(write_small)
 
     for window in range(WINDOWS):
         gt_copy(window).wait()
@@ -1063,7 +1074,6 @@
     out_in, gt_in, qkv_in, gin_in, gback_in, gout_in, small_in,
     out_h, gt_h, gq, gk, gv, gout, gin, gbi, gback, gbb, gg1, gs1, gg2, gs2, gemb,
     qkv, small, large, sems, large_sems,
-    *, size,
 ):
     pairs = (
         (small_in, small), (qkv_in, qkv), (gback_in, gback), (gin_in, gin), (gout_in, gout),
@@ -1091,21 +1101,11 @@
         load.wait()
         store.start()
     copies[0].wait()
-    band = lax.axis_index("band")
     share, back_share = gq.shape[0], gbi.shape[0]
-    mine = 0.0
-    for owner in range(size):
-        mine = mine + jnp.where(band == owner, small[:, owner * share : owner * share + share], 0.0)
     for row, ref in ((2, gbb), (3, gg1), (4, gs1), (0, gg2), (1, gs2)):
-        ref[...] = mine[row : row + 1].reshape(-1)
-    gemb[...] = small[9:12, 0:share]
-    per_row = small.shape[1] // back_share
-    bias = 0.0
-    for owner in range(size):
-        at = owner % per_row * back_share
-        row = small[5 + owner // per_row : 6 + owner // per_row, at : at + back_share]
-        bias = bias + jnp.where(band == owner, row, 0.0)
-    gbi[...] = bias.reshape(-1)
+        ref[...] = small[row : row + 1, 0:share].reshape(-1)
+    gemb[...] = small[8:11, 0:share]
+    gbi[...] = small[5:6, 0:back_share].reshape(-1)
     copies[1].wait()
     for pair in range(4):
         for index, ref in enumerate((gq, gk, gv)):
@@ -1155,7 +1155,7 @@
             shape((share, ff), F32),
             shape((back_share, width), F32),
             shape((share, width), F32),
-            shape((16, width), F32),
+            shape((16, 128), F32),
         ),
         in_specs=[smem()] * 2 + [vmem()] * 7 + [hbm()] * 8,
         out_specs=(hbm(),) * 3 + (vmem(),) * 5,
@@ -1178,12 +1178,11 @@
             pltpu.VMEM((8, HEAD_DIM + 16, PADDED), BF16),
             pltpu.VMEM((2, ff, LEN), BF16),
             pltpu.VMEM((SPAN, QUERIES), F32),
-            pltpu.VMEM((SPAN, 128), BF16),
-            pltpu.VMEM((128, QUERIES), BF16),
-            pltpu.VMEM((ROW_POS, width), BF16),
+            pltpu.VMEM((3 * FLANK_COLS, width), BF16),
             pltpu.VMEM((5, width, 128), BF16),
             pltpu.VMEM((ff, 128), BF16),
-            pltpu.VMEM((width, QUERIES), F32),
+            pltpu.VMEM((2, width, QUERIES), BF16),
+            pltpu.VMEM((2, 8, QUERIES), F32),
             flat,
             pltpu.VMEM((2 * PADDED // 128, 128, 128), F32),
             flat,
@@ -1203,9 +1202,12 @@
             pltpu.VMEM((4, width // 2, 384), BF16),
             pltpu.VMEM((4, width // 2, 384), BF16),
             pltpu.VMEM((4, groups, share, 384), BF16),
-            pltpu.VMEM((3, 24, width), F32),
-            pltpu.VMEM((size // 2 + groups - 1, 24, width), F32),
-            pltpu.VMEM((4, 8, 384), F32),
+            pltpu.VMEM((16, width), F32),
+            pltpu.VMEM((16 * size, 128), F32),
+            pltpu.VMEM((8 * size, 128), F32),
+            pltpu.VMEM((8 * size, 128), F32),
+            pltpu.VMEM((groups, 16, 128), F32),
+            pltpu.VMEM((16, width), F32),
             dma((8,)),
             dma((2, 2)),
             dma((WINDOWS, 2)),
@@ -1235,7 +1237,7 @@
     vector = shape((share,), F32)
     square = shape((share, width), F32)
     out, gt, gq, gk, gv, gout, gin, gbi, gback, gbb, gg1, gs1, gg2, gs2, gemb = pl.pallas_call(
-        functools.partial(emit_kernel, size=size),
+        emit_kernel,
         name="emit_shares",
         out_shape=(
             rows, rows, square, square, square, square, shape((share, ff), F32),
@@ -1246,7 +1248,7 @@
         out_specs=(hbm(),) * 2 + (vmem(),) * 3 + (vmem(), vmem(), vmem(), vmem()) + (vmem(),) * 6,
         scratch_shapes=[
             pltpu.VMEM((4, share, 384), F32),
-            pltpu.VMEM((16, width), F32),
+            pltpu.VMEM((16, 128), F32),
             pltpu.VMEM((2,) + rows.shape, BF16),
             dma((5,)),
             dma((2, 8)),

time: 175 us -> 159 us (0.909)
  Pallas kernels: 172 us -> 157 us
    pallas_call x1, Pallas kernels: 168 us -> 153 us  [shards(): pl.pallas_call(functools.partial(layer_kernel, size=size, groups=groups,...]
where the time goes in v5:
time: 159 us
  Pallas kernels  157 us (99%)
  between operations  2.13 us (1%)
    pallas_call x1, Pallas kernels, shards(): pl.pallas_call(functools.partial(layer_kernel, size=size, groups=groups,...  153 us
    pallas_call x1, Pallas kernels, shards(): pl.pallas_call(emit_kernel, name='emit_shares', out_shape=(rows, rows, sq...  4.3 us

profile of v5, /device:TPU:0, one launch (start us, length us, event | category | flops | bytes accessed | tf_op | source)
XLA Modules:
  0.0 159.2 jit_solution(278831643508899542)
XLA Ops:
  1.9 152.8 %layer_forward_and_back.1 = (bf16[8,192,512]{2,1,0:T(8,128)(2,1)}, bf16[8,192,512]{2,1,0:T(8,128)(2,1)}, bf16[6,2,1024,1024]{3,2,1,0:T(8,128)(2,1)}, f32[4,32,38...) custom-call(s32[1,1]{1,0:T(1,128)S(6)} %copy.32.place_ref, ...), custom_call_target="tpu_custom_call" | custom-call | tf_op jit(solution)/shard_map/layer_forward_and_back/pallas_call | solution.py:1145
  154.7 4.3 %emit_shares.1 = (bf16[8,192,512]{2,1,0:T(8,128)(2,1)}, bf16[8,192,512]{2,1,0:T(8,128)(2,1)}, f32[32,512]{1,0:T(8,128)}, f32[32,512]{1,0:T(8,128)}, f32[32,512]{...) custom-call(bf16[8,192,512]{2,1,0:T(8,128)(2,1)} %get-tuple-element., ...), custom_call_target="tpu_custom_call" | custom-call | tf_op jit(solution)/shard_map/emit_shares/pallas_call | solution.py:1239

commit v6 on v5

--- a/solution.py
+++ b/solution.py
@@ -162,7 +162,8 @@
 
 class Reduction:
     def __init__(
-        self, buf, shape, recv, later, across, gathered, send_sem, recv_sem, place, direct=False
+        self, buf, shape, recv, later, across, gathered, send_sem, recv_sem, place, direct=False,
+        late=False,
     ):
         self.buf, self.recv, self.later = buf, recv, later
         self.across, self.gathered = across, gathered
@@ -173,7 +174,9 @@
         halvings = [("halve", bit) for bit in range(1, depth)]
         self.stages = [("halve", 0)]
         if gathered is not None:
-            self.stages += [("split", 1)] + halvings + [("gather", depth)]
+            self.stages += halvings[:1] if late else []
+            self.stages += [("split", 2 if late else 1)] + halvings[1 if late else 0 :]
+            self.stages += [("gather", depth)]
         elif direct:
             self.stages += [("direct", 1), ("sum", depth)]
         else:
@@ -190,6 +193,10 @@
     def columns(self, stage):
         split = [kind for kind, _ in self.stages[:stage]].count("split")
         return self.columns_of(self.grp) if split else slice(None)
+
+    def width(self, stage):
+        split = [kind for kind, _ in self.stages[:stage]].count("split")
+        return slice(0, self.part) if split else slice(None)
 
     def shares(self, first, count=1):
         return pl.ds(pl.multiple_of(first * self.rows, self.rows), count * self.rows)
@@ -210,7 +217,7 @@
             pieces.append(
                 (
                     self.buf.at[self.shares(self.start_of(bits) + (1 - bit) * half, half), columns],
-                    self.landing(bits).at[self.landing_rows(bits, 0, half)],
+                    self.landing(bits).at[self.landing_rows(bits, 0, half), self.width(stage)],
                     bits,
                     (self.band + (1 << bits) * (1 - 2 * bit), self.grp),
                 )
@@ -262,7 +269,8 @@
             def _(index):
                 mine = self.shares(keep + index)
                 total = self.buf[mine, columns].astype(F32)
-                total = total + self.landing(bits)[self.landing_rows(bits, index, 1), :].astype(F32)
+                landed = self.landing(bits)[self.landing_rows(bits, index, 1), self.width(stage)]
+                total = total + landed.astype(F32)
                 self.buf[mine, columns] = total.astype(self.dtype)
         elif kind == "direct":
             mine = self.shares(self.start_of(self.depth))
@@ -451,11 +459,12 @@
         qt[:, pl.ds(at, QUERIES)] = q_low * BF16(0.125)
         qs[:, pl.ds(at, QUERIES)] = (q_low.astype(F32) * (0.125 * LOG2_E)).astype(BF16)
 
+    def await_upper(window):
+        @pl.when((band > 0) & (window < WINDOWS))
+        def _():
+            up_copy(window).wait_recv()
+
     def prepare_upper(window):
-        @pl.when(band > 0)
-        def _():
-            up_copy(window).wait_recv()
-
         at = pl.multiple_of(window * QUERIES, QUERIES)
         padded_at = pl.multiple_of(window * QUERIES + TILE, TILE)
         upper = (start_window(side, embed_rows, window) * has_up).astype(BF16)
@@ -464,24 +473,33 @@
         store_pairs(keys_up, padded_at, dot(upper, wk[...]).astype(BF16))
         store_heads(vt_up, padded_at, dot(wtb[...], upper_t).astype(BF16))
 
-    first_block = place_ref[0, 0] > 0
-    row_limit = width_ref[0, 0]
     mask_shape = (SPAN, QUERIES)
     memory, query = iota(mask_shape, 0), iota(mask_shape, 1)
     memory_col = (memory // TILE) * FLANK_COLS + memory % FLANK_COLS - FLANK_COLS
     query_col = (query // TILE) * FLANK_COLS + query % FLANK_COLS
     memory_row = (memory % TILE) // FLANK_COLS
     query_row = (query % TILE) // FLANK_COLS
+    same_row = memory_row == query_row
+    itself = same_row & (memory_col == query_col)
+    earlier = (memory_row < query_row) | (same_row & (memory_col <= query_col))
+    code_low, code_up = d_o.at[:, pl.ds(512, QUERIES)], d_o.at[:, pl.ds(768, 128)]
+    code = jnp.where(itself, 1024, jnp.where(earlier, memory_col, -1024))
+    code_low[...] = code.astype(F32).astype(BF16)
+    code = jnp.where(query[:, 0:128] == 0, memory_col[:, 0:128], 1024)
+    code_up[...] = code.astype(F32).astype(BF16)
+    row_limit = width_ref[0, 0]
+    upper_limit = jnp.where(place_ref[0, 0] > 0, row_limit, 0)
+
+    def bias_of(code_ref, window, limit):
+        code = code_ref[...].astype(F32)
+        first = (-window * BLOCK_COLS).astype(F32)
+        last = (limit - window * BLOCK_COLS).astype(F32)
+        allowed = ((code >= first) & (code < last)) | (code > 512.0)
+        return jnp.where(allowed, 0.0, big_negative)
 
     def prepare_masks(window):
-        column_at = memory_col + window * BLOCK_COLS
-        inside = (column_at >= 0) & (column_at < row_limit)
-        earlier = (memory_row < query_row) | ((memory_row == query_row) & (memory_col <= query_col))
-        itself = (memory_row == query_row) & (memory_col == query_col)
-        bias_low[...] = jnp.where((inside & earlier) | itself, 0.0, big_negative)
-        first = iota(bias_up.shape, 1) == 0
-        closed = jnp.where(inside[:, 0:128] & first_block, 0.0, big_negative)
-        bias_up[...] = jnp.where(first, closed, 0.0).astype(BF16)
+        bias_low[...] = bias_of(code_low, window, row_limit)
+        bias_up[...] = bias_of(code_up, window, upper_limit).astype(BF16)
 
     def e_out(window, half):
         slot = window % 2
@@ -491,15 +509,21 @@
             e_out_sem.at[slot, half],
         )
 
-    prepare_upper(0)
+    for window in range(2):
+        await_upper(window)
+        prepare_upper(window)
+    prepare_masks(jnp.int32(0))
 
     @pl.loop(0, WINDOWS)
     def _(window):
-        @pl.when(window < WINDOWS - 1)
-        def _():
-            prepare_upper(window + 1)
-
-        prepare_masks(window)
+        @pl.when(window == 1)
+        def _():
+            await_upper(2)
+            prepare_upper(2)
+
+        @pl.when(window > 0)
+        def _():
+            await_upper(window + 2)
 
         @pl.when(window > 1)
         def _():
@@ -534,6 +558,9 @@
         current, raised = scores(0), None
         for head in range(8):
             upcoming = scores(head + 1) if head < 7 else None
+            if head == 6:
+                prepare_upper(jnp.where(window == 0, 1, jnp.minimum(window + 2, WINDOWS - 1)))
+                prepare_masks(jnp.minimum(window + 1, WINDOWS - 1))
             upper, lower, peak = current
             e_up = jnp.exp2(upper - peak).astype(BF16)
             e_low = jnp.exp2(lower - peak).astype(BF16)
@@ -759,11 +786,11 @@
 
         return write
 
-    def sum_qkv(pair):
+    def sum_qkv(pair, direct=False):
         return Reduction(
             hd.at[1, pl.ds(qkv_at, width), pl.ds(pl.multiple_of(pair * 384, 128), 384)],
             (width, 384), qkv_recv.at[pair], qkv_later.at[pair], qkv_across.at[pair], None,
-            lambda k: qkv_ss.at[pair, k], lambda k: qkv_rs.at[pair, k], place, True,
+            lambda k: qkv_ss.at[pair, k], lambda k: qkv_rs.at[pair, k], place, direct,
         )
 
     sum_small = Reduction(
@@ -853,8 +880,6 @@
     chosen = jnp.where(channel == iota(shape, 0), 1.0, 0.0).astype(BF16)
 
     def pass_over(pair, part, v_rows, k_cols):
-        for window, half in items:
-            e_in(pair, part, window, half).wait()
         feats = pl.ds(pl.multiple_of(pair * 128, 128), 128)
         follow = pair + 1
         next_pair, next_part = follow % 4, jnp.minimum(part + follow // 4, 1)
@@ -882,6 +907,9 @@
 
         upcoming = grad_probs(*items[0])
         for index, (window, half) in enumerate(items):
+            if index % 6 == 0:
+                for coming in items[index : index + 6]:
+                    e_in(pair, part, *coming).wait()
             current = upcoming
             if index + 1 < len(items):
                 upcoming = grad_probs(*items[index + 1])
@@ -900,7 +928,9 @@
                 d3[at, here] = ((dq + d3[at, here].astype(F32)) * 0.125).astype(BF16)
             add_blocks(0, window, half, dot_nt(qt[mine, here], ds))
             add_blocks(blocks, window, half, dot_nt(d_o[mine, here], e))
-            e_in(next_pair, next_part, window, half).start()
+            if index % 6 == 5:
+                for done in items[index - 5 : index + 1]:
+                    e_in(next_pair, next_part, *done).start()
 
     def take_blocks(ref, at, base):
         for block in range(1, blocks - 1):
@@ -956,7 +986,9 @@
                 if turn < 3:
                     step_in()
                 if turn > 0:
-                    sum_qkv(turn - 1).advance(0)
+                    sum_qkv(turn - 1, turn != 2).advance(0)
+                if turn == 3:
+                    sum_qkv(1).advance(1)
                 if turn < 2:
                     send_halo(2 * turn + 2)
                     send_halo(2 * turn + 3)
@@ -1023,16 +1055,16 @@
 
         @pl.when(window == 0)
         def _():
-            sum_qkv(0).advance(1)
+            sum_qkv(0, True).advance(1)
 
         @pl.when(window == 1)
         def _():
-            sum_qkv(3).advance(0)
+            sum_qkv(3, True).advance(0)
             sum_small.advance(0)
+            sum_qkv(1).advance(2)
 
         @pl.when(window == 2)
         def _():
-            sum_qkv(1).advance(1)
             step_back.last()
 
         @pl.when(window == 3)
@@ -1042,18 +1074,24 @@
         @pl.when(window == 4)
         def _():
             step_out.last()
-            sum_qkv(2).advance(1)
-            sum_qkv(0).finish(write_qkv(0))
-
-    sum_qkv(3).advance(1)
+            sum_qkv(2, True).advance(1)
+
+        @pl.when(window == 5)
+        def _():
+            sum_qkv(1).advance(3)
+
+    for stage in range(4, depth):
+        sum_qkv(1).advance(stage)
+    sum_qkv(3, True).advance(1)
     sum_small.advance(1)
+    sum_qkv(0, True).finish(write_qkv(0))
     sum_qkv(1).finish(write_qkv(1))
-    sum_qkv(2).finish(write_qkv(2))
+    sum_qkv(2, True).finish(write_qkv(2))
 
     def write_small(value):
         small_ref[...] = value
 
-    sum_qkv(3).finish(write_qkv(3))
+    sum_qkv(3, True).finish(write_qkv(3))
     sum_small.finish(write_small)
 
     for window in range(WINDOWS):

time: 159 us -> 157 us (0.987)
  Pallas kernels: 157 us -> 154 us
    pallas_call x1, Pallas kernels: 153 us -> 150 us  [shards(): pl.pallas_call(functools.partial(layer_kernel, size=size, groups=groups,...]
where the time goes in v6:
time: 157 us
  Pallas kernels  154 us (98%)
  between operations  2.13 us (1%)
    pallas_call x1, Pallas kernels, shards(): pl.pallas_call(functools.partial(layer_kernel, size=size, groups=groups,...  150 us
    pallas_call x1, Pallas kernels, shards(): pl.pallas_call(emit_kernel, name='emit_shares', out_shape=(rows, rows, sq...  4.3 us

profile of v6, /device:TPU:0, one launch (start us, length us, event | category | flops | bytes accessed | tf_op | source)
XLA Modules:
  0.0 156.6 jit_solution(12122482299726389702)
XLA Ops:
  1.9 150.2 %layer_forward_and_back.1 = (bf16[8,192,512]{2,1,0:T(8,128)(2,1)}, bf16[8,192,512]{2,1,0:T(8,128)(2,1)}, bf16[6,2,1024,1024]{3,2,1,0:T(8,128)(2,1)}, f32[4,32,38...) custom-call(s32[1,1]{1,0:T(1,128)S(6)} %copy.32.place_ref, ...), custom_call_target="tpu_custom_call" | custom-call | tf_op jit(solution)/shard_map/layer_forward_and_back/pallas_call | solution.py:1183
  152.1 4.3 %emit_shares.1 = (bf16[8,192,512]{2,1,0:T(8,128)(2,1)}, bf16[8,192,512]{2,1,0:T(8,128)(2,1)}, f32[32,512]{1,0:T(8,128)}, f32[32,512]{1,0:T(8,128)}, f32[32,512]{...) custom-call(bf16[8,192,512]{2,1,0:T(8,128)(2,1)} %get-tuple-element., ...), custom_call_target="tpu_custom_call" | custom-call | tf_op jit(solution)/shard_map/emit_shares/pallas_call | solution.py:1277
